TPU v7x, 256 devices: a whole 4x4x8 slice. The times are simulated.
256 devices in a mesh: ctx: 32 (over x_hi, z, core), grp: 4 (over y), dp: 2 (over x_lo).
Axes of the slice: x: 4 (x_hi: 2, x_lo: 2; x = x_hi * 2 + x_lo), y: 4, z: 8, core: 2. Of those that a mesh axis runs over, the one named last changes fastest.
Arguments:
- query_rows: bfloat16 [2, 4096, 4096], P('dp', 'ctx', 'grp'), may hold values from -64 to 64, as said below
- key_rows: bfloat16 [2, 4096, 4096], P('dp', 'ctx', 'grp'), may hold values from -8 to 8, as said below
- value_rows: bfloat16 [2, 4096, 4096], P('dp', 'ctx', 'grp'), may hold values from -6 to 6
- seq_length: int32 [2], P('dp'), may hold values from 1024 to 4096
- out_weight: bfloat16 [4096, 2048], P('grp'), may hold values from -0.09375 to 0.09375
- out_grad: bfloat16 [2, 4096, 2048], P('dp', ('ctx', 'grp')), may hold values from -0.75 to 0.75
Outputs:
- block_out: bfloat16 [2, 4096, 2048], P('dp', ('ctx', 'grp'))
- weight_grad: float32 [4096, 2048], P('grp', ('ctx', 'dp'))
Inputs may be any that keep to these rules, and one draw needn't show every extreme that they name: `query_rows`: every entry lies between the bounds given. `key_rows`: every entry lies between the bounds given.
All inputs are finite; a program needn't handle non-finite values.
Results may differ from a plain program's by a relative error of at most 0.015.
Values may be sent and summed in bfloat16 or wider, within the bound.
No kernel may reach another device: no remote copies, remote signals or barrier semaphores. Data moves between devices by JAX's collectives and lax.ppermute only.
A program may use at most 64 MiB of HBM per device.

v0:
```python
import math

import jax
import jax.numpy as jnp
from jax import lax
from jax.sharding import PartitionSpec as P

HEAD_DIM = 256


masked_score = -1e30


def shifted(value, axis, steps):
    count = lax.axis_size(axis)
    pairs = [(source, (source + steps) % count) for source in range(count)]
    return lax.ppermute(value, axis, pairs)


def attend(state_now, query_heads, key_piece, value_piece, key_start, length):
    row_best, row_total, numerator = state_now
    key_count = key_piece.shape[0]
    head_count = query_heads.shape[1]
    key_heads = key_piece.reshape(key_count, head_count, HEAD_DIM)
    value_heads = value_piece.reshape(key_count, head_count, HEAD_DIM)
    scores = jnp.einsum(
        "qhd,khd->hqk", query_heads, key_heads, preferred_element_type=jnp.float32
    ) * (1.0 / math.sqrt(HEAD_DIM))
    live_keys = (key_start + jnp.arange(key_count) < length)[None, None, :]
    scores = jnp.where(live_keys, scores, masked_score)
    new_best = jnp.maximum(row_best, jnp.max(scores, axis=2))
    exp_terms = jnp.where(live_keys, jnp.exp(scores - new_best[:, :, None]), 0.0)
    fade_factor = jnp.exp(row_best - new_best)
    row_total = row_total * fade_factor + jnp.sum(exp_terms, axis=2)
    added_terms = jnp.einsum(
        "hqk,khd->qhd",
        exp_terms.astype(jnp.bfloat16),
        value_heads,
        preferred_element_type=jnp.float32,
    )
    numerator = numerator * fade_factor.T[:, :, None] + added_terms
    return (new_best, row_total, numerator)


def local(query_rows, key_rows, value_rows, seq_length, out_weight, out_grad):
    queries = query_rows[0]
    key_local = key_rows[0]
    value_local = value_rows[0]
    query_count, local_width = queries.shape
    local_heads = local_width // HEAD_DIM
    length = seq_length[0]
    ctx_size = lax.axis_size("ctx")
    ctx_place = lax.axis_index("ctx")
    query_start = ctx_place * query_count
    query_heads = queries.reshape(query_count, local_heads, HEAD_DIM)

    def visit(state_now, query_part, key_piece, value_piece, key_start):
        return attend(state_now, query_part, key_piece, value_piece, key_start, length)

    cycle_start = jnp.stack((key_local, value_local))

    def cycle_step(turn_index, carried):
        state_now, cycle_pair = carried
        source = (ctx_place - turn_index) % ctx_size
        state_now = visit(
            state_now, query_heads, cycle_pair[0], cycle_pair[1], source * query_count
        )
        cycle_pair = shifted(cycle_pair, "ctx", 1)
        return (state_now, cycle_pair)

    state_now, cycle_pair = lax.fori_loop(
        0,
        ctx_size - 1,
        cycle_step,
        (
            (
                jnp.full((local_heads, query_count), masked_score, jnp.float32),
                jnp.zeros((local_heads, query_count), jnp.float32),
                jnp.zeros((query_count, local_heads, HEAD_DIM), jnp.float32),
            ),
            cycle_start,
        ),
    )
    last_source = (ctx_place - (ctx_size - 1)) % ctx_size
    row_best, row_total, numerator = visit(
        state_now, query_heads, cycle_pair[0], cycle_pair[1], last_source * query_count
    )
    live_rows = query_start + jnp.arange(query_count) < length
    safe_total = jnp.where(live_rows[None, :], row_total, 1.0)
    context = numerator / safe_total.T[:, :, None]
    context = (
        jnp.where(live_rows[:, None, None], context, 0.0)
        .reshape(query_count, local_width)
        .astype(jnp.bfloat16)
    )
    part_rows = context
    projected = lax.psum_scatter(
        jnp.dot(part_rows, out_weight, preferred_element_type=jnp.float32).astype(jnp.bfloat16),
        "grp",
        scatter_dimension=0,
        tiled=True,
    )
    block_out = projected[None]
    part_rows = context
    grad_total = lax.dot_general(
        part_rows,
        lax.all_gather(out_grad[0], "grp", axis=0, tiled=True),
        (((0,), (0,)), ((), ())),
        preferred_element_type=jnp.float32,
    )
    weight_grad = lax.psum_scatter(grad_total, ("ctx", "dp"), scatter_dimension=1, tiled=True)
    return (block_out, weight_grad)


def solution(mesh):
    in_specs = (
        P("dp", "ctx", "grp"),
        P("dp", "ctx", "grp"),
        P("dp", "ctx", "grp"),
        P("dp"),
        P("grp", None),
        P("dp", ("ctx", "grp"), None),
    )
    out_specs = (P("dp", ("ctx", "grp"), None), P("grp", ("ctx", "dp")))
    return jax.shard_map(local, mesh=mesh, in_specs=in_specs, out_specs=out_specs, check_vma=False)
```

profile of v0, /device:TPU:8, one launch (start us, length us, event | category | flops | bytes accessed | tf_op | source)
XLA Modules:
  0.0 702.6 jit_solution(4540500715523753546)
XLA Ops:
  11.5 384.8 %while.22 = (s32[]{:T(128)}, f32[4,128]{1,0:T(4,128)S(1)}, f32[4,128]{1,0:T(4,128)S(1)}, f32[128,4,256]{2,0,1:T(8,128)S(1)}, bf16[2,128,1024]{1,2,0:T(8,128)(2,1...) while((s32[]{:T(128)}, f32[4,128]{1,0:T(4,128)S(1)}, ...), condition=%wide.region_3.4_spmd.clone, body=%wide.region_0.3_spmd.clone.sunk | while | flops 68095248 | bytes 6849342 | solution.py:71
  13.2 13.0 %collective-permute-done = bf16[2,128,1024]{1,2,0:T(8,128)(2,1)S(1)} collective-permute-done((bf16[2,128,1024]{1,2,0:T(8,128)(2,1)S(1)}, bf16[2,128,1024]{1,2,0:T(8,128)(2,1)S(1)}, u32[]{:S(2)}, u32[]{:S(2)}) %collective-permute-start) | collective-permute-done | bytes 524320 | tf_op jit(solution)/shard_map/while/body/eval_jaxpr/ppermute | solution.py:17
  28.0 10.6 %collective-permute-done = bf16[2,128,1024]{1,2,0:T(8,128)(2,1)S(1)} collective-permute-done((bf16[2,128,1024]{1,2,0:T(8,128)(2,1)S(1)}, bf16[2,128,1024]{1,2,0:T(8,128)(2,1)S(1)}, u32[]{:S(2)}, u32[]{:S(2)}) %collective-permute-start) | collective-permute-done | bytes 524320 | tf_op jit(solution)/shard_map/while/body/eval_jaxpr/ppermute | solution.py:17
  40.3 10.6 %collective-permute-done = bf16[2,128,1024]{1,2,0:T(8,128)(2,1)S(1)} collective-permute-done((bf16[2,128,1024]{1,2,0:T(8,128)(2,1)S(1)}, bf16[2,128,1024]{1,2,0:T(8,128)(2,1)S(1)}, u32[]{:S(2)}, u32[]{:S(2)}) %collective-permute-start) | collective-permute-done | bytes 524320 | tf_op jit(solution)/shard_map/while/body/eval_jaxpr/ppermute | solution.py:17
  52.7 10.6 %collective-permute-done = bf16[2,128,1024]{1,2,0:T(8,128)(2,1)S(1)} collective-permute-done((bf16[2,128,1024]{1,2,0:T(8,128)(2,1)S(1)}, bf16[2,128,1024]{1,2,0:T(8,128)(2,1)S(1)}, u32[]{:S(2)}, u32[]{:S(2)}) %collective-permute-start) | collective-permute-done | bytes 524320 | tf_op jit(solution)/shard_map/while/body/eval_jaxpr/ppermute | solution.py:17
  65.0 10.6 %collective-permute-done = bf16[2,128,1024]{1,2,0:T(8,128)(2,1)S(1)} collective-permute-done((bf16[2,128,1024]{1,2,0:T(8,128)(2,1)S(1)}, bf16[2,128,1024]{1,2,0:T(8,128)(2,1)S(1)}, u32[]{:S(2)}, u32[]{:S(2)}) %collective-permute-start) | collective-permute-done | bytes 524320 | tf_op jit(solution)/shard_map/while/body/eval_jaxpr/ppermute | solution.py:17
  77.3 10.6 %collective-permute-done = bf16[2,128,1024]{1,2,0:T(8,128)(2,1)S(1)} collective-permute-done((bf16[2,128,1024]{1,2,0:T(8,128)(2,1)S(1)}, bf16[2,128,1024]{1,2,0:T(8,128)(2,1)S(1)}, u32[]{:S(2)}, u32[]{:S(2)}) %collective-permute-start) | collective-permute-done | bytes 524320 | tf_op jit(solution)/shard_map/while/body/eval_jaxpr/ppermute | solution.py:17
  89.7 10.6 %collective-permute-done = bf16[2,128,1024]{1,2,0:T(8,128)(2,1)S(1)} collective-permute-done((bf16[2,128,1024]{1,2,0:T(8,128)(2,1)S(1)}, bf16[2,128,1024]{1,2,0:T(8,128)(2,1)S(1)}, u32[]{:S(2)}, u32[]{:S(2)}) %collective-permute-start) | collective-permute-done | bytes 524320 | tf_op jit(solution)/shard_map/while/body/eval_jaxpr/ppermute | solution.py:17
  114.3 10.6 %collective-permute-done = bf16[2,128,1024]{1,2,0:T(8,128)(2,1)S(1)} collective-permute-done((bf16[2,128,1024]{1,2,0:T(8,128)(2,1)S(1)}, bf16[2,128,1024]{1,2,0:T(8,128)(2,1)S(1)}, u32[]{:S(2)}, u32[]{:S(2)}) %collective-permute-start) | collective-permute-done | bytes 524320 | tf_op jit(solution)/shard_map/while/body/eval_jaxpr/ppermute | solution.py:17
  126.7 10.6 %collective-permute-done = bf16[2,128,1024]{1,2,0:T(8,128)(2,1)S(1)} collective-permute-done((bf16[2,128,1024]{1,2,0:T(8,128)(2,1)S(1)}, bf16[2,128,1024]{1,2,0:T(8,128)(2,1)S(1)}, u32[]{:S(2)}, u32[]{:S(2)}) %collective-permute-start) | collective-permute-done | bytes 524320 | tf_op jit(solution)/shard_map/while/body/eval_jaxpr/ppermute | solution.py:17
  176.0 10.6 %collective-permute-done = bf16[2,128,1024]{1,2,0:T(8,128)(2,1)S(1)} collective-permute-done((bf16[2,128,1024]{1,2,0:T(8,128)(2,1)S(1)}, bf16[2,128,1024]{1,2,0:T(8,128)(2,1)S(1)}, u32[]{:S(2)}, u32[]{:S(2)}) %collective-permute-start) | collective-permute-done | bytes 524320 | tf_op jit(solution)/shard_map/while/body/eval_jaxpr/ppermute | solution.py:17
  188.4 10.6 %collective-permute-done = bf16[2,128,1024]{1,2,0:T(8,128)(2,1)S(1)} collective-permute-done((bf16[2,128,1024]{1,2,0:T(8,128)(2,1)S(1)}, bf16[2,128,1024]{1,2,0:T(8,128)(2,1)S(1)}, u32[]{:S(2)}, u32[]{:S(2)}) %collective-permute-start) | collective-permute-done | bytes 524320 | tf_op jit(solution)/shard_map/while/body/eval_jaxpr/ppermute | solution.py:17
  200.7 10.6 %collective-permute-done = bf16[2,128,1024]{1,2,0:T(8,128)(2,1)S(1)} collective-permute-done((bf16[2,128,1024]{1,2,0:T(8,128)(2,1)S(1)}, bf16[2,128,1024]{1,2,0:T(8,128)(2,1)S(1)}, u32[]{:S(2)}, u32[]{:S(2)}) %collective-permute-start) | collective-permute-done | bytes 524320 | tf_op jit(solution)/shard_map/while/body/eval_jaxpr/ppermute | solution.py:17
  213.0 10.6 %collective-permute-done = bf16[2,128,1024]{1,2,0:T(8,128)(2,1)S(1)} collective-permute-done((bf16[2,128,1024]{1,2,0:T(8,128)(2,1)S(1)}, bf16[2,128,1024]{1,2,0:T(8,128)(2,1)S(1)}, u32[]{:S(2)}, u32[]{:S(2)}) %collective-permute-start) | collective-permute-done | bytes 524320 | tf_op jit(solution)/shard_map/while/body/eval_jaxpr/ppermute | solution.py:17
  225.4 10.6 %collective-permute-done = bf16[2,128,1024]{1,2,0:T(8,128)(2,1)S(1)} collective-permute-done((bf16[2,128,1024]{1,2,0:T(8,128)(2,1)S(1)}, bf16[2,128,1024]{1,2,0:T(8,128)(2,1)S(1)}, u32[]{:S(2)}, u32[]{:S(2)}) %collective-permute-start) | collective-permute-done | bytes 524320 | tf_op jit(solution)/shard_map/while/body/eval_jaxpr/ppermute | solution.py:17
  237.7 10.6 %collective-permute-done = bf16[2,128,1024]{1,2,0:T(8,128)(2,1)S(1)} collective-permute-done((bf16[2,128,1024]{1,2,0:T(8,128)(2,1)S(1)}, bf16[2,128,1024]{1,2,0:T(8,128)(2,1)S(1)}, u32[]{:S(2)}, u32[]{:S(2)}) %collective-permute-start) | collective-permute-done | bytes 524320 | tf_op jit(solution)/shard_map/while/body/eval_jaxpr/ppermute | solution.py:17
  250.0 10.6 %collective-permute-done = bf16[2,128,1024]{1,2,0:T(8,128)(2,1)S(1)} collective-permute-done((bf16[2,128,1024]{1,2,0:T(8,128)(2,1)S(1)}, bf16[2,128,1024]{1,2,0:T(8,128)(2,1)S(1)}, u32[]{:S(2)}, u32[]{:S(2)}) %collective-permute-start) | collective-permute-done | bytes 524320 | tf_op jit(solution)/shard_map/while/body/eval_jaxpr/ppermute | solution.py:17
  262.4 10.6 %collective-permute-done = bf16[2,128,1024]{1,2,0:T(8,128)(2,1)S(1)} collective-permute-done((bf16[2,128,1024]{1,2,0:T(8,128)(2,1)S(1)}, bf16[2,128,1024]{1,2,0:T(8,128)(2,1)S(1)}, u32[]{:S(2)}, u32[]{:S(2)}) %collective-permute-start) | collective-permute-done | bytes 524320 | tf_op jit(solution)/shard_map/while/body/eval_jaxpr/ppermute | solution.py:17
  274.7 10.6 %collective-permute-done = bf16[2,128,1024]{1,2,0:T(8,128)(2,1)S(1)} collective-permute-done((bf16[2,128,1024]{1,2,0:T(8,128)(2,1)S(1)}, bf16[2,128,1024]{1,2,0:T(8,128)(2,1)S(1)}, u32[]{:S(2)}, u32[]{:S(2)}) %collective-permute-start) | collective-permute-done | bytes 524320 | tf_op jit(solution)/shard_map/while/body/eval_jaxpr/ppermute | solution.py:17
  336.4 10.6 %collective-permute-done = bf16[2,128,1024]{1,2,0:T(8,128)(2,1)S(1)} collective-permute-done((bf16[2,128,1024]{1,2,0:T(8,128)(2,1)S(1)}, bf16[2,128,1024]{1,2,0:T(8,128)(2,1)S(1)}, u32[]{:S(2)}, u32[]{:S(2)}) %collective-permute-start) | collective-permute-done | bytes 524320 | tf_op jit(solution)/shard_map/while/body/eval_jaxpr/ppermute | solution.py:17
  373.4 10.6 %collective-permute-done = bf16[2,128,1024]{1,2,0:T(8,128)(2,1)S(1)} collective-permute-done((bf16[2,128,1024]{1,2,0:T(8,128)(2,1)S(1)}, bf16[2,128,1024]{1,2,0:T(8,128)(2,1)S(1)}, u32[]{:S(2)}, u32[]{:S(2)}) %collective-permute-start) | collective-permute-done | bytes 524320 | tf_op jit(solution)/shard_map/while/body/eval_jaxpr/ppermute | solution.py:17
  385.7 10.6 %collective-permute-done = bf16[2,128,1024]{1,2,0:T(8,128)(2,1)S(1)} collective-permute-done((bf16[2,128,1024]{1,2,0:T(8,128)(2,1)S(1)}, bf16[2,128,1024]{1,2,0:T(8,128)(2,1)S(1)}, u32[]{:S(2)}, u32[]{:S(2)}) %collective-permute-start) | collective-permute-done | bytes 524320 | tf_op jit(solution)/shard_map/while/body/eval_jaxpr/ppermute | solution.py:17
  401.2 13.5 %all-gather = bf16[1,128,2048]{2,1,0:T(8,128)(2,1)S(1)} all-gather(bf16[1,32,2048]{2,1,0:T(8,128)(2,1)S(1)} %copy-done), channel_id=2, replica_groups=mesh['ctx'=32,'grp'=4,'dp'=2] {'grp'}, dimensions={1}, use_global_device_ids=true | all-gather | bytes 655360 | tf_op jit(solution)/shard_map/all_gather | solution.py:107
  419.3 276.4 %reduce-scatter.5.cloned.1.call-done = f32[1024,32]{0,1:T(8,128)} async-done(((f32[1024,2048]{0,1:T(8,128)}), f32[1024,32]{0,1:T(8,128)}) %reduce-scatter.5.cloned.1.call-update) | async-done | bytes 131088 | tf_op jit(solution)/shard_map/reduce_scatter | solution.py:111
  (345 shorter events, 170.1 us)
Async XLA Ops:
  7.2 412.2 %reduce-scatter.3.cloned.1.call-start = ((), (), s32[]{:S(2)}) async-start(), calls=%async_computation.2 | async-start | bytes 655360 | tf_op jit(solution)/shard_map/reduce_scatter | solution.py:97
  11.6 14.7 %collective-permute-start = (bf16[2,128,1024]{1,2,0:T(8,128)(2,1)S(1)}, bf16[2,128,1024]{1,2,0:T(8,128)(2,1)S(1)}, u32[]{:S(2)}, u32[]{:S(2)}) collective-permute-start(bf16[2,128,1024]{1,2,0:T(8,128)(2,1)S(1)} %copy.38), channel_id=1, source_target_pairs={{0,8},{8,16},{16,24},{24,32},{32,40},{40,48},{48,56},{56,64},{64,7... | collective-permute-start | bytes 1572872 | tf_op jit(solution)/shard_map/while/body/eval_jaxpr/ppermute | solution.py:17
  26.3 12.3 %collective-permute-start = (bf16[2,128,1024]{1,2,0:T(8,128)(2,1)S(1)}, bf16[2,128,1024]{1,2,0:T(8,128)(2,1)S(1)}, u32[]{:S(2)}, u32[]{:S(2)}) collective-permute-start(bf16[2,128,1024]{1,2,0:T(8,128)(2,1)S(1)} %copy.38), channel_id=1, source_target_pairs={{0,8},{8,16},{16,24},{24,32},{32,40},{40,48},{48,56},{56,64},{64,7... | collective-permute-start | bytes 1572872 | tf_op jit(solution)/shard_map/while/body/eval_jaxpr/ppermute | solution.py:17
  38.6 12.3 %collective-permute-start = (bf16[2,128,1024]{1,2,0:T(8,128)(2,1)S(1)}, bf16[2,128,1024]{1,2,0:T(8,128)(2,1)S(1)}, u32[]{:S(2)}, u32[]{:S(2)}) collective-permute-start(bf16[2,128,1024]{1,2,0:T(8,128)(2,1)S(1)} %copy.38), channel_id=1, source_target_pairs={{0,8},{8,16},{16,24},{24,32},{32,40},{40,48},{48,56},{56,64},{64,7... | collective-permute-start | bytes 1572872 | tf_op jit(solution)/shard_map/while/body/eval_jaxpr/ppermute | solution.py:17
  51.0 12.3 %collective-permute-start = (bf16[2,128,1024]{1,2,0:T(8,128)(2,1)S(1)}, bf16[2,128,1024]{1,2,0:T(8,128)(2,1)S(1)}, u32[]{:S(2)}, u32[]{:S(2)}) collective-permute-start(bf16[2,128,1024]{1,2,0:T(8,128)(2,1)S(1)} %copy.38), channel_id=1, source_target_pairs={{0,8},{8,16},{16,24},{24,32},{32,40},{40,48},{48,56},{56,64},{64,7... | collective-permute-start | bytes 1572872 | tf_op jit(solution)/shard_map/while/body/eval_jaxpr/ppermute | solution.py:17
  63.3 12.3 %collective-permute-start = (bf16[2,128,1024]{1,2,0:T(8,128)(2,1)S(1)}, bf16[2,128,1024]{1,2,0:T(8,128)(2,1)S(1)}, u32[]{:S(2)}, u32[]{:S(2)}) collective-permute-start(bf16[2,128,1024]{1,2,0:T(8,128)(2,1)S(1)} %copy.38), channel_id=1, source_target_pairs={{0,8},{8,16},{16,24},{24,32},{32,40},{40,48},{48,56},{56,64},{64,7... | collective-permute-start | bytes 1572872 | tf_op jit(solution)/shard_map/while/body/eval_jaxpr/ppermute | solution.py:17
  75.6 12.3 %collective-permute-start = (bf16[2,128,1024]{1,2,0:T(8,128)(2,1)S(1)}, bf16[2,128,1024]{1,2,0:T(8,128)(2,1)S(1)}, u32[]{:S(2)}, u32[]{:S(2)}) collective-permute-start(bf16[2,128,1024]{1,2,0:T(8,128)(2,1)S(1)} %copy.38), channel_id=1, source_target_pairs={{0,8},{8,16},{16,24},{24,32},{32,40},{40,48},{48,56},{56,64},{64,7... | collective-permute-start | bytes 1572872 | tf_op jit(solution)/shard_map/while/body/eval_jaxpr/ppermute | solution.py:17
  88.0 12.3 %collective-permute-start = (bf16[2,128,1024]{1,2,0:T(8,128)(2,1)S(1)}, bf16[2,128,1024]{1,2,0:T(8,128)(2,1)S(1)}, u32[]{:S(2)}, u32[]{:S(2)}) collective-permute-start(bf16[2,128,1024]{1,2,0:T(8,128)(2,1)S(1)} %copy.38), channel_id=1, source_target_pairs={{0,8},{8,16},{16,24},{24,32},{32,40},{40,48},{48,56},{56,64},{64,7... | collective-permute-start | bytes 1572872 | tf_op jit(solution)/shard_map/while/body/eval_jaxpr/ppermute | solution.py:17
  100.3 12.3 %collective-permute-start = (bf16[2,128,1024]{1,2,0:T(8,128)(2,1)S(1)}, bf16[2,128,1024]{1,2,0:T(8,128)(2,1)S(1)}, u32[]{:S(2)}, u32[]{:S(2)}) collective-permute-start(bf16[2,128,1024]{1,2,0:T(8,128)(2,1)S(1)} %copy.38), channel_id=1, source_target_pairs={{0,8},{8,16},{16,24},{24,32},{32,40},{40,48},{48,56},{56,64},{64,7... | collective-permute-start | bytes 1572872 | tf_op jit(solution)/shard_map/while/body/eval_jaxpr/ppermute | solution.py:17
  112.7 12.3 %collective-permute-start = (bf16[2,128,1024]{1,2,0:T(8,128)(2,1)S(1)}, bf16[2,128,1024]{1,2,0:T(8,128)(2,1)S(1)}, u32[]{:S(2)}, u32[]{:S(2)}) collective-permute-start(bf16[2,128,1024]{1,2,0:T(8,128)(2,1)S(1)} %copy.38), channel_id=1, source_target_pairs={{0,8},{8,16},{16,24},{24,32},{32,40},{40,48},{48,56},{56,64},{64,7... | collective-permute-start | bytes 1572872 | tf_op jit(solution)/shard_map/while/body/eval_jaxpr/ppermute | solution.py:17
  125.0 12.3 %collective-permute-start = (bf16[2,128,1024]{1,2,0:T(8,128)(2,1)S(1)}, bf16[2,128,1024]{1,2,0:T(8,128)(2,1)S(1)}, u32[]{:S(2)}, u32[]{:S(2)}) collective-permute-start(bf16[2,128,1024]{1,2,0:T(8,128)(2,1)S(1)} %copy.38), channel_id=1, source_target_pairs={{0,8},{8,16},{16,24},{24,32},{32,40},{40,48},{48,56},{56,64},{64,7... | collective-permute-start | bytes 1572872 | tf_op jit(solution)/shard_map/while/body/eval_jaxpr/ppermute | solution.py:17
  137.3 12.3 %collective-permute-start = (bf16[2,128,1024]{1,2,0:T(8,128)(2,1)S(1)}, bf16[2,128,1024]{1,2,0:T(8,128)(2,1)S(1)}, u32[]{:S(2)}, u32[]{:S(2)}) collective-permute-start(bf16[2,128,1024]{1,2,0:T(8,128)(2,1)S(1)} %copy.38), channel_id=1, source_target_pairs={{0,8},{8,16},{16,24},{24,32},{32,40},{40,48},{48,56},{56,64},{64,7... | collective-permute-start | bytes 1572872 | tf_op jit(solution)/shard_map/while/body/eval_jaxpr/ppermute | solution.py:17
  149.7 12.3 %collective-permute-start = (bf16[2,128,1024]{1,2,0:T(8,128)(2,1)S(1)}, bf16[2,128,1024]{1,2,0:T(8,128)(2,1)S(1)}, u32[]{:S(2)}, u32[]{:S(2)}) collective-permute-start(bf16[2,128,1024]{1,2,0:T(8,128)(2,1)S(1)} %copy.38), channel_id=1, source_target_pairs={{0,8},{8,16},{16,24},{24,32},{32,40},{40,48},{48,56},{56,64},{64,7... | collective-permute-start | bytes 1572872 | tf_op jit(solution)/shard_map/while/body/eval_jaxpr/ppermute | solution.py:17
  162.0 12.3 %collective-permute-start = (bf16[2,128,1024]{1,2,0:T(8,128)(2,1)S(1)}, bf16[2,128,1024]{1,2,0:T(8,128)(2,1)S(1)}, u32[]{:S(2)}, u32[]{:S(2)}) collective-permute-start(bf16[2,128,1024]{1,2,0:T(8,128)(2,1)S(1)} %copy.38), channel_id=1, source_target_pairs={{0,8},{8,16},{16,24},{24,32},{32,40},{40,48},{48,56},{56,64},{64,7... | collective-permute-start | bytes 1572872 | tf_op jit(solution)/shard_map/while/body/eval_jaxpr/ppermute | solution.py:17
  174.3 12.3 %collective-permute-start = (bf16[2,128,1024]{1,2,0:T(8,128)(2,1)S(1)}, bf16[2,128,1024]{1,2,0:T(8,128)(2,1)S(1)}, u32[]{:S(2)}, u32[]{:S(2)}) collective-permute-start(bf16[2,128,1024]{1,2,0:T(8,128)(2,1)S(1)} %copy.38), channel_id=1, source_target_pairs={{0,8},{8,16},{16,24},{24,32},{32,40},{40,48},{48,56},{56,64},{64,7... | collective-permute-start | bytes 1572872 | tf_op jit(solution)/shard_map/while/body/eval_jaxpr/ppermute | solution.py:17
  186.7 12.3 %collective-permute-start = (bf16[2,128,1024]{1,2,0:T(8,128)(2,1)S(1)}, bf16[2,128,1024]{1,2,0:T(8,128)(2,1)S(1)}, u32[]{:S(2)}, u32[]{:S(2)}) collective-permute-start(bf16[2,128,1024]{1,2,0:T(8,128)(2,1)S(1)} %copy.38), channel_id=1, source_target_pairs={{0,8},{8,16},{16,24},{24,32},{32,40},{40,48},{48,56},{56,64},{64,7... | collective-permute-start | bytes 1572872 | tf_op jit(solution)/shard_map/while/body/eval_jaxpr/ppermute | solution.py:17
  199.0 12.3 %collective-permute-start = (bf16[2,128,1024]{1,2,0:T(8,128)(2,1)S(1)}, bf16[2,128,1024]{1,2,0:T(8,128)(2,1)S(1)}, u32[]{:S(2)}, u32[]{:S(2)}) collective-permute-start(bf16[2,128,1024]{1,2,0:T(8,128)(2,1)S(1)} %copy.38), channel_id=1, source_target_pairs={{0,8},{8,16},{16,24},{24,32},{32,40},{40,48},{48,56},{56,64},{64,7... | collective-permute-start | bytes 1572872 | tf_op jit(solution)/shard_map/while/body/eval_jaxpr/ppermute | solution.py:17
  211.3 12.3 %collective-permute-start = (bf16[2,128,1024]{1,2,0:T(8,128)(2,1)S(1)}, bf16[2,128,1024]{1,2,0:T(8,128)(2,1)S(1)}, u32[]{:S(2)}, u32[]{:S(2)}) collective-permute-start(bf16[2,128,1024]{1,2,0:T(8,128)(2,1)S(1)} %copy.38), channel_id=1, source_target_pairs={{0,8},{8,16},{16,24},{24,32},{32,40},{40,48},{48,56},{56,64},{64,7... | collective-permute-start | bytes 1572872 | tf_op jit(solution)/shard_map/while/body/eval_jaxpr/ppermute | solution.py:17
  260.7 12.3 %collective-permute-start = (bf16[2,128,1024]{1,2,0:T(8,128)(2,1)S(1)}, bf16[2,128,1024]{1,2,0:T(8,128)(2,1)S(1)}, u32[]{:S(2)}, u32[]{:S(2)}) collective-permute-start(bf16[2,128,1024]{1,2,0:T(8,128)(2,1)S(1)} %copy.38), channel_id=1, source_target_pairs={{0,8},{8,16},{16,24},{24,32},{32,40},{40,48},{48,56},{56,64},{64,7... | collective-permute-start | bytes 1572872 | tf_op jit(solution)/shard_map/while/body/eval_jaxpr/ppermute | solution.py:17
  273.0 12.3 %collective-permute-start = (bf16[2,128,1024]{1,2,0:T(8,128)(2,1)S(1)}, bf16[2,128,1024]{1,2,0:T(8,128)(2,1)S(1)}, u32[]{:S(2)}, u32[]{:S(2)}) collective-permute-start(bf16[2,128,1024]{1,2,0:T(8,128)(2,1)S(1)} %copy.38), channel_id=1, source_target_pairs={{0,8},{8,16},{16,24},{24,32},{32,40},{40,48},{48,56},{56,64},{64,7... | collective-permute-start | bytes 1572872 | tf_op jit(solution)/shard_map/while/body/eval_jaxpr/ppermute | solution.py:17
  322.4 12.3 %collective-permute-start = (bf16[2,128,1024]{1,2,0:T(8,128)(2,1)S(1)}, bf16[2,128,1024]{1,2,0:T(8,128)(2,1)S(1)}, u32[]{:S(2)}, u32[]{:S(2)}) collective-permute-start(bf16[2,128,1024]{1,2,0:T(8,128)(2,1)S(1)} %copy.38), channel_id=1, source_target_pairs={{0,8},{8,16},{16,24},{24,32},{32,40},{40,48},{48,56},{56,64},{64,7... | collective-permute-start | bytes 1572872 | tf_op jit(solution)/shard_map/while/body/eval_jaxpr/ppermute | solution.py:17
  334.7 12.3 %collective-permute-start = (bf16[2,128,1024]{1,2,0:T(8,128)(2,1)S(1)}, bf16[2,128,1024]{1,2,0:T(8,128)(2,1)S(1)}, u32[]{:S(2)}, u32[]{:S(2)}) collective-permute-start(bf16[2,128,1024]{1,2,0:T(8,128)(2,1)S(1)} %copy.38), channel_id=1, source_target_pairs={{0,8},{8,16},{16,24},{24,32},{32,40},{40,48},{48,56},{56,64},{64,7... | collective-permute-start | bytes 1572872 | tf_op jit(solution)/shard_map/while/body/eval_jaxpr/ppermute | solution.py:17
  384.1 12.3 %collective-permute-start = (bf16[2,128,1024]{1,2,0:T(8,128)(2,1)S(1)}, bf16[2,128,1024]{1,2,0:T(8,128)(2,1)S(1)}, u32[]{:S(2)}, u32[]{:S(2)}) collective-permute-start(bf16[2,128,1024]{1,2,0:T(8,128)(2,1)S(1)} %copy.38), channel_id=1, source_target_pairs={{0,8},{8,16},{16,24},{24,32},{32,40},{40,48},{48,56},{56,64},{64,7... | collective-permute-start | bytes 1572872 | tf_op jit(solution)/shard_map/while/body/eval_jaxpr/ppermute | solution.py:17
  401.2 294.6 %reduce-scatter.5.cloned.1.call-start = ((), (), s32[]{:S(2)}) async-start(), calls=%async_computation.3 | async-start | bytes 8519680 | tf_op jit(solution)/shard_map/reduce_scatter | solution.py:111
  (10 other events, 114.9 us)
Sparse Core Ops, SparseCore 0:
  401.3 16.9 reduce-scatter.2
  421.4 274.3 reduce-scatter.4
where the time goes:
time: 703 us
  waiting for transfers between devices  608 us (86%)
  matrix products  30.7 us (4%)
  other arithmetic  24.6 us (3%)
  between operations  14.8 us (2%)
  blocking collectives  13.5 us (2%)
    ppermute x31, waiting for transfers between devices, shifted(): return lax.ppermute(value, axis, pairs)  331 us
    reduce_scatter x1, waiting for transfers between devices, local(): lax.psum_scatter(grad_total, ('ctx', 'dp'), scatter_dimension=1, tiled=True)  276 us
    lt x32, other arithmetic, attend(): live_keys = (key_start + jnp.arange(key_count) < length)[None, None, :]  20.3 us
  transfers between devices with their start and end apart: 33, of which 32 were waited for; matrix products, arithmetic and copies ran while one was open for 7% of the time, Pallas kernels for 0%

commit v1 on v0

v1 whole, which is shorter than its diff:
```python
import math

import jax
import jax.numpy as jnp
from jax import lax
from jax.experimental import pallas as pl
from jax.experimental.pallas import tpu as pltpu
from jax.sharding import Mesh, PartitionSpec as P

HEAD_DIM = 256
SPLIT = (("xh", 2), ("zq", 4), ("zr", 2), ("core", 2), ("y", 4), ("xl", 2))
AXES = tuple(name for name, _ in SPLIT)
SIZE = dict(SPLIT)
MASKED = -1e30
BF = jnp.bfloat16
F32 = jnp.float32


def moved(value, shift):
    names = tuple(shift)
    sizes = [SIZE[n] for n in names]
    count = math.prod(sizes)
    pairs = []
    for source in range(count):
        rest, place = source, []
        for s in reversed(sizes):
            place.append(rest % s)
            rest //= s
        place = place[::-1]
        target = 0
        for p, s, n in zip(place, sizes, names):
            target = target * s + (p + shift[n]) % s
        pairs.append((source, target))
    return lax.ppermute(value, names, pairs)


def scores_body(q0, q1, k0, k1, k2, k3, bias, p_out, stat_out):
    tile = p_out.shape[0]
    own = pl.program_id(0) < pl.num_programs(0) // 2

    def run(q_ref):
        q = q_ref[...]
        parts = []
        for i, k in enumerate((k0, k1, k2, k3)):
            s = lax.dot_general(q, k[...], (((1,), (1,)), ((), ())), preferred_element_type=F32)
            width = k.shape[0]
            parts.append(s * (math.log2(math.e) / math.sqrt(HEAD_DIM)) + bias[:, i * width : (i + 1) * width])
        top = parts[0].max(axis=1, keepdims=True)
        for s in parts[1:]:
            top = jnp.maximum(top, s.max(axis=1, keepdims=True))
        total = jnp.zeros((tile, 1), F32)
        for i, s in enumerate(parts):
            e = jnp.exp2(s - top)
            total += e.sum(axis=1, keepdims=True)
            width = s.shape[1]
            p_out[:, i * width : (i + 1) * width] = e.astype(BF)
        stat_out[:, :128] = jnp.broadcast_to(top, (tile, 128))
        stat_out[:, 128:] = jnp.broadcast_to(total, (tile, 128))

    @pl.when(own)
    def _():
        run(q0)

    @pl.when(jnp.logical_not(own))
    def _():
        run(q1)


def score_kernel(q_own, q_other, ks, bias):
    half = q_own.shape[0]
    tile = 256
    steps = half // tile
    keys = sum(k.shape[0] for k in ks)
    return pl.pallas_call(
        scores_body,
        grid=(2 * steps,),
        in_specs=[
            pl.BlockSpec((tile, HEAD_DIM), lambda i: (jnp.minimum(i, steps - 1), 0)),
            pl.BlockSpec((tile, HEAD_DIM), lambda i: (jnp.maximum(i - steps, 0), 0)),
        ]
        + [pl.BlockSpec(k.shape, lambda i: (0, 0)) for k in ks]
        + [pl.BlockSpec((1, keys), lambda i: (0, 0))],
        out_specs=[
            pl.BlockSpec((tile, keys), lambda i: (i, 0)),
            pl.BlockSpec((tile, 256), lambda i: (i, 0)),
        ],
        out_shape=[
            jax.ShapeDtypeStruct((2 * half, keys), BF),
            jax.ShapeDtypeStruct((2 * half, 256), F32),
        ],
        compiler_params=pltpu.CompilerParams(vmem_limit_bytes=40 * 2**20),
        cost_estimate=pl.CostEstimate(
            flops=2 * 2 * half * keys * HEAD_DIM, bytes_accessed=2 * 2 * half * keys, transcendentals=2 * half * keys
        ),
    )(q_own, q_other, *ks, bias)


def values_body(p_ref, v0, v1, v2, v3, mine, theirs, live, out):
    acc = jnp.zeros(out.shape, F32)
    for i, v in enumerate((v0, v1, v2, v3)):
        width = v.shape[0]
        acc += jnp.dot(p_ref[:, i * width : (i + 1) * width], v[...], preferred_element_type=F32)
    top_mine, top_theirs = mine[:, :128], theirs[:, :128]
    top = jnp.maximum(top_mine, top_theirs)
    fade = jnp.exp2(top_mine - top)
    total = mine[:, 128:] * fade + theirs[:, 128:] * jnp.exp2(top_theirs - top)
    factor = fade / total * live[...]
    out[:, :128] = acc[:, :128] * factor
    out[:, 128:] = acc[:, 128:] * factor


def value_kernel(p, vs, mine, theirs, live):
    rows, keys = p.shape
    tile = 256
    return pl.pallas_call(
        values_body,
        grid=(rows // tile,),
        in_specs=[pl.BlockSpec((tile, keys), lambda i: (i, 0))]
        + [pl.BlockSpec(v.shape, lambda i: (0, 0)) for v in vs]
        + [pl.BlockSpec((tile, 256), lambda i: (i, 0))] * 2
        + [pl.BlockSpec((tile, 1), lambda i: (i, 0))],
        out_specs=pl.BlockSpec((tile, HEAD_DIM), lambda i: (i, 0)),
        out_shape=jax.ShapeDtypeStruct((rows, HEAD_DIM), F32),
        compiler_params=pltpu.CompilerParams(vmem_limit_bytes=40 * 2**20),
        cost_estimate=pl.CostEstimate(flops=2 * rows * keys * HEAD_DIM, bytes_accessed=4 * rows * keys, transcendentals=0),
    )(p, *vs, mine, theirs, live)


def local(query_rows, key_rows, value_rows, seq_length, out_weight, out_grad):
    query, key, value = query_rows[0], key_rows[0], value_rows[0]
    length = seq_length[0]
    count = query.shape[0]
    xh, zq, zr, core, y = (lax.axis_index(n) for n in ("xh", "zq", "zr", "core", "y"))

    def head_of(array, steps):
        return lax.dynamic_slice_in_dim(array, ((zq + steps) % 4) * HEAD_DIM, HEAD_DIM, 1)

    kq = [jnp.stack([head_of(key, d), head_of(query, d)]) for d in range(4)]
    kq = [kq[0]] + [moved(kq[d], {"zq": d}) for d in (1, 2, 3)]
    vv = [head_of(value, 0)] + [moved(head_of(value, d), {"zq": d}) for d in (1, 2, 3)]
    q_own = jnp.concatenate([pair[1] for pair in kq])
    k_own = jnp.concatenate([pair[0] for pair in kq])
    v_own = jnp.concatenate(vv)
    q_other = moved(q_own, {"core": 1})
    quad = ({"zr": 1}, {"xh": 1}, {"xh": 1, "zr": 1})
    ks = [k_own] + [moved(k_own, s) for s in quad]
    vs = [v_own] + [moved(v_own, s) for s in quad]

    def positions(xh, zr, core):
        source = (zq - jnp.arange(4)) % 4
        block = xh * 16 + source * 4 + zr * 2 + core
        return (block[:, None] * count + jnp.arange(count)[None, :]).reshape(-1)

    key_place = jnp.concatenate(
        [positions(xh, zr, core), positions(xh, 1 - zr, core), positions(1 - xh, zr, core), positions(1 - xh, 1 - zr, core)]
    )
    bias = jnp.where(key_place < length, 0.0, MASKED).astype(F32)[None, :]
    query_place = jnp.concatenate([positions(xh, zr, core), positions(xh, zr, 1 - core)])
    live = (query_place < length).astype(F32)[:, None]

    weights, mine = score_kernel(q_own, q_other, ks, bias)
    theirs_swapped = moved(mine, {"core": 1})
    half = q_own.shape[0]
    theirs = jnp.concatenate([theirs_swapped[half:], theirs_swapped[:half]])
    partial = value_kernel(weights, vs, mine, theirs, live)
    from_other = moved(partial, {"core": 1})
    context_own = (partial[:half] + from_other[half:]).astype(BF)
    context_other = (partial[half:] + from_other[:half]).astype(BF)

    grad = out_grad[0]
    rows, width = grad.shape
    grad = grad.reshape(rows, 16, 2, 64)
    keep = lax.dynamic_index_in_dim(grad, core, 2, keepdims=False).reshape(rows, width // 2)
    give = lax.dynamic_index_in_dim(grad, 1 - core, 2, keepdims=False).reshape(rows, width // 2)
    grad = jnp.stack([keep, moved(give, {"core": 1})])
    grad = jnp.stack([grad] + [moved(grad, {"zq": d}) for d in (1, 2, 3)])
    grads = [grad] + [moved(grad, {"y": d}) for d in (1, 2, 3)]
    contexts = jnp.stack([context_own, context_other]).reshape(2, 4, 4, rows, HEAD_DIM)
    total = jnp.zeros((width // 2, HEAD_DIM), F32)
    for d in range(4):
        part = lax.dynamic_index_in_dim(contexts, (y - d) % 4, 2, keepdims=False)
        part = part.transpose(1, 0, 2, 3).reshape(8 * rows, HEAD_DIM)
        total += lax.dot_general(
            grads[d].reshape(8 * rows, width // 2), part, (((0,), (0,)), ((), ())), preferred_element_type=F32
        )
    xl = lax.axis_index("xl")
    total = total.reshape(2, 4, 2, 2, 32, HEAD_DIM)

    def for_x(dh, dl):
        part = lax.dynamic_index_in_dim(total, (xh + dh) % 2, 0, keepdims=False)
        return lax.dynamic_index_in_dim(part, (xl + dl) % 2, 2, keepdims=False)

    summed = for_x(0, 0)
    for dh, dl in ((0, 1), (1, 0), (1, 1)):
        summed += moved(for_x(dh, dl).astype(BF), {"xh": dh, "xl": dl}).astype(F32)
    keep = lax.dynamic_index_in_dim(summed, zr, 1, keepdims=False)
    give = lax.dynamic_index_in_dim(summed, 1 - zr, 1, keepdims=False)
    summed = keep + moved(give.astype(BF), {"zr": 1}).astype(F32)

    def for_zq(steps):
        return lax.dynamic_index_in_dim(summed, (zq + steps) % 4, 0, keepdims=False)

    heads = [for_zq(0)] + [moved(for_zq(d), {"zq": d}) for d in (1, 2, 3)]
    weight_grad = jnp.zeros((4, 32, HEAD_DIM), F32)
    for d, part in enumerate(heads):
        weight_grad = lax.dynamic_update_index_in_dim(weight_grad, part, (zq - d) % 4, 0)
    weight_grad = weight_grad.transpose(0, 2, 1).reshape(4 * HEAD_DIM, 32)

    back = context_own.reshape(4, count, HEAD_DIM)
    mine_back = jnp.zeros((count, 4 * HEAD_DIM), BF)
    for d in range(4):
        part = back[d] if d == 0 else moved(back[d], {"zq": -d})
        mine_back = lax.dynamic_update_slice_in_dim(mine_back, part, ((zq + d) % 4) * HEAD_DIM, 1)
    projected = jnp.dot(mine_back, out_weight, preferred_element_type=F32).reshape(4, rows, width)

    def for_y(steps):
        return lax.dynamic_index_in_dim(projected, (y + steps) % 4, 0, keepdims=False)

    block = for_y(0)
    for d in (1, 2, 3):
        block += moved(for_y(d).astype(BF), {"y": d}).astype(F32)
    return block.astype(BF)[None], weight_grad


def solution(mesh):
    fine = Mesh(mesh.devices.reshape([s for _, s in SPLIT]), AXES)
    ctx = ("xh", "zq", "zr", "core")
    in_specs = (
        P("xl", ctx, "y"),
        P("xl", ctx, "y"),
        P("xl", ctx, "y"),
        P("xl"),
        P("y", None),
        P("xl", ctx + ("y",), None),
    )
    out_specs = (P("xl", ctx + ("y",), None), P("y", ctx + ("xl",)))
    return jax.shard_map(local, mesh=fine, in_specs=in_specs, out_specs=out_specs, check_vma=False)
```

time: 703 us -> 160 us (0.23)
  waiting for transfers between devices: 608 us -> 71 us
  starting transfers between devices: 2.66 us -> 69.7 us
  matrix products: 30.7 us -> 2.14 us
  other arithmetic: 24.6 us -> 1.7 us
  blocking collectives: 13.5 us -> 0 us
  between operations: 14.8 us -> 1.79 us
    reduce_scatter x2 -> x0, waiting for transfers between devices: 276 us -> none  [the longest x1 276 us: local(): lax.psum_scatter(grad_total, ('ctx', 'dp'), scatter_dimension=1, tiled=True)]
    ppermute x31 -> x35, waiting for transfers between devices: 331 us -> 71 us  [moved(): return lax.ppermute(value, names, pairs)]
    ppermute x31 -> x35, starting transfers between devices: 2.58 us -> 69.7 us  [moved(): return lax.ppermute(value, names, pairs)]
    dot_general x66 -> x5, matrix products: 30.7 us -> 2.14 us  [the longest x4 1.42 us: local(): lax.dot_general(grads[d].reshape(8 * rows, width // 2), part, (((0,), (0,...]
    lt x32 -> x0, other arithmetic: 20.3 us -> none  [attend(): live_keys = (key_start + jnp.arange(key_count) < length)[None, None, :]]
    all_gather x1 -> x0, blocking collectives: 13.5 us -> none  [local(): lax.all_gather(out_grad[0], 'grp', axis=0, tiled=True)]
  transfers between devices with their start and end apart: 33 -> 35, of which waited for: 32 -> 20; matrix products, arithmetic and copies ran while one was open for 7% -> 5% of each run, Pallas kernels for 0% -> 0%
where the time goes in v1:
time: 160 us; the launch traced here: 159 us
  waiting for transfers between devices  71 us (44%)
  starting transfers between devices  69.7 us (44%)
  local copies, waits for them, and re-layouts  7.43 us (5%)
  Pallas kernels  5.18 us (3%)
  matrix products  2.14 us (1%)
  between operations  1.79 us (1%)
  other arithmetic  1.7 us (1%)
    ppermute x35, waiting for transfers between devices, moved(): return lax.ppermute(value, names, pairs)  71 us
    ppermute x35, starting transfers between devices, moved(): return lax.ppermute(value, names, pairs)  69.7 us
    pallas_call x1, Pallas kernels, score_kernel(): pl.pallas_call(scores_body, grid=(2 * steps,), in_specs=[pl.BlockSpec((ti...  3.4 us
  transfers between devices with their start and end apart: 35, of which 20 were waited for; matrix products, arithmetic and copies ran while one was open for 5% of the time, Pallas kernels for 0%

profile of v1, /device:TPU:8, one launch (start us, length us, event | category | flops | bytes accessed | tf_op | source)
XLA Modules:
  0.0 159.0 jit_solution(6628418801461672590)
XLA Ops:
  1.8 3.3 %collective-permute-start = (bf16[2,128,256]{2,1,0:T(8,128)(2,1)S(1)}, bf16[2,128,256]{2,1,0:T(8,128)(2,1)S(1)}, u32[]{:S(2)}, u32[]{:S(2)}) collective-permute-start(bf16[2,128,256]{2,1,0:T(8,128)(2,1)S(1)} %pad_maximum_fusion.5), channel_id=1, source_target_pairs={{0,32},{32,64},{64,96},{96,0},{1,33},{33,65},{65,97},{97,1},{2,34}... | collective-permute-start | bytes 393224 | tf_op jit(solution)/shard_map/ppermute | solution.py:34
  5.2 5.5 %collective-permute-start.1 = (bf16[2,128,256]{2,1,0:T(8,128)(2,1)S(1)}, bf16[2,128,256]{2,1,0:T(8,128)(2,1)S(1)}, u32[]{:S(2)}, u32[]{:S(2)}) collective-permute-start(bf16[2,128,256]{2,1,0:T(8,128)(2,1)S(1)} %pad_maximum_fusion.6), channel_id=1, source_target_pairs={{0,64},{32,96},{64,0},{96,32},{1,65},{33,97},{65,1},{97,33},{2,66}... | collective-permute-start | bytes 393224 | tf_op jit(solution)/shard_map/ppermute | solution.py:34
  10.7 2.7 %collective-permute-start.2 = (bf16[2,128,256]{2,1,0:T(8,128)(2,1)S(1)}, bf16[2,128,256]{2,1,0:T(8,128)(2,1)S(1)}, u32[]{:S(2)}, u32[]{:S(2)}) collective-permute-start(bf16[2,128,256]{2,1,0:T(8,128)(2,1)S(1)} %pad_maximum_fusion.7), channel_id=1, source_target_pairs={{0,96},{32,0},{64,32},{96,64},{1,97},{33,1},{65,33},{97,65},{2,98}... | collective-permute-start | bytes 393224 | tf_op jit(solution)/shard_map/ppermute | solution.py:34
  13.7 5.8 %collective-permute-done.1 = bf16[2,128,256]{2,1,0:T(8,128)(2,1)S(1)} collective-permute-done((bf16[2,128,256]{2,1,0:T(8,128)(2,1)S(1)}, bf16[2,128,256]{2,1,0:T(8,128)(2,1)S(1)}, u32[]{:S(2)}, u32[]{:S(2)}) %collective-permute-start.1) | collective-permute-done | bytes 131104 | tf_op jit(solution)/shard_map/ppermute | solution.py:34
  19.6 3.2 %collective-permute-done.2 = bf16[2,128,256]{2,1,0:T(8,128)(2,1)S(1)} collective-permute-done((bf16[2,128,256]{2,1,0:T(8,128)(2,1)S(1)}, bf16[2,128,256]{2,1,0:T(8,128)(2,1)S(1)}, u32[]{:S(2)}, u32[]{:S(2)}) %collective-permute-start.2) | collective-permute-done | bytes 131104 | tf_op jit(solution)/shard_map/ppermute | solution.py:34
  22.9 3.1 %collective-permute-start.5 = (bf16[512,256]{1,0:T(8,128)(2,1)S(1)}, bf16[512,256]{1,0:T(8,128)(2,1)S(1)}, u32[]{:S(2)}, u32[]{:S(2)}) collective-permute-start(bf16[512,256]{1,0:T(8,128)(2,1)S(1)} %pad_maximum_fusion.3.k0), channel_id=1, source_target_pairs={{0,128},{128,0},{1,129},{129,1},{2,130},{130,2},{3,131},{131,3},{4... | collective-permute-start | bytes 786440 | tf_op jit(solution)/shard_map/ppermute | solution.py:34
  28.8 3.3 %collective-permute-done.4.k1 = bf16[512,256]{1,0:T(8,128)(2,1)S(1)} collective-permute-done((bf16[512,256]{1,0:T(8,128)(2,1)S(1)}, bf16[512,256]{1,0:T(8,128)(2,1)S(1)}, u32[]{:S(2)}, u32[]{:S(2)}) %collective-permute-start.4) | collective-permute-done | bytes 262176 | tf_op jit(solution)/shard_map/ppermute | solution.py:34
  32.1 5.3 %collective-permute-done.5.k2 = bf16[512,256]{1,0:T(8,128)(2,1)S(1)} collective-permute-done((bf16[512,256]{1,0:T(8,128)(2,1)S(1)}, bf16[512,256]{1,0:T(8,128)(2,1)S(1)}, u32[]{:S(2)}, u32[]{:S(2)}) %collective-permute-start.5) | collective-permute-done | bytes 262176 | tf_op jit(solution)/shard_map/ppermute | solution.py:34
  39.2 3.4 %shard_map.77 = (bf16[1024,2048]{1,0:T(8,128)(2,1)S(1)}, f32[1024,256]{1,0:T(8,128)S(1)}) custom-call(bf16[512,256]{1,0:T(8,128)(2,1)S(1)} %pad_maximum_fusion.2.q0, bf16[512,256]{1,0:T(8,128)(2,1)S(1)} %collective-permute-done.3.q1, bf16[512,256]{1,0:T(8,128)(2,1)S(1)} %pad_maximum_fusion.3.k0, bf16[512,256]{1,0:T(8,128)(2,1)S(1)} %collective-permute-done.4.k1, ...), custom_call_target="tpu_custom_call" | custom-call | flops 1073741824 | bytes 4194304 | tf_op jit(solution)/shard_map/pallas_call | solution.py:74
  46.1 4.6 %collective-permute-start.8 = (bf16[128,256]{1,0:T(8,128)(2,1)S(1)}, bf16[128,256]{1,0:T(8,128)(2,1)S(1)}, u32[]{:S(2)}, u32[]{:S(2)}) collective-permute-start(bf16[128,256]{1,0:T(8,128)(2,1)S(1)} %get-tuple-element.29), channel_id=1, source_target_pairs={{0,64},{32,96},{64,0},{96,32},{1,65},{33,97},{65,1},{97,33},{2,66}... | collective-permute-start | bytes 196616 | tf_op jit(solution)/shard_map/ppermute | solution.py:34
  53.2 4.1 %collective-permute-done.8 = bf16[128,256]{1,0:T(8,128)(2,1)S(1)} collective-permute-done((bf16[128,256]{1,0:T(8,128)(2,1)S(1)}, bf16[128,256]{1,0:T(8,128)(2,1)S(1)}, u32[]{:S(2)}, u32[]{:S(2)}) %collective-permute-start.8) | collective-permute-done | bytes 65568 | tf_op jit(solution)/shard_map/ppermute | solution.py:34
  58.0 3.2 %collective-permute-start.11 = (bf16[512,256]{1,0:T(8,128)(2,1)S(1)}, bf16[512,256]{1,0:T(8,128)(2,1)S(1)}, u32[]{:S(2)}, u32[]{:S(2)}) collective-permute-start(bf16[512,256]{1,0:T(8,128)(2,1)S(1)} %pad_maximum_fusion.4.v0), channel_id=1, source_target_pairs={{0,128},{128,0},{1,129},{129,1},{2,130},{130,2},{3,131},{131,3},{4... | collective-permute-start | bytes 786440 | tf_op jit(solution)/shard_map/ppermute | solution.py:34
  63.2 4.0 %collective-permute-done.10.v1 = bf16[512,256]{1,0:T(8,128)(2,1)S(1)} collective-permute-done((bf16[512,256]{1,0:T(8,128)(2,1)S(1)}, bf16[512,256]{1,0:T(8,128)(2,1)S(1)}, u32[]{:S(2)}, u32[]{:S(2)}) %collective-permute-start.10) | collective-permute-done | bytes 262176 | tf_op jit(solution)/shard_map/ppermute | solution.py:34
  67.2 5.3 %collective-permute-done.11.v2 = bf16[512,256]{1,0:T(8,128)(2,1)S(1)} collective-permute-done((bf16[512,256]{1,0:T(8,128)(2,1)S(1)}, bf16[512,256]{1,0:T(8,128)(2,1)S(1)}, u32[]{:S(2)}, u32[]{:S(2)}) %collective-permute-start.11) | collective-permute-done | bytes 262176 | tf_op jit(solution)/shard_map/ppermute | solution.py:34
  81.1 4.9 %collective-permute-start.23 = (bf16[2,32,1024]{2,1,0:T(8,128)(2,1)S(1)}, bf16[2,32,1024]{2,1,0:T(8,128)(2,1)S(1)}, u32[]{:S(2)}, u32[]{:S(2)}) collective-permute-start(bf16[2,32,1024]{2,1,0:T(8,128)(2,1)S(1)} %get-tuple-element.43), channel_id=1, source_target_pairs={{0,64},{32,96},{64,0},{96,32},{1,65},{33,97},{65,1},{97,33},{2,66}... | collective-permute-start | bytes 393224 | tf_op jit(solution)/shard_map/ppermute | solution.py:34
  89.4 8.0 %collective-permute-done.23 = bf16[2,32,1024]{2,1,0:T(8,128)(2,1)S(1)} collective-permute-done((bf16[2,32,1024]{2,1,0:T(8,128)(2,1)S(1)}, bf16[2,32,1024]{2,1,0:T(8,128)(2,1)S(1)}, u32[]{:S(2)}, u32[]{:S(2)}) %collective-permute-start.23) | collective-permute-done | bytes 131104 | tf_op jit(solution)/shard_map/ppermute | solution.py:34
  104.1 3.6 %collective-permute-start.15 = (bf16[128,256]{1,0:T(8,128)(2,1)S(1)}, bf16[128,256]{1,0:T(8,128)(2,1)S(1)}, u32[]{:S(2)}, u32[]{:S(2)}) collective-permute-start(bf16[128,256]{1,0:T(8,128)(2,1)S(1)} %get-tuple-element.24), channel_id=1, source_target_pairs={{0,96},{32,0},{64,32},{96,64},{1,97},{33,1},{65,33},{97,65},{2,98}... | collective-permute-start | bytes 196616 | tf_op jit(solution)/shard_map/ppermute | solution.py:34
  107.7 6.0 %collective-permute-done.25 = bf16[4,2,32,1024]{3,2,1,0:T(8,128)(2,1)S(1)} collective-permute-done((bf16[4,2,32,1024]{3,2,1,0:T(8,128)(2,1)S(1)}, bf16[4,2,32,1024]{3,2,1,0:T(8,128)(2,1)S(1)}, u32[]{:S(2)}, u32[]{:S(2)}) %collective-permute-start.25) | collective-permute-done | bytes 524320 | tf_op jit(solution)/shard_map/ppermute | solution.py:34
  114.1 2.8 %collective-permute-done.26 = bf16[4,2,32,1024]{3,2,1,0:T(8,128)(2,1)S(1)} collective-permute-done((bf16[4,2,32,1024]{3,2,1,0:T(8,128)(2,1)S(1)}, bf16[4,2,32,1024]{3,2,1,0:T(8,128)(2,1)S(1)}, u32[]{:S(2)}, u32[]{:S(2)}) %collective-permute-start.26) | collective-permute-done | bytes 524320 | tf_op jit(solution)/shard_map/ppermute | solution.py:34
  117.2 8.9 %collective-permute-done.27 = bf16[4,2,32,1024]{3,2,1,0:T(8,128)(2,1)S(1)} collective-permute-done((bf16[4,2,32,1024]{3,2,1,0:T(8,128)(2,1)S(1)}, bf16[4,2,32,1024]{3,2,1,0:T(8,128)(2,1)S(1)}, u32[]{:S(2)}, u32[]{:S(2)}) %collective-permute-start.27) | collective-permute-done | bytes 524320 | tf_op jit(solution)/shard_map/ppermute | solution.py:34
  128.5 2.7 %collective-permute-start.29 = (bf16[4,2,32,256]{3,2,1,0:T(8,128)(2,1)S(1)}, bf16[4,2,32,256]{3,2,1,0:T(8,128)(2,1)S(1)}, u32[]{:S(2)}, u32[]{:S(2)}) collective-permute-start(bf16[4,2,32,256]{3,2,1,0:T(8,128)(2,1)S(1)} %get-tuple-element.12), channel_id=1, source_target_pairs={{0,128},{1,129},{128,0},{129,1},{2,130},{3,131},{130,2},{131,3},{4... | collective-permute-start | bytes 393224 | tf_op jit(solution)/shard_map/ppermute | solution.py:34
  133.9 3.7 %collective-permute-start.17 = (bf16[128,256]{1,0:T(8,128)(2,1)S(1)}, bf16[128,256]{1,0:T(8,128)(2,1)S(1)}, u32[]{:S(2)}, u32[]{:S(2)}) collective-permute-start(bf16[128,256]{1,0:T(8,128)(2,1)S(1)} %get-tuple-element.22), channel_id=1, source_target_pairs={{0,32},{32,64},{64,96},{96,0},{1,33},{33,65},{65,97},{97,1},{2,34}... | collective-permute-start | bytes 196616 | tf_op jit(solution)/shard_map/ppermute | solution.py:34
  137.6 4.3 %collective-permute-done.16 = bf16[128,256]{1,0:T(8,128)(2,1)S(1)} collective-permute-done((bf16[128,256]{1,0:T(8,128)(2,1)S(1)}, bf16[128,256]{1,0:T(8,128)(2,1)S(1)}, u32[]{:S(2)}, u32[]{:S(2)}) %collective-permute-start.16) | collective-permute-done | bytes 65568 | tf_op jit(solution)/shard_map/ppermute | solution.py:34
  149.4 3.6 %collective-permute-start.33 = (f32[32,256]{1,0:T(8,128)S(1)}, f32[32,256]{1,0:T(8,128)S(1)}, u32[]{:S(2)}, u32[]{:S(2)}) collective-permute-start(f32[32,256]{1,0:T(8,128)S(1)} %get-tuple-element.39), channel_id=1, source_target_pairs={{0,64},{32,96},{64,0},{96,32},{1,65},{33,97},{65,1},{97,33},{2,66}... | collective-permute-start | bytes 98312 | tf_op jit(solution)/shard_map/ppermute | solution.py:34
  (117 shorter events, 51.7 us)
Async XLA Ops:
  1.8 11.9 %collective-permute-start = (bf16[2,128,256]{2,1,0:T(8,128)(2,1)S(1)}, bf16[2,128,256]{2,1,0:T(8,128)(2,1)S(1)}, u32[]{:S(2)}, u32[]{:S(2)}) collective-permute-start(bf16[2,128,256]{2,1,0:T(8,128)(2,1)S(1)} %pad_maximum_fusion.5), channel_id=1, source_target_pairs={{0,32},{32,64},{64,96},{96,0},{1,33},{33,65},{65,97},{97,1},{2,34}... | collective-permute-start | bytes 393224 | tf_op jit(solution)/shard_map/ppermute | solution.py:34
  5.2 14.4 %collective-permute-start.1 = (bf16[2,128,256]{2,1,0:T(8,128)(2,1)S(1)}, bf16[2,128,256]{2,1,0:T(8,128)(2,1)S(1)}, u32[]{:S(2)}, u32[]{:S(2)}) collective-permute-start(bf16[2,128,256]{2,1,0:T(8,128)(2,1)S(1)} %pad_maximum_fusion.6), channel_id=1, source_target_pairs={{0,64},{32,96},{64,0},{96,32},{1,65},{33,97},{65,1},{97,33},{2,66}... | collective-permute-start | bytes 393224 | tf_op jit(solution)/shard_map/ppermute | solution.py:34
  10.7 12.1 %collective-permute-start.2 = (bf16[2,128,256]{2,1,0:T(8,128)(2,1)S(1)}, bf16[2,128,256]{2,1,0:T(8,128)(2,1)S(1)}, u32[]{:S(2)}, u32[]{:S(2)}) collective-permute-start(bf16[2,128,256]{2,1,0:T(8,128)(2,1)S(1)} %pad_maximum_fusion.7), channel_id=1, source_target_pairs={{0,96},{32,0},{64,32},{96,64},{1,97},{33,1},{65,33},{97,65},{2,98}... | collective-permute-start | bytes 393224 | tf_op jit(solution)/shard_map/ppermute | solution.py:34
  22.9 14.5 %collective-permute-start.5 = (bf16[512,256]{1,0:T(8,128)(2,1)S(1)}, bf16[512,256]{1,0:T(8,128)(2,1)S(1)}, u32[]{:S(2)}, u32[]{:S(2)}) collective-permute-start(bf16[512,256]{1,0:T(8,128)(2,1)S(1)} %pad_maximum_fusion.3.k0), channel_id=1, source_target_pairs={{0,128},{128,0},{1,129},{129,1},{2,130},{130,2},{3,131},{131,3},{4... | collective-permute-start | bytes 786440 | tf_op jit(solution)/shard_map/ppermute | solution.py:34
  26.1 13.2 %collective-permute-start.6 = (bf16[512,256]{1,0:T(8,128)(2,1)S(1)}, bf16[512,256]{1,0:T(8,128)(2,1)S(1)}, u32[]{:S(2)}, u32[]{:S(2)}) collective-permute-start(bf16[512,256]{1,0:T(8,128)(2,1)S(1)} %pad_maximum_fusion.3.k0), channel_id=1, source_target_pairs={{0,144},{16,128},{128,16},{144,0},{1,145},{17,129},{129,17},{145,1... | collective-permute-start | bytes 786440 | tf_op jit(solution)/shard_map/ppermute | solution.py:34
  27.9 11.3 %collective-permute-start.3 = (bf16[512,256]{1,0:T(8,128)(2,1)S(1)}, bf16[512,256]{1,0:T(8,128)(2,1)S(1)}, u32[]{:S(2)}, u32[]{:S(2)}) collective-permute-start(bf16[512,256]{1,0:T(8,128)(2,1)S(1)} %pad_maximum_fusion.2.q0), channel_id=1, source_target_pairs={{0,8},{8,0},{1,9},{9,1},{2,10},{10,2},{3,11},{11,3},{4,12},{12,4},... | collective-permute-start | bytes 786440 | tf_op jit(solution)/shard_map/ppermute | solution.py:34
  44.6 18.4 %collective-permute-start.13 = (f32[1024,256]{1,0:T(8,128)S(1)}, f32[1024,256]{1,0:T(8,128)S(1)}, u32[]{:S(2)}, u32[]{:S(2)}) collective-permute-start(f32[1024,256]{1,0:T(8,128)S(1)} %get-tuple-element.5.mine), channel_id=1, source_target_pairs={{0,8},{8,0},{1,9},{9,1},{2,10},{10,2},{3,11},{11,3},{4,12},{12,4},... | collective-permute-start | bytes 3145736 | tf_op jit(solution)/shard_map/ppermute | solution.py:34
  46.1 11.3 %collective-permute-start.8 = (bf16[128,256]{1,0:T(8,128)(2,1)S(1)}, bf16[128,256]{1,0:T(8,128)(2,1)S(1)}, u32[]{:S(2)}, u32[]{:S(2)}) collective-permute-start(bf16[128,256]{1,0:T(8,128)(2,1)S(1)} %get-tuple-element.29), channel_id=1, source_target_pairs={{0,64},{32,96},{64,0},{96,32},{1,65},{33,97},{65,1},{97,33},{2,66}... | collective-permute-start | bytes 196616 | tf_op jit(solution)/shard_map/ppermute | solution.py:34
  58.0 14.5 %collective-permute-start.11 = (bf16[512,256]{1,0:T(8,128)(2,1)S(1)}, bf16[512,256]{1,0:T(8,128)(2,1)S(1)}, u32[]{:S(2)}, u32[]{:S(2)}) collective-permute-start(bf16[512,256]{1,0:T(8,128)(2,1)S(1)} %pad_maximum_fusion.4.v0), channel_id=1, source_target_pairs={{0,128},{128,0},{1,129},{129,1},{2,130},{130,2},{3,131},{131,3},{4... | collective-permute-start | bytes 786440 | tf_op jit(solution)/shard_map/ppermute | solution.py:34
  61.2 13.1 %collective-permute-start.12 = (bf16[512,256]{1,0:T(8,128)(2,1)S(1)}, bf16[512,256]{1,0:T(8,128)(2,1)S(1)}, u32[]{:S(2)}, u32[]{:S(2)}) collective-permute-start(bf16[512,256]{1,0:T(8,128)(2,1)S(1)} %pad_maximum_fusion.4.v0), channel_id=1, source_target_pairs={{0,144},{16,128},{128,16},{144,0},{1,145},{17,129},{129,17},{145,1... | collective-permute-start | bytes 786440 | tf_op jit(solution)/shard_map/ppermute | solution.py:34
  76.1 27.7 %collective-permute-start.14 = (f32[1024,256]{1,0:T(8,128)S(1)}, f32[1024,256]{1,0:T(8,128)S(1)}, u32[]{:S(2)}, u32[]{:S(2)}) collective-permute-start(f32[1024,256]{1,0:T(8,128)S(1)} %shard_map.78), channel_id=1, source_target_pairs={{0,8},{8,0},{1,9},{9,1},{2,10},{10,2},{3,11},{11,3},{4,12},{12,4},... | collective-permute-start | bytes 3145736 | tf_op jit(solution)/shard_map/ppermute | solution.py:34
  80.1 9.3 %collective-permute-start.22 = (bf16[2,32,1024]{2,1,0:T(8,128)(2,1)S(1)}, bf16[2,32,1024]{2,1,0:T(8,128)(2,1)S(1)}, u32[]{:S(2)}, u32[]{:S(2)}) collective-permute-start(bf16[2,32,1024]{2,1,0:T(8,128)(2,1)S(1)} %get-tuple-element.43), channel_id=1, source_target_pairs={{0,32},{32,64},{64,96},{96,0},{1,33},{33,65},{65,97},{97,1},{2,34}... | collective-permute-start | bytes 393224 | tf_op jit(solution)/shard_map/ppermute | solution.py:34
  81.1 16.2 %collective-permute-start.23 = (bf16[2,32,1024]{2,1,0:T(8,128)(2,1)S(1)}, bf16[2,32,1024]{2,1,0:T(8,128)(2,1)S(1)}, u32[]{:S(2)}, u32[]{:S(2)}) collective-permute-start(bf16[2,32,1024]{2,1,0:T(8,128)(2,1)S(1)} %get-tuple-element.43), channel_id=1, source_target_pairs={{0,64},{32,96},{64,0},{96,32},{1,65},{33,97},{65,1},{97,33},{2,66}... | collective-permute-start | bytes 393224 | tf_op jit(solution)/shard_map/ppermute | solution.py:34
  86.0 12.8 %collective-permute-start.24 = (bf16[2,32,1024]{2,1,0:T(8,128)(2,1)S(1)}, bf16[2,32,1024]{2,1,0:T(8,128)(2,1)S(1)}, u32[]{:S(2)}, u32[]{:S(2)}) collective-permute-start(bf16[2,32,1024]{2,1,0:T(8,128)(2,1)S(1)} %get-tuple-element.43), channel_id=1, source_target_pairs={{0,96},{32,0},{64,32},{96,64},{1,97},{33,1},{65,33},{97,65},{2,98}... | collective-permute-start | bytes 393224 | tf_op jit(solution)/shard_map/ppermute | solution.py:34
  98.9 14.9 %collective-permute-start.25 = (bf16[4,2,32,1024]{3,2,1,0:T(8,128)(2,1)S(1)}, bf16[4,2,32,1024]{3,2,1,0:T(8,128)(2,1)S(1)}, u32[]{:S(2)}, u32[]{:S(2)}) collective-permute-start(bf16[4,2,32,1024]{3,2,1,0:T(8,128)(2,1)S(1)} %pad_maximum_fusion.1), channel_id=1, source_target_pairs={{0,2},{2,4},{4,6},{6,0},{1,3},{3,5},{5,7},{7,1},{8,10},{10,12},{12... | collective-permute-start | bytes 1572872 | tf_op jit(solution)/shard_map/ppermute | solution.py:34
  100.5 16.3 %collective-permute-start.26 = (bf16[4,2,32,1024]{3,2,1,0:T(8,128)(2,1)S(1)}, bf16[4,2,32,1024]{3,2,1,0:T(8,128)(2,1)S(1)}, u32[]{:S(2)}, u32[]{:S(2)}) collective-permute-start(bf16[4,2,32,1024]{3,2,1,0:T(8,128)(2,1)S(1)} %pad_maximum_fusion.1), channel_id=1, source_target_pairs={{0,4},{2,6},{4,0},{6,2},{1,5},{3,7},{5,1},{7,3},{8,12},{10,14},{12... | collective-permute-start | bytes 1572872 | tf_op jit(solution)/shard_map/ppermute | solution.py:34
  101.5 24.7 %collective-permute-start.27 = (bf16[4,2,32,1024]{3,2,1,0:T(8,128)(2,1)S(1)}, bf16[4,2,32,1024]{3,2,1,0:T(8,128)(2,1)S(1)}, u32[]{:S(2)}, u32[]{:S(2)}) collective-permute-start(bf16[4,2,32,1024]{3,2,1,0:T(8,128)(2,1)S(1)} %pad_maximum_fusion.1), channel_id=1, source_target_pairs={{0,6},{2,0},{4,2},{6,4},{1,7},{3,1},{5,3},{7,5},{8,14},{10,8},{12,... | collective-permute-start | bytes 1572872 | tf_op jit(solution)/shard_map/ppermute | solution.py:34
  104.1 29.8 %collective-permute-start.15 = (bf16[128,256]{1,0:T(8,128)(2,1)S(1)}, bf16[128,256]{1,0:T(8,128)(2,1)S(1)}, u32[]{:S(2)}, u32[]{:S(2)}) collective-permute-start(bf16[128,256]{1,0:T(8,128)(2,1)S(1)} %get-tuple-element.24), channel_id=1, source_target_pairs={{0,96},{32,0},{64,32},{96,64},{1,97},{33,1},{65,33},{97,65},{2,98}... | collective-permute-start | bytes 196616 | tf_op jit(solution)/shard_map/ppermute | solution.py:34
  126.9 15.7 %collective-permute-start.28 = (bf16[4,2,32,256]{3,2,1,0:T(8,128)(2,1)S(1)}, bf16[4,2,32,256]{3,2,1,0:T(8,128)(2,1)S(1)}, u32[]{:S(2)}, u32[]{:S(2)}) collective-permute-start(bf16[4,2,32,256]{3,2,1,0:T(8,128)(2,1)S(1)} %get-tuple-element.10), channel_id=1, source_target_pairs={{0,1},{1,0},{128,129},{129,128},{2,3},{3,2},{130,131},{131,130},{4... | collective-permute-start | bytes 393224 | tf_op jit(solution)/shard_map/ppermute | solution.py:34
  128.5 14.2 %collective-permute-start.29 = (bf16[4,2,32,256]{3,2,1,0:T(8,128)(2,1)S(1)}, bf16[4,2,32,256]{3,2,1,0:T(8,128)(2,1)S(1)}, u32[]{:S(2)}, u32[]{:S(2)}) collective-permute-start(bf16[4,2,32,256]{3,2,1,0:T(8,128)(2,1)S(1)} %get-tuple-element.12), channel_id=1, source_target_pairs={{0,128},{1,129},{128,0},{129,1},{2,130},{3,131},{130,2},{131,3},{4... | collective-permute-start | bytes 393224 | tf_op jit(solution)/shard_map/ppermute | solution.py:34
  131.2 11.5 %collective-permute-start.30 = (bf16[4,2,32,256]{3,2,1,0:T(8,128)(2,1)S(1)}, bf16[4,2,32,256]{3,2,1,0:T(8,128)(2,1)S(1)}, u32[]{:S(2)}, u32[]{:S(2)}) collective-permute-start(bf16[4,2,32,256]{3,2,1,0:T(8,128)(2,1)S(1)} %get-tuple-element.11), channel_id=1, source_target_pairs={{0,129},{1,128},{128,1},{129,0},{2,131},{3,130},{130,3},{131,2},{4... | collective-permute-start | bytes 393224 | tf_op jit(solution)/shard_map/ppermute | solution.py:34
  131.7 10.2 %collective-permute-start.16 = (bf16[128,256]{1,0:T(8,128)(2,1)S(1)}, bf16[128,256]{1,0:T(8,128)(2,1)S(1)}, u32[]{:S(2)}, u32[]{:S(2)}) collective-permute-start(bf16[128,256]{1,0:T(8,128)(2,1)S(1)} %get-tuple-element.23), channel_id=1, source_target_pairs={{0,64},{32,96},{64,0},{96,32},{1,65},{33,97},{65,1},{97,33},{2,66}... | collective-permute-start | bytes 196616 | tf_op jit(solution)/shard_map/ppermute | solution.py:34
  143.0 10.1 %collective-permute-start.18 = (bf16[32,2048]{1,0:T(8,128)(2,1)S(1)}, bf16[32,2048]{1,0:T(8,128)(2,1)S(1)}, u32[]{:S(2)}, u32[]{:S(2)}) collective-permute-start(bf16[32,2048]{1,0:T(8,128)(2,1)S(1)} %get-tuple-element.13), channel_id=1, source_target_pairs={{0,2},{2,4},{4,6},{6,0},{1,3},{3,5},{5,7},{7,1},{8,10},{10,12},{12... | collective-permute-start | bytes 393224 | tf_op jit(solution)/shard_map/ppermute | solution.py:34
  144.0 11.7 %collective-permute-start.19 = (bf16[32,2048]{1,0:T(8,128)(2,1)S(1)}, bf16[32,2048]{1,0:T(8,128)(2,1)S(1)}, u32[]{:S(2)}, u32[]{:S(2)}) collective-permute-start(bf16[32,2048]{1,0:T(8,128)(2,1)S(1)} %get-tuple-element.15), channel_id=1, source_target_pairs={{0,4},{2,6},{4,0},{6,2},{1,5},{3,7},{5,1},{7,3},{8,12},{10,14},{12... | collective-permute-start | bytes 393224 | tf_op jit(solution)/shard_map/ppermute | solution.py:34
  (16 other events, 164.7 us)

commit v2 on v1

v2 whole, which is shorter than its diff:
```python
import math

import jax
import jax.numpy as jnp
from jax import lax
from jax.experimental import pallas as pl
from jax.experimental.pallas import tpu as pltpu
from jax.sharding import Mesh, PartitionSpec as P

HEAD_DIM = 256
SPLIT = (("xh", 2), ("zq", 4), ("zr", 2), ("core", 2), ("y", 4), ("xl", 2))
AXES = tuple(name for name, _ in SPLIT)
SIZE = dict(SPLIT)
MASKED = -1e30
BF = jnp.bfloat16
F32 = jnp.float32
VMEM = 14 * 2**20


def moved(value, **shift):
    names = tuple(shift)
    sizes = [SIZE[n] for n in names]
    count = math.prod(sizes)
    pairs = []
    for source in range(count):
        rest, place = source, []
        for s in reversed(sizes):
            place.append(rest % s)
            rest //= s
        place = place[::-1]
        target = 0
        for p, s, n in zip(place, sizes, names):
            target = target * s + (p + shift[n]) % s
        pairs.append((source, target))
    return lax.ppermute(value, names, pairs)


def after(value, *earlier):
    return lax.optimization_barrier((value, *earlier))[0]


def attend_body(q_ref, k0, k1, k2, k3, v0, v1, v2, v3, bias, out, *stat_out):
    tile = q_ref.shape[0]
    q = q_ref[...]
    parts = []
    for i, k in enumerate((k0, k1, k2, k3)):
        s = lax.dot_general(q, k[...], (((1,), (1,)), ((), ())), preferred_element_type=F32)
        width = k.shape[0]
        parts.append(s * (math.log2(math.e) / math.sqrt(HEAD_DIM)) + bias[:, i * width : (i + 1) * width])
    top = parts[0].max(axis=1, keepdims=True)
    for s in parts[1:]:
        top = jnp.maximum(top, s.max(axis=1, keepdims=True))
    total = jnp.zeros((tile, 1), F32)
    acc = jnp.zeros((tile, HEAD_DIM), F32)
    for s, v in zip(parts, (v0, v1, v2, v3)):
        e = jnp.exp2(s - top)
        total += e.sum(axis=1, keepdims=True)
        acc += jnp.dot(e.astype(BF), v[...], preferred_element_type=F32)
    if stat_out:
        out[...] = acc / total
        stat_out[0][:4, :] = jnp.broadcast_to(top, (tile, 128)).T[:4]
        stat_out[0][4:, :] = jnp.broadcast_to(total, (tile, 128)).T[:4]
        return
    step = pl.program_id(0)
    out[pl.ds(pl.multiple_of(step * tile, tile), tile), :] = (acc / total).astype(BF)
    lines = []
    for stat in (top, total):
        left = jnp.broadcast_to(stat, (tile, 128)).T[:1]
        for _ in range(3):
            lines.append(left.astype(BF).astype(F32))
            left = left - lines[-1]
        lines.append(jnp.zeros((5, tile), F32))
    below = pl.multiple_of(pl.num_programs(0) * tile + step * 16, 16)
    out[pl.ds(below, 16), :] = jnp.concatenate(lines).astype(BF)


def attend(q, pieces, bias, dtype):
    rows = q.shape[0]
    tile = 256
    steps = rows // tile
    part = pieces[0].shape[0] // 4
    keys = 4 * part
    if dtype == F32:
        out_specs = [pl.BlockSpec((tile, HEAD_DIM), lambda i: (i, 0)), pl.BlockSpec((8, tile), lambda i: (0, i))]
        out_shape = [jax.ShapeDtypeStruct((rows, HEAD_DIM), F32), jax.ShapeDtypeStruct((8, rows), F32)]
    else:
        out_shape = jax.ShapeDtypeStruct((rows + 16 * steps, HEAD_DIM), BF)
        out_specs = pl.BlockSpec(out_shape.shape, lambda i: (0, 0))
    return pl.pallas_call(
        attend_body,
        grid=(steps,),
        in_specs=[pl.BlockSpec((tile, HEAD_DIM), lambda i: (i, 0))]
        + [pl.BlockSpec((part, HEAD_DIM), lambda i, at=at: (at, 0)) for at in (0, 0, 2, 2, 1, 1, 3, 3)]
        + [pl.BlockSpec((1, keys), lambda i: (0, 0))],
        out_specs=out_specs,
        out_shape=out_shape,
        compiler_params=pltpu.CompilerParams(vmem_limit_bytes=VMEM),
        cost_estimate=pl.CostEstimate(
            flops=4 * rows * keys * HEAD_DIM, bytes_accessed=4 * keys * HEAD_DIM, transcendentals=rows * keys
        ),
    )(q, *pieces * 4, bias)


def combine_body(mine, mine_stat, theirs, theirs_stat, live, out):
    def joined(at):
        parts = theirs_stat[at : at + 8, :].astype(F32)
        return parts[0:1] + parts[1:2] + parts[2:3]

    top_mine, top_theirs = mine_stat[0:1], joined(0)
    top = jnp.maximum(top_mine, top_theirs)
    part_mine = mine_stat[4:5] * jnp.exp2(top_mine - top)
    part_theirs = joined(8) * jnp.exp2(top_theirs - top)
    factor = live[...] / (part_mine + part_theirs)
    tile = out.shape[0]

    def down(row):
        wide = jnp.broadcast_to(row, (128, tile)).T
        return jnp.concatenate([wide, wide], axis=1)

    out[...] = (mine[...] * down(part_mine * factor) + theirs[...].astype(F32) * down(part_theirs * factor)).astype(BF)


def combine(mine, mine_stat, theirs, live):
    rows = mine.shape[0]
    tile = 256
    return pl.pallas_call(
        combine_body,
        grid=(rows // tile,),
        in_specs=[
            pl.BlockSpec((tile, HEAD_DIM), lambda i: (i, 0)),
            pl.BlockSpec((8, tile), lambda i: (0, i)),
            pl.BlockSpec((tile, HEAD_DIM), lambda i: (i, 0)),
            pl.BlockSpec((16, tile), lambda i: (rows // 16 + i, 0)),
            pl.BlockSpec((1, tile), lambda i: (0, i)),
        ],
        out_specs=pl.BlockSpec((tile, HEAD_DIM), lambda i: (i, 0)),
        out_shape=jax.ShapeDtypeStruct((rows, HEAD_DIM), BF),
        compiler_params=pltpu.CompilerParams(vmem_limit_bytes=VMEM // 2),
    )(mine, mine_stat, theirs, theirs, live)


def columns_body(grad, swap, out):
    for xh in range(2):
        for zq in range(4):
            at = (xh * 4 + zq) * 256
            both = jnp.dot(grad[:, at : at + 256], swap[...], preferred_element_type=F32).astype(BF)
            for xl in range(2):
                out[xh, xl, :, zq * 128 : (zq + 1) * 128] = both[:, xl * 128 : (xl + 1) * 128]


def by_owner(grad):
    rows, width = grad.shape
    place = jnp.arange(256)
    source = place % 128 // 32 * 64 + place // 128 * 32 + place % 32
    swap = (place[:, None] == source[None, :]).astype(BF)
    return pl.pallas_call(
        columns_body,
        out_shape=jax.ShapeDtypeStruct((2, 2, rows, width // 4), BF),
        compiler_params=pltpu.CompilerParams(vmem_limit_bytes=VMEM // 2),
        cost_estimate=pl.CostEstimate(flops=2 * rows * width * 256, bytes_accessed=2**19, transcendentals=0),
    )(grad, swap)


def beside(value, dh, dl):
    return moved(value, xh=dh, xl=dl) if dh or dl else value


def local(query_rows, key_rows, value_rows, seq_length, out_weight, out_grad):
    query, key, value = query_rows[0], key_rows[0], value_rows[0]
    length = seq_length[0]
    count = query.shape[0]
    xh, zq, zr, core, y, xl = (lax.axis_index(n) for n in AXES)

    def head_of(array, steps):
        return lax.dynamic_slice_in_dim(array, ((zq + steps) % 4) * HEAD_DIM, HEAD_DIM, 1)

    sent = {d: jnp.concatenate([head_of(key, d), head_of(query, d), head_of(value, d)]) for d in range(4)}
    sent = {d: moved(sent[d], zq=d) if d else sent[d] for d in (1, 3, 2, 0)}
    k_own, q_own, v_own = (
        jnp.concatenate([sent[d][i * count : (i + 1) * count] for d in range(4)]) for i in range(3)
    )
    rows, width = out_grad.shape[1:]
    grad = by_owner(out_grad[0])

    sides = ((0, 0), (0, 1), (1, 1), (1, 0))

    def for_x(dh, dl):
        part = lax.dynamic_index_in_dim(grad, (xh + dh) % 2, 0, keepdims=False)
        return lax.dynamic_index_in_dim(part, (xl + dl) % 2, 0, keepdims=False)

    grad = jnp.stack([beside(for_x(*side), *side) for side in sides])

    def positions(xh, zr, core):
        source = (zq - jnp.arange(4)) % 4
        block = xh * 16 + source * 4 + zr * 2 + core
        return (block[:, None] * count + jnp.arange(count)[None, :]).reshape(-1)

    key_place = jnp.concatenate(
        [positions(xh, zr, core), positions(xh, zr, 1 - core), positions(1 - xh, zr, core), positions(1 - xh, zr, 1 - core)]
    )
    bias = jnp.where(key_place < length, 0.0, MASKED).astype(F32)[None, :]
    live = (positions(xh, zr, core) < length).astype(F32)[None, :]
    grad_y = {0: grad, 1: moved(grad, y=1), 3: moved(grad, y=3)}
    k_own, q_own, v_own, bias, live, grad_y = lax.optimization_barrier((k_own, q_own, v_own, bias, live, grad_y))

    own = jnp.concatenate([k_own, v_own])
    other = moved(own, xh=1)
    q_other = moved(q_own, zr=1)
    other, q_other = lax.optimization_barrier((other, q_other))
    pieces = jnp.concatenate([own, other])
    pieces = (pieces, moved(pieces, core=1))

    theirs = attend(q_other, pieces, bias, BF)
    theirs = moved(theirs, zr=1)
    mine, mine_stat = attend(q_own, pieces, bias, F32)
    grad_y[2] = moved(after(grad_y[0], mine_stat), y=2)
    context = combine(mine, mine_stat, theirs, live)

    back = context.reshape(4, count, HEAD_DIM)
    mine_back = jnp.zeros((count, 4 * HEAD_DIM), BF)
    for d in (0, 1, 3, 2):
        part = moved(back[d], zq=-d) if d else back[d]
        mine_back = lax.dynamic_update_slice_in_dim(mine_back, part, ((zq + d) % 4) * HEAD_DIM, 1)

    grad_y[2] = after(grad_y[2], context)
    grad_rows = jnp.zeros((4, 4, rows, width // 4), BF)
    for d in range(4):
        grad_rows = lax.dynamic_update_index_in_dim(grad_rows, grad_y[d], (y - d) % 4, 1)
    grad_rows = grad_rows.reshape(16 * rows, width // 4)

    gathered = jnp.concatenate([beside(mine_back, *side) for side in sides])
    projected = jnp.dot(mine_back, out_weight, preferred_element_type=F32).astype(BF).reshape(4, rows, width)
    gathered, projected = lax.optimization_barrier((gathered, projected))
    total = lax.dot_general(grad_rows, gathered, (((0,), (0,)), ((), ())), preferred_element_type=F32)
    total = total.reshape(4, 2, 2, 32, 4 * HEAD_DIM)
    for axis, name, place in ((2, "core", core), (1, "zr", zr)):
        keep = lax.dynamic_index_in_dim(total, place, axis, keepdims=False)
        give = lax.dynamic_index_in_dim(total, 1 - place, axis, keepdims=False)
        total = keep + moved(give.astype(BF), **{name: 1}).astype(F32)
    weight_grad = lax.dynamic_index_in_dim(total, zq, 0, keepdims=False)
    for d in (1, 3, 2):
        part = lax.dynamic_index_in_dim(total, (zq + d) % 4, 0, keepdims=False)
        weight_grad += moved(part.astype(BF), zq=d).astype(F32)


    def for_y(steps):
        return lax.dynamic_index_in_dim(projected, (y + steps) % 4, 0, keepdims=False)

    block = for_y(0).astype(F32)
    for d in (1, 3, 2):
        block += moved(for_y(d), y=d).astype(F32)
    return block.astype(BF)[None], weight_grad.T


def solution(mesh):
    fine = Mesh(mesh.devices.reshape([s for _, s in SPLIT]), AXES)
    ctx = ("xh", "zq", "zr", "core")
    in_specs = (
        P("xl", ctx, "y"),
        P("xl", ctx, "y"),
        P("xl", ctx, "y"),
        P("xl"),
        P("y", None),
        P("xl", ctx + ("y",), None),
    )
    out_specs = (P("xl", ctx + ("y",), None), P("y", ctx + ("xl",)))
    return jax.shard_map(local, mesh=fine, in_specs=in_specs, out_specs=out_specs, check_vma=False)
```

time: 160 us -> 114 us (0.71)
  waiting for transfers between devices: 71 us -> 36.2 us
  starting transfers between devices: 69.7 us -> 55.4 us
  local copies, waits for them, and re-layouts: 7.43 us -> 3.82 us
  other arithmetic: 1.7 us -> 4.27 us
  matrix products: 2.14 us -> 4.44 us
    ppermute x35 -> x27, waiting for transfers between devices: 71 us -> 36.2 us  [moved(): return lax.ppermute(value, names, pairs)]
    ppermute x35 -> x27, starting transfers between devices: 69.7 us -> 55.4 us  [moved(): return lax.ppermute(value, names, pairs)]
    unnamed x11 -> x4, local copies, waits for them, and re-layouts: 2.66 us -> 0.04 us
    dot_general x5 -> x2, matrix products: 2.14 us -> 4.44 us  [the longest x1 3.7 us: local(): jnp.dot(mine_back, out_weight, preferred_element_type=F32).astype(BF)]
    dynamic_slice x2 -> x1, local copies, waits for them, and re-layouts: 1.77 us -> 0.02 us  [for_x(): return lax.dynamic_index_in_dim(part, (xl + dl) % 2, 0, keepdims=False)]
    pallas_call x2 -> x4, Pallas kernels: 5.18 us -> 6.72 us  [the longest x2 6.08 us: attend(): pl.pallas_call(attend_body, grid=(steps,), in_specs=[pl.BlockSpec((tile,...]
  transfers between devices with their start and end apart: 35 -> 27, of which waited for: 20 -> 16; matrix products, arithmetic and copies ran while one was open for 5% -> 7% of each run, Pallas kernels for 0% -> 3%
where the time goes in v2:
time: 114 us; the launch traced here: 113 us
  starting transfers between devices  55.4 us (49%)
  waiting for transfers between devices  36.2 us (32%)
  Pallas kernels  6.72 us (6%)
  matrix products  4.44 us (4%)
  other arithmetic  4.27 us (4%)
  local copies, waits for them, and re-layouts  3.82 us (3%)
  between operations  1.8 us (2%)
    ppermute x27, starting transfers between devices, moved(): return lax.ppermute(value, names, pairs)  55.4 us
    ppermute x27, waiting for transfers between devices, moved(): return lax.ppermute(value, names, pairs)  36.2 us
    pallas_call x2, Pallas kernels, attend(): pl.pallas_call(attend_body, grid=(steps,), in_specs=[pl.BlockSpec((tile,...  6.08 us
    dot_general x1, matrix products, local(): jnp.dot(mine_back, out_weight, preferred_element_type=F32).astype(BF)  3.7 us
  transfers between devices with their start and end apart: 27, of which 16 were waited for; matrix products, arithmetic and copies ran while one was open for 7% of the time, Pallas kernels for 3%

profile of v2, /device:TPU:8, one launch (start us, length us, event | category | flops | bytes accessed | tf_op | source)
XLA Modules:
  0.0 112.7 jit_solution(17806743474162739726)
XLA Ops:
  2.8 6.4 %collective-permute-start.2 = (bf16[384,256]{1,0:T(8,128)(2,1)S(1)}, bf16[384,256]{1,0:T(8,128)(2,1)S(1)}, u32[]{:S(2)}, u32[]{:S(2)}) collective-permute-start(bf16[384,256]{1,0:T(8,128)(2,1)S(1)} %pad_maximum_fusion.7), channel_id=1, source_target_pairs={{0,96},{32,0},{64,32},{96,64},{1,97},{33,1},{65,33},{97,65},{2,98}... | collective-permute-start | bytes 589832 | tf_op jit(solution)/shard_map/ppermute | solution.py:35
  10.6 3.1 %collective-permute-start.5 = (bf16[32,512]{1,0:T(8,128)(2,1)S(1)}, bf16[32,512]{1,0:T(8,128)(2,1)S(1)}, u32[]{:S(2)}, u32[]{:S(2)}) collective-permute-start(bf16[32,512]{1,0:T(8,128)(2,1)S(1)} %get-tuple-element.66), channel_id=1, source_target_pairs={{0,128},{1,129},{128,0},{129,1},{2,130},{3,131},{130,2},{131,3},{4... | collective-permute-start | bytes 98312 | tf_op jit(solution)/shard_map/ppermute | solution.py:35
  16.1 2.9 %collective-permute-start = (bf16[384,256]{1,0:T(8,128)(2,1)S(1)}, bf16[384,256]{1,0:T(8,128)(2,1)S(1)}, u32[]{:S(2)}, u32[]{:S(2)}) collective-permute-start(bf16[384,256]{1,0:T(8,128)(2,1)S(1)} %pad_maximum_fusion.5), channel_id=1, source_target_pairs={{0,32},{32,64},{64,96},{96,0},{1,33},{33,65},{65,97},{97,1},{2,34}... | collective-permute-start | bytes 589832 | tf_op jit(solution)/shard_map/ppermute | solution.py:35
  21.1 4.9 %collective-permute-done.2 = bf16[384,256]{1,0:T(8,128)(2,1)S(1)} collective-permute-done((bf16[384,256]{1,0:T(8,128)(2,1)S(1)}, bf16[384,256]{1,0:T(8,128)(2,1)S(1)}, u32[]{:S(2)}, u32[]{:S(2)}) %collective-permute-start.2) | collective-permute-done | bytes 196640 | tf_op jit(solution)/shard_map/ppermute | solution.py:35
  27.6 3.4 %collective-permute-start.8 = (bf16[1024,256]{1,0:T(8,128)(2,1)S(1)}, bf16[1024,256]{1,0:T(8,128)(2,1)S(1)}, u32[]{:S(2)}, u32[]{:S(2)}) collective-permute-start(bf16[1024,256]{1,0:T(8,128)(2,1)S(1)} %pad_maximum_fusion.1), channel_id=1, source_target_pairs={{0,128},{128,0},{1,129},{129,1},{2,130},{130,2},{3,131},{131,3},{4... | collective-permute-start | bytes 1572872 | tf_op jit(solution)/shard_map/ppermute | solution.py:35
  31.0 5.2 %collective-permute-start.9 = (bf16[512,256]{1,0:T(8,128)(2,1)S(1)}, bf16[512,256]{1,0:T(8,128)(2,1)S(1)}, u32[]{:S(2)}, u32[]{:S(2)}) collective-permute-start(bf16[512,256]{1,0:T(8,128)(2,1)S(1)} %pad_maximum_fusion.3.q_ref), channel_id=1, source_target_pairs={{0,16},{16,0},{1,17},{17,1},{2,18},{18,2},{3,19},{19,3},{4,20},{20... | collective-permute-start | bytes 786440 | tf_op jit(solution)/shard_map/ppermute | solution.py:35
  36.2 6.0 %collective-permute-done.9.q_ref = bf16[512,256]{1,0:T(8,128)(2,1)S(1)} collective-permute-done((bf16[512,256]{1,0:T(8,128)(2,1)S(1)}, bf16[512,256]{1,0:T(8,128)(2,1)S(1)}, u32[]{:S(2)}, u32[]{:S(2)}) %collective-permute-start.9) | collective-permute-done | bytes 262176 | tf_op jit(solution)/shard_map/ppermute | solution.py:35
  42.9 2.5 %collective-permute-done.10.k1.k3.v1.v3 = bf16[2048,256]{1,0:T(8,128)(2,1)S(1)} collective-permute-done((bf16[2048,256]{1,0:T(8,128)(2,1)S(1)}, bf16[2048,256]{1,0:T(8,128)(2,1)S(1)}, u32[]{:S(2)}, u32[]{:S(2)}) %collective-permute-start.10) | collective-permute-done | bytes 1048608 | tf_op jit(solution)/shard_map/ppermute | solution.py:35
  45.4 3.0 %shard_map.79 = bf16[544,256]{1,0:T(8,128)(2,1)S(1)} custom-call(bf16[512,256]{1,0:T(8,128)(2,1)S(1)} %collective-permute-done.9.q_ref, bf16[2048,256]{1,0:T(8,128)(2,1)S(1)} %constant_dynamic-update-slice_fusion.3.k0.k2.v0.v2, bf16[2048,256]{1,0:T(8,128)(2,1)S(1)} %collective-permute-done.10.k1.k3.v1.v3, ...), custom_call_target="tpu_custom_call" | custom-call | flops 1073741824 | bytes 2097152 | tf_op jit(solution)/shard_map/pallas_call | solution.py:89
  48.4 5.6 %collective-permute-start.11 = (bf16[544,256]{1,0:T(8,128)(2,1)S(1)}, bf16[544,256]{1,0:T(8,128)(2,1)S(1)}, u32[]{:S(2)}, u32[]{:S(2)}) collective-permute-start(bf16[544,256]{1,0:T(8,128)(2,1)S(1)} %shard_map.79), channel_id=1, source_target_pairs={{0,16},{16,0},{1,17},{17,1},{2,18},{18,2},{3,19},{19,3},{4,20},{20... | collective-permute-start | bytes 835592 | tf_op jit(solution)/shard_map/ppermute | solution.py:35
  54.0 3.0 %shard_map.78 = (f32[512,256]{1,0:T(8,128)S(1)}, f32[8,512]{1,0:T(8,128)S(1)}) custom-call(bf16[512,256]{1,0:T(8,128)(2,1)S(1)} %pad_maximum_fusion.3.q_ref, bf16[2048,256]{1,0:T(8,128)(2,1)S(1)} %constant_dynamic-update-slice_fusion.3.k0.k2.v0.v2, bf16[2048,256]{1,0:T(8,128)(2,1)S(1)} %collective-permute-done.10.k1.k3.v1.v3, ...), custom_call_target="tpu_custom_call" | custom-call | flops 1073741824 | bytes 2097152 | tf_op jit(solution)/shard_map/pallas_call | solution.py:89
  57.1 2.4 %collective-permute-start.21 = (bf16[4,32,512]{2,1,0:T(8,128)(2,1)S(1)}, bf16[4,32,512]{2,1,0:T(8,128)(2,1)S(1)}, u32[]{:S(2)}, u32[]{:S(2)}) collective-permute-start(bf16[4,32,512]{2,1,0:T(8,128)(2,1)S(1)} %pad_maximum_fusion.8), channel_id=1, source_target_pairs={{0,4},{2,6},{4,0},{6,2},{1,5},{3,7},{5,1},{7,3},{8,12},{10,14},{12... | collective-permute-start | bytes 393224 | tf_op jit(solution)/shard_map/ppermute | solution.py:35
  61.4 2.1 %collective-permute-start.12 = (bf16[128,256]{1,0:T(8,128)(2,1)S(1)}, bf16[128,256]{1,0:T(8,128)(2,1)S(1)}, u32[]{:S(2)}, u32[]{:S(2)}) collective-permute-start(bf16[128,256]{1,0:T(8,128)(2,1)S(1)} %get-tuple-element.42), channel_id=1, source_target_pairs={{0,96},{32,0},{64,32},{96,64},{1,97},{33,1},{65,33},{97,65},{2,98}... | collective-permute-start | bytes 196616 | tf_op jit(solution)/shard_map/ppermute | solution.py:35
  64.6 2.3 %collective-permute-start.14 = (bf16[128,256]{1,0:T(8,128)(2,1)S(1)}, bf16[128,256]{1,0:T(8,128)(2,1)S(1)}, u32[]{:S(2)}, u32[]{:S(2)}) collective-permute-start(bf16[128,256]{1,0:T(8,128)(2,1)S(1)} %get-tuple-element.40), channel_id=1, source_target_pairs={{0,64},{32,96},{64,0},{96,32},{1,65},{33,97},{65,1},{97,33},{2,66}... | collective-permute-start | bytes 196616 | tf_op jit(solution)/shard_map/ppermute | solution.py:35
  67.2 4.4 %collective-permute-done.13 = bf16[128,256]{1,0:T(8,128)(2,1)S(1)} collective-permute-done((bf16[128,256]{1,0:T(8,128)(2,1)S(1)}, bf16[128,256]{1,0:T(8,128)(2,1)S(1)}, u32[]{:S(2)}, u32[]{:S(2)}) %collective-permute-start.13) | collective-permute-done | bytes 65568 | tf_op jit(solution)/shard_map/ppermute | solution.py:35
  72.9 3.3 %collective-permute-start.17 = (bf16[128,1024]{1,0:T(8,128)(2,1)S(1)}, bf16[128,1024]{1,0:T(8,128)(2,1)S(1)}, u32[]{:S(2)}, u32[]{:S(2)}) collective-permute-start(bf16[128,1024]{1,0:T(8,128)(2,1)S(1)} %constant_dynamic-update-slice_fusion), channel_id=1, source_target_pairs={{0,128},{1,129},{128,0},{129,1},{2,130},{3,131},{130,2},{131,3},{4... | collective-permute-start | bytes 786440 | tf_op jit(solution)/shard_map/ppermute | solution.py:35
  77.3 3.7 %convolution_convert_fusion = bf16[128,2048]{1,0:T(8,128)(2,1)} fusion(bf16[128,1024]{1,0:T(8,128)(2,1)S(1)} %constant_dynamic-update-slice_fusion, bf16[1024,2048]{1,0:T(8,128)(2,1)} %param.10), kind=kOutput, calls=%fused_computation | convolution fusion | flops 537133056 | bytes 4980736 | tf_op jit(solution)/shard_map/dot_general | solution.py:232
  81.0 1.9 %collective-permute-done.17 = bf16[128,1024]{1,0:T(8,128)(2,1)S(1)} collective-permute-done((bf16[128,1024]{1,0:T(8,128)(2,1)S(1)}, bf16[128,1024]{1,0:T(8,128)(2,1)S(1)}, u32[]{:S(2)}, u32[]{:S(2)}) %collective-permute-start.17) | collective-permute-done | bytes 262176 | tf_op jit(solution)/shard_map/ppermute | solution.py:35
  83.0 3.8 %collective-permute-done.16 = bf16[128,1024]{1,0:T(8,128)(2,1)S(1)} collective-permute-done((bf16[128,1024]{1,0:T(8,128)(2,1)S(1)}, bf16[128,1024]{1,0:T(8,128)(2,1)S(1)}, u32[]{:S(2)}, u32[]{:S(2)}) %collective-permute-start.16) | collective-permute-done | bytes 262176 | tf_op jit(solution)/shard_map/ppermute | solution.py:35
  87.8 2.0 %collective-permute-done.22 = bf16[4,2,32,1024]{3,2,1,0:T(8,128)(2,1)} collective-permute-done((bf16[4,2,32,1024]{3,2,1,0:T(8,128)(2,1)S(1)}, bf16[4,2,32,1024]{3,2,1,0:T(8,128)(2,1)}, u32[]{:S(2)}, u32[]{:S(2)}) %collective-permute-start.22) | collective-permute-done | bytes 524320 | tf_op jit(solution)/shard_map/ppermute | solution.py:35
  93.4 2.4 %collective-permute-start.20 = (bf16[32,2048]{1,0:T(8,128)(2,1)S(1)}, bf16[32,2048]{1,0:T(8,128)(2,1)S(1)}, u32[]{:S(2)}, u32[]{:S(2)}) collective-permute-start(bf16[32,2048]{1,0:T(8,128)(2,1)S(1)} %get-tuple-element.38), channel_id=1, source_target_pairs={{0,4},{2,6},{4,0},{6,2},{1,5},{3,7},{5,1},{7,3},{8,12},{10,14},{12... | collective-permute-start | bytes 393224 | tf_op jit(solution)/shard_map/ppermute | solution.py:35
  99.6 3.0 %collective-permute-start.26 = (bf16[32,1024]{1,0:T(8,128)(2,1)S(1)}, bf16[32,1024]{1,0:T(8,128)(2,1)S(1)}, u32[]{:S(2)}, u32[]{:S(2)}) collective-permute-start(bf16[32,1024]{1,0:T(8,128)(2,1)S(1)} %get-tuple-element.35), channel_id=1, source_target_pairs={{0,64},{32,96},{64,0},{96,32},{1,65},{33,97},{65,1},{97,33},{2,66}... | collective-permute-start | bytes 196616 | tf_op jit(solution)/shard_map/ppermute | solution.py:35
  102.6 3.0 %collective-permute-start.25 = (bf16[32,1024]{1,0:T(8,128)(2,1)S(1)}, bf16[32,1024]{1,0:T(8,128)(2,1)S(1)}, u32[]{:S(2)}, u32[]{:S(2)}) collective-permute-start(bf16[32,1024]{1,0:T(8,128)(2,1)S(1)} %get-tuple-element.36), channel_id=1, source_target_pairs={{0,96},{32,0},{64,32},{96,64},{1,97},{33,1},{65,33},{97,65},{2,98}... | collective-permute-start | bytes 196616 | tf_op jit(solution)/shard_map/ppermute | solution.py:35
  108.0 3.6 %collective-permute-done.25 = bf16[32,1024]{1,0:T(8,128)(2,1)S(1)} collective-permute-done((bf16[32,1024]{1,0:T(8,128)(2,1)S(1)}, bf16[32,1024]{1,0:T(8,128)(2,1)S(1)}, u32[]{:S(2)}, u32[]{:S(2)}) %collective-permute-start.25) | collective-permute-done | bytes 65568 | tf_op jit(solution)/shard_map/ppermute | solution.py:35
  (85 shorter events, 27.0 us)
Async XLA Ops:
  2.8 23.2 %collective-permute-start.2 = (bf16[384,256]{1,0:T(8,128)(2,1)S(1)}, bf16[384,256]{1,0:T(8,128)(2,1)S(1)}, u32[]{:S(2)}, u32[]{:S(2)}) collective-permute-start(bf16[384,256]{1,0:T(8,128)(2,1)S(1)} %pad_maximum_fusion.7), channel_id=1, source_target_pairs={{0,96},{32,0},{64,32},{96,64},{1,97},{33,1},{65,33},{97,65},{2,98}... | collective-permute-start | bytes 589832 | tf_op jit(solution)/shard_map/ppermute | solution.py:35
  9.2 16.8 %collective-permute-start.1 = (bf16[384,256]{1,0:T(8,128)(2,1)S(1)}, bf16[384,256]{1,0:T(8,128)(2,1)S(1)}, u32[]{:S(2)}, u32[]{:S(2)}) collective-permute-start(bf16[384,256]{1,0:T(8,128)(2,1)S(1)} %pad_maximum_fusion.6), channel_id=1, source_target_pairs={{0,64},{32,96},{64,0},{96,32},{1,65},{33,97},{65,1},{97,33},{2,66}... | collective-permute-start | bytes 589832 | tf_op jit(solution)/shard_map/ppermute | solution.py:35
  10.6 5.5 %collective-permute-start.5 = (bf16[32,512]{1,0:T(8,128)(2,1)S(1)}, bf16[32,512]{1,0:T(8,128)(2,1)S(1)}, u32[]{:S(2)}, u32[]{:S(2)}) collective-permute-start(bf16[32,512]{1,0:T(8,128)(2,1)S(1)} %get-tuple-element.66), channel_id=1, source_target_pairs={{0,128},{1,129},{128,0},{129,1},{2,130},{3,131},{130,2},{131,3},{4... | collective-permute-start | bytes 98312 | tf_op jit(solution)/shard_map/ppermute | solution.py:35
  13.7 5.3 %collective-permute-start.4 = (bf16[32,512]{1,0:T(8,128)(2,1)S(1)}, bf16[32,512]{1,0:T(8,128)(2,1)S(1)}, u32[]{:S(2)}, u32[]{:S(2)}) collective-permute-start(bf16[32,512]{1,0:T(8,128)(2,1)S(1)} %get-tuple-element.67), channel_id=1, source_target_pairs={{0,129},{1,128},{128,1},{129,0},{2,131},{3,130},{130,3},{131,2},{4... | collective-permute-start | bytes 98312 | tf_op jit(solution)/shard_map/ppermute | solution.py:35
  16.1 11.3 %collective-permute-start = (bf16[384,256]{1,0:T(8,128)(2,1)S(1)}, bf16[384,256]{1,0:T(8,128)(2,1)S(1)}, u32[]{:S(2)}, u32[]{:S(2)}) collective-permute-start(bf16[384,256]{1,0:T(8,128)(2,1)S(1)} %pad_maximum_fusion.5), channel_id=1, source_target_pairs={{0,32},{32,64},{64,96},{96,0},{1,33},{33,65},{65,97},{97,1},{2,34}... | collective-permute-start | bytes 589832 | tf_op jit(solution)/shard_map/ppermute | solution.py:35
  19.0 8.5 %collective-permute-start.6 = (bf16[4,32,512]{2,1,0:T(8,128)(2,1)S(1)}, bf16[4,32,512]{2,1,0:T(8,128)(2,1)S(1)}, u32[]{:S(2)}, u32[]{:S(2)}) collective-permute-start(bf16[4,32,512]{2,1,0:T(8,128)(2,1)S(1)} %pad_maximum_fusion.8), channel_id=1, source_target_pairs={{0,2},{2,4},{4,6},{6,0},{1,3},{3,5},{5,7},{7,1},{8,10},{10,12},{12... | collective-permute-start | bytes 393224 | tf_op jit(solution)/shard_map/ppermute | solution.py:35
  20.7 6.9 %collective-permute-start.7 = (bf16[4,32,512]{2,1,0:T(8,128)(2,1)S(1)}, bf16[4,32,512]{2,1,0:T(8,128)(2,1)S(1)}, u32[]{:S(2)}, u32[]{:S(2)}) collective-permute-start(bf16[4,32,512]{2,1,0:T(8,128)(2,1)S(1)} %pad_maximum_fusion.8), channel_id=1, source_target_pairs={{0,6},{2,0},{4,2},{6,4},{1,7},{3,1},{5,3},{7,5},{8,14},{10,8},{12,... | collective-permute-start | bytes 393224 | tf_op jit(solution)/shard_map/ppermute | solution.py:35
  27.6 15.0 %collective-permute-start.8 = (bf16[1024,256]{1,0:T(8,128)(2,1)S(1)}, bf16[1024,256]{1,0:T(8,128)(2,1)S(1)}, u32[]{:S(2)}, u32[]{:S(2)}) collective-permute-start(bf16[1024,256]{1,0:T(8,128)(2,1)S(1)} %pad_maximum_fusion.1), channel_id=1, source_target_pairs={{0,128},{128,0},{1,129},{129,1},{2,130},{130,2},{3,131},{131,3},{4... | collective-permute-start | bytes 1572872 | tf_op jit(solution)/shard_map/ppermute | solution.py:35
  31.0 11.2 %collective-permute-start.9 = (bf16[512,256]{1,0:T(8,128)(2,1)S(1)}, bf16[512,256]{1,0:T(8,128)(2,1)S(1)}, u32[]{:S(2)}, u32[]{:S(2)}) collective-permute-start(bf16[512,256]{1,0:T(8,128)(2,1)S(1)} %pad_maximum_fusion.3.q_ref), channel_id=1, source_target_pairs={{0,16},{16,0},{1,17},{17,1},{2,18},{18,2},{3,19},{19,3},{4,20},{20... | collective-permute-start | bytes 786440 | tf_op jit(solution)/shard_map/ppermute | solution.py:35
  48.4 12.5 %collective-permute-start.11 = (bf16[544,256]{1,0:T(8,128)(2,1)S(1)}, bf16[544,256]{1,0:T(8,128)(2,1)S(1)}, u32[]{:S(2)}, u32[]{:S(2)}) collective-permute-start(bf16[544,256]{1,0:T(8,128)(2,1)S(1)} %shard_map.79), channel_id=1, source_target_pairs={{0,16},{16,0},{1,17},{17,1},{2,18},{18,2},{3,19},{19,3},{4,20},{20... | collective-permute-start | bytes 835592 | tf_op jit(solution)/shard_map/ppermute | solution.py:35
  57.1 9.8 %collective-permute-start.21 = (bf16[4,32,512]{2,1,0:T(8,128)(2,1)S(1)}, bf16[4,32,512]{2,1,0:T(8,128)(2,1)S(1)}, u32[]{:S(2)}, u32[]{:S(2)}) collective-permute-start(bf16[4,32,512]{2,1,0:T(8,128)(2,1)S(1)} %pad_maximum_fusion.8), channel_id=1, source_target_pairs={{0,4},{2,6},{4,0},{6,2},{1,5},{3,7},{5,1},{7,3},{8,12},{10,14},{12... | collective-permute-start | bytes 393224 | tf_op jit(solution)/shard_map/ppermute | solution.py:35
  61.4 5.7 %collective-permute-start.12 = (bf16[128,256]{1,0:T(8,128)(2,1)S(1)}, bf16[128,256]{1,0:T(8,128)(2,1)S(1)}, u32[]{:S(2)}, u32[]{:S(2)}) collective-permute-start(bf16[128,256]{1,0:T(8,128)(2,1)S(1)} %get-tuple-element.42), channel_id=1, source_target_pairs={{0,96},{32,0},{64,32},{96,64},{1,97},{33,1},{65,33},{97,65},{2,98}... | collective-permute-start | bytes 196616 | tf_op jit(solution)/shard_map/ppermute | solution.py:35
  63.5 8.1 %collective-permute-start.13 = (bf16[128,256]{1,0:T(8,128)(2,1)S(1)}, bf16[128,256]{1,0:T(8,128)(2,1)S(1)}, u32[]{:S(2)}, u32[]{:S(2)}) collective-permute-start(bf16[128,256]{1,0:T(8,128)(2,1)S(1)} %get-tuple-element.41), channel_id=1, source_target_pairs={{0,32},{32,64},{64,96},{96,0},{1,33},{33,65},{65,97},{97,1},{2,34}... | collective-permute-start | bytes 196616 | tf_op jit(solution)/shard_map/ppermute | solution.py:35
  64.6 8.3 %collective-permute-start.14 = (bf16[128,256]{1,0:T(8,128)(2,1)S(1)}, bf16[128,256]{1,0:T(8,128)(2,1)S(1)}, u32[]{:S(2)}, u32[]{:S(2)}) collective-permute-start(bf16[128,256]{1,0:T(8,128)(2,1)S(1)} %get-tuple-element.40), channel_id=1, source_target_pairs={{0,64},{32,96},{64,0},{96,32},{1,65},{33,97},{65,1},{97,33},{2,66}... | collective-permute-start | bytes 196616 | tf_op jit(solution)/shard_map/ppermute | solution.py:35
  72.9 10.1 %collective-permute-start.17 = (bf16[128,1024]{1,0:T(8,128)(2,1)S(1)}, bf16[128,1024]{1,0:T(8,128)(2,1)S(1)}, u32[]{:S(2)}, u32[]{:S(2)}) collective-permute-start(bf16[128,1024]{1,0:T(8,128)(2,1)S(1)} %constant_dynamic-update-slice_fusion), channel_id=1, source_target_pairs={{0,128},{1,129},{128,0},{129,1},{2,130},{3,131},{130,2},{131,3},{4... | collective-permute-start | bytes 786440 | tf_op jit(solution)/shard_map/ppermute | solution.py:35
  76.2 10.6 %collective-permute-start.16 = (bf16[128,1024]{1,0:T(8,128)(2,1)S(1)}, bf16[128,1024]{1,0:T(8,128)(2,1)S(1)}, u32[]{:S(2)}, u32[]{:S(2)}) collective-permute-start(bf16[128,1024]{1,0:T(8,128)(2,1)S(1)} %constant_dynamic-update-slice_fusion), channel_id=1, source_target_pairs={{0,129},{1,128},{128,1},{129,0},{2,131},{3,130},{130,3},{131,2},{4... | collective-permute-start | bytes 786440 | tf_op jit(solution)/shard_map/ppermute | solution.py:35
  77.3 9.4 %collective-permute-start.15 = (bf16[128,1024]{1,0:T(8,128)(2,1)S(1)}, bf16[128,1024]{1,0:T(8,128)(2,1)S(1)}, u32[]{:S(2)}, u32[]{:S(2)}) collective-permute-start(bf16[128,1024]{1,0:T(8,128)(2,1)S(1)} %constant_dynamic-update-slice_fusion), channel_id=1, source_target_pairs={{0,1},{1,0},{128,129},{129,128},{2,3},{3,2},{130,131},{131,130},{4... | collective-permute-start | bytes 786440 | tf_op jit(solution)/shard_map/ppermute | solution.py:35
  91.1 8.4 %collective-permute-start.23 = (bf16[4,32,1024]{2,1,0:T(8,128)(2,1)S(1)}, bf16[4,32,1024]{2,1,0:T(8,128)(2,1)S(1)}, u32[]{:S(2)}, u32[]{:S(2)}) collective-permute-start(bf16[4,32,1024]{2,1,0:T(8,128)(2,1)S(1)} %fusion.3), channel_id=1, source_target_pairs={{0,16},{16,0},{1,17},{17,1},{2,18},{18,2},{3,19},{19,3},{4,20},{20... | collective-permute-start | bytes 786440 | tf_op jit(solution)/shard_map/ppermute | solution.py:35
  93.4 12.2 %collective-permute-start.20 = (bf16[32,2048]{1,0:T(8,128)(2,1)S(1)}, bf16[32,2048]{1,0:T(8,128)(2,1)S(1)}, u32[]{:S(2)}, u32[]{:S(2)}) collective-permute-start(bf16[32,2048]{1,0:T(8,128)(2,1)S(1)} %get-tuple-element.38), channel_id=1, source_target_pairs={{0,4},{2,6},{4,0},{6,2},{1,5},{3,7},{5,1},{7,3},{8,12},{10,14},{12... | collective-permute-start | bytes 393224 | tf_op jit(solution)/shard_map/ppermute | solution.py:35
  95.8 10.3 %collective-permute-start.19 = (bf16[32,2048]{1,0:T(8,128)(2,1)S(1)}, bf16[32,2048]{1,0:T(8,128)(2,1)S(1)}, u32[]{:S(2)}, u32[]{:S(2)}) collective-permute-start(bf16[32,2048]{1,0:T(8,128)(2,1)S(1)} %get-tuple-element.39), channel_id=1, source_target_pairs={{0,6},{2,0},{4,2},{6,4},{1,7},{3,1},{5,3},{7,5},{8,14},{10,8},{12,... | collective-permute-start | bytes 393224 | tf_op jit(solution)/shard_map/ppermute | solution.py:35
  97.1 9.0 %collective-permute-start.18 = (bf16[32,2048]{1,0:T(8,128)(2,1)S(1)}, bf16[32,2048]{1,0:T(8,128)(2,1)S(1)}, u32[]{:S(2)}, u32[]{:S(2)}) collective-permute-start(bf16[32,2048]{1,0:T(8,128)(2,1)S(1)} %get-tuple-element.37), channel_id=1, source_target_pairs={{0,2},{2,4},{4,6},{6,0},{1,3},{3,5},{5,7},{7,1},{8,10},{10,12},{12... | collective-permute-start | bytes 393224 | tf_op jit(solution)/shard_map/ppermute | solution.py:35
  99.6 8.4 %collective-permute-start.26 = (bf16[32,1024]{1,0:T(8,128)(2,1)S(1)}, bf16[32,1024]{1,0:T(8,128)(2,1)S(1)}, u32[]{:S(2)}, u32[]{:S(2)}) collective-permute-start(bf16[32,1024]{1,0:T(8,128)(2,1)S(1)} %get-tuple-element.35), channel_id=1, source_target_pairs={{0,64},{32,96},{64,0},{96,32},{1,65},{33,97},{65,1},{97,33},{2,66}... | collective-permute-start | bytes 196616 | tf_op jit(solution)/shard_map/ppermute | solution.py:35
  102.6 9.0 %collective-permute-start.25 = (bf16[32,1024]{1,0:T(8,128)(2,1)S(1)}, bf16[32,1024]{1,0:T(8,128)(2,1)S(1)}, u32[]{:S(2)}, u32[]{:S(2)}) collective-permute-start(bf16[32,1024]{1,0:T(8,128)(2,1)S(1)} %get-tuple-element.36), channel_id=1, source_target_pairs={{0,96},{32,0},{64,32},{96,64},{1,97},{33,1},{65,33},{97,65},{2,98}... | collective-permute-start | bytes 196616 | tf_op jit(solution)/shard_map/ppermute | solution.py:35
  105.6 6.4 %collective-permute-start.24 = (bf16[32,1024]{1,0:T(8,128)(2,1)S(1)}, bf16[32,1024]{1,0:T(8,128)(2,1)S(1)}, u32[]{:S(2)}, u32[]{:S(2)}) collective-permute-start(bf16[32,1024]{1,0:T(8,128)(2,1)S(1)} %get-tuple-element.34), channel_id=1, source_target_pairs={{0,32},{32,64},{64,96},{96,0},{1,33},{33,65},{65,97},{97,1},{2,34}... | collective-permute-start | bytes 196616 | tf_op jit(solution)/shard_map/ppermute | solution.py:35
  (4 other events, 18.7 us)

commit v3 on v2

--- a/solution.py
+++ b/solution.py
@@ -1,3 +1,4 @@
+import functools
 import math
 
 import jax
@@ -39,27 +40,42 @@
     return lax.optimization_barrier((value, *earlier))[0]
 
 
-def attend_body(q_ref, k0, k1, k2, k3, v0, v1, v2, v3, bias, out, *stat_out):
+def attend_body(q_ref, k0, k1, v0, v1, bias, *refs, first, packed):
     tile = q_ref.shape[0]
     q = q_ref[...]
+    if first:
+        out, stat_out = refs
+        acc = jnp.zeros((tile, HEAD_DIM), F32)
+        total = jnp.zeros((tile, 1), F32)
+        top = jnp.full((tile, 1), -jnp.inf, F32)
+    else:
+        acc_in, stat_in, out, *stat_out = refs
+
+        def down(row):
+            return jnp.broadcast_to(row, (128, tile)).T[:, :1]
+
+        top, total = down(stat_in[0:1]), down(stat_in[4:5])
     parts = []
-    for i, k in enumerate((k0, k1, k2, k3)):
+    new_top = top
+    for i, k in enumerate((k0, k1)):
         s = lax.dot_general(q, k[...], (((1,), (1,)), ((), ())), preferred_element_type=F32)
         width = k.shape[0]
         parts.append(s * (math.log2(math.e) / math.sqrt(HEAD_DIM)) + bias[:, i * width : (i + 1) * width])
-    top = parts[0].max(axis=1, keepdims=True)
-    for s in parts[1:]:
-        top = jnp.maximum(top, s.max(axis=1, keepdims=True))
-    total = jnp.zeros((tile, 1), F32)
-    acc = jnp.zeros((tile, HEAD_DIM), F32)
-    for s, v in zip(parts, (v0, v1, v2, v3)):
+        new_top = jnp.maximum(new_top, parts[-1].max(axis=1, keepdims=True))
+    if not first:
+        fade = jnp.exp2(top - new_top)
+        total = total * fade
+        acc = acc_in[...] * fade
+    top = new_top
+    for s, v in zip(parts, (v0, v1)):
         e = jnp.exp2(s - top)
         total += e.sum(axis=1, keepdims=True)
         acc += jnp.dot(e.astype(BF), v[...], preferred_element_type=F32)
-    if stat_out:
-        out[...] = acc / total
-        stat_out[0][:4, :] = jnp.broadcast_to(top, (tile, 128)).T[:4]
-        stat_out[0][4:, :] = jnp.broadcast_to(total, (tile, 128)).T[:4]
+    if not packed:
+        out[...] = acc if first else acc / total
+        stat_out = stat_out if first else stat_out[0]
+        stat_out[:4, :] = jnp.broadcast_to(top, (tile, 128)).T[:4]
+        stat_out[4:, :] = jnp.broadcast_to(total, (tile, 128)).T[:4]
         return
     step = pl.program_id(0)
     out[pl.ds(pl.multiple_of(step * tile, tile), tile), :] = (acc / total).astype(BF)
@@ -74,31 +90,34 @@
     out[pl.ds(below, 16), :] = jnp.concatenate(lines).astype(BF)
 
 
-def attend(q, pieces, bias, dtype):
+def attend(q, pieces, bias, before=None, packed=False):
     rows = q.shape[0]
     tile = 256
     steps = rows // tile
-    part = pieces[0].shape[0] // 4
-    keys = 4 * part
-    if dtype == F32:
-        out_specs = [pl.BlockSpec((tile, HEAD_DIM), lambda i: (i, 0)), pl.BlockSpec((8, tile), lambda i: (0, i))]
-        out_shape = [jax.ShapeDtypeStruct((rows, HEAD_DIM), F32), jax.ShapeDtypeStruct((8, rows), F32)]
-    else:
+    part = pieces[0].shape[0] // 2
+    first = before is None
+    rows_spec = pl.BlockSpec((tile, HEAD_DIM), lambda i: (i, 0))
+    stat_spec = pl.BlockSpec((8, tile), lambda i: (0, i))
+    if packed:
         out_shape = jax.ShapeDtypeStruct((rows + 16 * steps, HEAD_DIM), BF)
         out_specs = pl.BlockSpec(out_shape.shape, lambda i: (0, 0))
+    else:
+        out_specs = [rows_spec, stat_spec]
+        out_shape = [jax.ShapeDtypeStruct((rows, HEAD_DIM), F32), jax.ShapeDtypeStruct((8, rows), F32)]
     return pl.pallas_call(
-        attend_body,
+        functools.partial(attend_body, first=first, packed=packed),
         grid=(steps,),
-        in_specs=[pl.BlockSpec((tile, HEAD_DIM), lambda i: (i, 0))]
-        + [pl.BlockSpec((part, HEAD_DIM), lambda i, at=at: (at, 0)) for at in (0, 0, 2, 2, 1, 1, 3, 3)]
-        + [pl.BlockSpec((1, keys), lambda i: (0, 0))],
+        in_specs=[rows_spec]
+        + [pl.BlockSpec((part, HEAD_DIM), lambda i, at=at: (at, 0)) for at in (0, 0, 1, 1)]
+        + [pl.BlockSpec((1, 2 * part), lambda i: (0, 0 if first else 1))]
+        + ([] if first else [rows_spec, stat_spec]),
         out_specs=out_specs,
         out_shape=out_shape,
         compiler_params=pltpu.CompilerParams(vmem_limit_bytes=VMEM),
         cost_estimate=pl.CostEstimate(
-            flops=4 * rows * keys * HEAD_DIM, bytes_accessed=4 * keys * HEAD_DIM, transcendentals=rows * keys
+            flops=8 * rows * part * HEAD_DIM, bytes_accessed=8 * part * HEAD_DIM, transcendentals=2 * rows * part
         ),
-    )(q, *pieces * 4, bias)
+    )(q, *pieces * 2, bias, *(() if first else before))
 
 
 def combine_body(mine, mine_stat, theirs, theirs_stat, live, out):
@@ -206,13 +225,13 @@
     own = jnp.concatenate([k_own, v_own])
     other = moved(own, xh=1)
     q_other = moved(q_own, zr=1)
-    other, q_other = lax.optimization_barrier((other, q_other))
-    pieces = jnp.concatenate([own, other])
-    pieces = (pieces, moved(pieces, core=1))
-
-    theirs = attend(q_other, pieces, bias, BF)
+    here = (own, moved(own, core=1))
+    begun = attend(q_other, here, bias), attend(q_own, here, bias)
+    other, begun = lax.optimization_barrier((other, begun))
+    there = (other, moved(other, core=1))
+    theirs = attend(q_other, there, bias, begun[0], packed=True)
     theirs = moved(theirs, zr=1)
-    mine, mine_stat = attend(q_own, pieces, bias, F32)
+    mine, mine_stat = attend(q_own, there, bias, begun[1])
     grad_y[2] = moved(after(grad_y[0], mine_stat), y=2)
     context = combine(mine, mine_stat, theirs, live)
 

time: 114 us -> 112 us (0.982)
  waiting for transfers between devices: 36.2 us -> 33 us
  Pallas kernels: 6.72 us -> 8.45 us
  starting transfers between devices: 55.4 us -> 54 us
    ppermute x27 -> x28, waiting for transfers between devices: 36.2 us -> 33 us  [moved(): return lax.ppermute(value, names, pairs)]
    pallas_call x2 -> x4, Pallas kernels: 6.08 us -> 7.81 us  [attend(): pl.pallas_call(functools.partial(attend_body, first=first, packed=packed)...]
    ppermute x27 -> x28, starting transfers between devices: 55.4 us -> 54 us  [moved(): return lax.ppermute(value, names, pairs)]
  transfers between devices with their start and end apart: 27 -> 28, of which waited for: 16 -> 16; matrix products, arithmetic and copies ran while one was open for 7% -> 8% of each run, Pallas kernels for 3% -> 6%
where the time goes in v3:
time: 112 us; the launch traced here: 111 us
  starting transfers between devices  54 us (48%)
  waiting for transfers between devices  33 us (29%)
  Pallas kernels  8.45 us (8%)
  local copies, waits for them, and re-layouts  4.7 us (4%)
  matrix products  4.43 us (4%)
  other arithmetic  4.23 us (4%)
  between operations  1.83 us (2%)
    ppermute x28, starting transfers between devices, moved(): return lax.ppermute(value, names, pairs)  54 us
    ppermute x28, waiting for transfers between devices, moved(): return lax.ppermute(value, names, pairs)  33 us
    pallas_call x4, Pallas kernels, attend(): pl.pallas_call(functools.partial(attend_body, first=first, packed=packed)...  7.81 us
    dot_general x1, matrix products, local(): jnp.dot(mine_back, out_weight, preferred_element_type=F32).astype(BF)  3.69 us
  transfers between devices with their start and end apart: 28, of which 16 were waited for; matrix products, arithmetic and copies ran while one was open for 8% of the time, Pallas kernels for 6%

profile of v3, /device:TPU:8, one launch (start us, length us, event | category | flops | bytes accessed | tf_op | source)
XLA Modules:
  0.0 110.7 jit_solution(79234214412727480)
XLA Ops:
  2.8 6.4 %collective-permute-start.2 = (bf16[384,256]{1,0:T(8,128)(2,1)S(1)}, bf16[384,256]{1,0:T(8,128)(2,1)S(1)}, u32[]{:S(2)}, u32[]{:S(2)}) collective-permute-start(bf16[384,256]{1,0:T(8,128)(2,1)S(1)} %pad_maximum_fusion.6), channel_id=1, source_target_pairs={{0,96},{32,0},{64,32},{96,64},{1,97},{33,1},{65,33},{97,65},{2,98}... | collective-permute-start | bytes 589832 | tf_op jit(solution)/shard_map/ppermute | solution.py:36
  10.6 3.1 %collective-permute-start.5 = (bf16[32,512]{1,0:T(8,128)(2,1)S(1)}, bf16[32,512]{1,0:T(8,128)(2,1)S(1)}, u32[]{:S(2)}, u32[]{:S(2)}) collective-permute-start(bf16[32,512]{1,0:T(8,128)(2,1)S(1)} %get-tuple-element.80), channel_id=1, source_target_pairs={{0,128},{1,129},{128,0},{129,1},{2,130},{3,131},{130,2},{131,3},{4... | collective-permute-start | bytes 98312 | tf_op jit(solution)/shard_map/ppermute | solution.py:36
  16.1 2.9 %collective-permute-start = (bf16[384,256]{1,0:T(8,128)(2,1)S(1)}, bf16[384,256]{1,0:T(8,128)(2,1)S(1)}, u32[]{:S(2)}, u32[]{:S(2)}) collective-permute-start(bf16[384,256]{1,0:T(8,128)(2,1)S(1)} %pad_maximum_fusion.4), channel_id=1, source_target_pairs={{0,32},{32,64},{64,96},{96,0},{1,33},{33,65},{65,97},{97,1},{2,34}... | collective-permute-start | bytes 589832 | tf_op jit(solution)/shard_map/ppermute | solution.py:36
  21.1 4.9 %collective-permute-done.2 = bf16[384,256]{1,0:T(8,128)(2,1)S(1)} collective-permute-done((bf16[384,256]{1,0:T(8,128)(2,1)S(1)}, bf16[384,256]{1,0:T(8,128)(2,1)S(1)}, u32[]{:S(2)}, u32[]{:S(2)}) %collective-permute-start.2) | collective-permute-done | bytes 196640 | tf_op jit(solution)/shard_map/ppermute | solution.py:36
  27.7 3.4 %collective-permute-start.8 = (bf16[1024,256]{1,0:T(8,128)(2,1)S(1)}, bf16[1024,256]{1,0:T(8,128)(2,1)S(1)}, u32[]{:S(2)}, u32[]{:S(2)}) collective-permute-start(bf16[1024,256]{1,0:T(8,128)(2,1)S(1)} %constant_dynamic-update-slice_fusion.3.k0.v0), channel_id=1, source_target_pairs={{0,128},{128,0},{1,129},{129,1},{2,130},{130,2},{3,131},{131,3},{4... | collective-permute-start | bytes 1572872 | tf_op jit(solution)/shard_map/ppermute | solution.py:36
  31.1 5.2 %collective-permute-start.9 = (bf16[512,256]{1,0:T(8,128)(2,1)S(1)}, bf16[512,256]{1,0:T(8,128)(2,1)S(1)}, u32[]{:S(2)}, u32[]{:S(2)}) collective-permute-start(bf16[512,256]{1,0:T(8,128)(2,1)S(1)} %pad_maximum_fusion.2.q_ref), channel_id=1, source_target_pairs={{0,16},{16,0},{1,17},{17,1},{2,18},{18,2},{3,19},{19,3},{4,20},{20... | collective-permute-start | bytes 786440 | tf_op jit(solution)/shard_map/ppermute | solution.py:36
  38.1 4.8 %collective-permute-done.9.q_ref = bf16[512,256]{1,0:T(8,128)(2,1)S(1)} collective-permute-done((bf16[512,256]{1,0:T(8,128)(2,1)S(1)}, bf16[512,256]{1,0:T(8,128)(2,1)S(1)}, u32[]{:S(2)}, u32[]{:S(2)}) %collective-permute-start.9) | collective-permute-done | bytes 262176 | tf_op jit(solution)/shard_map/ppermute | solution.py:36
  42.9 1.8 %shard_map.78 = (f32[512,256]{1,0:T(8,128)S(1)}, f32[8,512]{1,0:T(8,128)S(1)}) custom-call(bf16[512,256]{1,0:T(8,128)(2,1)S(1)} %collective-permute-done.9.q_ref, bf16[1024,256]{1,0:T(8,128)(2,1)S(1)} %constant_dynamic-update-slice_fusion.3.k0.v0, bf16[1024,256]{1,0:T(8,128)(2,1)S(1)} %collective-permute-done.10.k1.v1, ...), custom_call_target="tpu_custom_call" | custom-call | flops 536870912 | bytes 1048576 | tf_op jit(solution)/shard_map/pallas_call | solution.py:107
  46.7 2.1 %shard_map.81 = bf16[544,256]{1,0:T(8,128)(2,1)S(1)} custom-call(bf16[512,256]{1,0:T(8,128)(2,1)S(1)} %collective-permute-done.9.q_ref, bf16[1024,256]{1,0:T(8,128)(2,1)S(1)} %collective-permute-done.8.k0.v0, bf16[1024,256]{1,0:T(8,128)(2,1)S(1)} %collective-permute-done.11.k1.v1, bf16[1024,256]{1,0:T(8,128)(2,1)S(1)} %collective-permute-done.8.k0.v0, ...), custom_call_target="tpu_custom_call" | custom-call | flops 536870912 | bytes 1048576 | tf_op jit(solution)/shard_map/pallas_call | solution.py:107
  48.8 4.0 %collective-permute-start.12 = (bf16[544,256]{1,0:T(8,128)(2,1)S(1)}, bf16[544,256]{1,0:T(8,128)(2,1)S(1)}, u32[]{:S(2)}, u32[]{:S(2)}) collective-permute-start(bf16[544,256]{1,0:T(8,128)(2,1)S(1)} %shard_map.81), channel_id=1, source_target_pairs={{0,16},{16,0},{1,17},{17,1},{2,18},{18,2},{3,19},{19,3},{4,20},{20... | collective-permute-start | bytes 835592 | tf_op jit(solution)/shard_map/ppermute | solution.py:36
  53.8 2.1 %shard_map.80 = (f32[512,256]{1,0:T(8,128)S(1)}, f32[8,512]{1,0:T(8,128)S(1)}) custom-call(bf16[512,256]{1,0:T(8,128)(2,1)S(1)} %pad_maximum_fusion.2.q_ref, bf16[1024,256]{1,0:T(8,128)(2,1)S(1)} %collective-permute-done.8.k0.v0, bf16[1024,256]{1,0:T(8,128)(2,1)S(1)} %collective-permute-done.11.k1.v1, bf16[1024,256]{1,0:T(8,128)(2,1)S(1)} %collective-permute-done.8.k0.v0, ...), custom_call_target="tpu_custom_call" | custom-call | flops 536870912 | bytes 1048576 | tf_op jit(solution)/shard_map/pallas_call | solution.py:107
  55.9 2.6 %collective-permute-start.22 = (bf16[4,32,512]{2,1,0:T(8,128)(2,1)S(1)}, bf16[4,32,512]{2,1,0:T(8,128)(2,1)S(1)}, u32[]{:S(2)}, u32[]{:S(2)}) collective-permute-start(bf16[4,32,512]{2,1,0:T(8,128)(2,1)S(1)} %pad_maximum_fusion.7), channel_id=1, source_target_pairs={{0,4},{2,6},{4,0},{6,2},{1,5},{3,7},{5,1},{7,3},{8,12},{10,14},{12... | collective-permute-start | bytes 393224 | tf_op jit(solution)/shard_map/ppermute | solution.py:36
  63.3 2.8 %collective-permute-start.15 = (bf16[128,256]{1,0:T(8,128)(2,1)S(1)}, bf16[128,256]{1,0:T(8,128)(2,1)S(1)}, u32[]{:S(2)}, u32[]{:S(2)}) collective-permute-start(bf16[128,256]{1,0:T(8,128)(2,1)S(1)} %get-tuple-element.54), channel_id=1, source_target_pairs={{0,64},{32,96},{64,0},{96,32},{1,65},{33,97},{65,1},{97,33},{2,66}... | collective-permute-start | bytes 196616 | tf_op jit(solution)/shard_map/ppermute | solution.py:36
  66.3 3.2 %collective-permute-done.14 = bf16[128,256]{1,0:T(8,128)(2,1)S(1)} collective-permute-done((bf16[128,256]{1,0:T(8,128)(2,1)S(1)}, bf16[128,256]{1,0:T(8,128)(2,1)S(1)}, u32[]{:S(2)}, u32[]{:S(2)}) %collective-permute-start.14) | collective-permute-done | bytes 65568 | tf_op jit(solution)/shard_map/ppermute | solution.py:36
  69.6 2.1 %collective-permute-done.15 = bf16[128,256]{1,0:T(8,128)(2,1)S(1)} collective-permute-done((bf16[128,256]{1,0:T(8,128)(2,1)S(1)}, bf16[128,256]{1,0:T(8,128)(2,1)S(1)}, u32[]{:S(2)}, u32[]{:S(2)}) %collective-permute-start.15) | collective-permute-done | bytes 65568 | tf_op jit(solution)/shard_map/ppermute | solution.py:36
  71.6 3.4 %collective-permute-start.18 = (bf16[128,1024]{1,0:T(8,128)(2,1)S(1)}, bf16[128,1024]{1,0:T(8,128)(2,1)S(1)}, u32[]{:S(2)}, u32[]{:S(2)}) collective-permute-start(bf16[128,1024]{1,0:T(8,128)(2,1)S(1)} %constant_dynamic-update-slice_fusion), channel_id=1, source_target_pairs={{0,128},{1,129},{128,0},{129,1},{2,130},{3,131},{130,2},{131,3},{4... | collective-permute-start | bytes 786440 | tf_op jit(solution)/shard_map/ppermute | solution.py:36
  76.2 3.7 %convolution_convert_fusion = bf16[128,2048]{1,0:T(8,128)(2,1)} fusion(bf16[128,1024]{1,0:T(8,128)(2,1)S(1)} %constant_dynamic-update-slice_fusion, bf16[1024,2048]{1,0:T(8,128)(2,1)} %param.10), kind=kOutput, calls=%fused_computation | convolution fusion | flops 537133056 | bytes 4980736 | tf_op jit(solution)/shard_map/dot_general | solution.py:251
  79.9 1.9 %collective-permute-done.18 = bf16[128,1024]{1,0:T(8,128)(2,1)S(1)} collective-permute-done((bf16[128,1024]{1,0:T(8,128)(2,1)S(1)}, bf16[128,1024]{1,0:T(8,128)(2,1)S(1)}, u32[]{:S(2)}, u32[]{:S(2)}) %collective-permute-start.18) | collective-permute-done | bytes 262176 | tf_op jit(solution)/shard_map/ppermute | solution.py:36
  81.8 3.6 %collective-permute-done.17 = bf16[128,1024]{1,0:T(8,128)(2,1)S(1)} collective-permute-done((bf16[128,1024]{1,0:T(8,128)(2,1)S(1)}, bf16[128,1024]{1,0:T(8,128)(2,1)S(1)}, u32[]{:S(2)}, u32[]{:S(2)}) %collective-permute-start.17) | collective-permute-done | bytes 262176 | tf_op jit(solution)/shard_map/ppermute | solution.py:36
  86.7 2.0 %collective-permute-done.23 = bf16[4,2,32,1024]{3,2,1,0:T(8,128)(2,1)} collective-permute-done((bf16[4,2,32,1024]{3,2,1,0:T(8,128)(2,1)S(1)}, bf16[4,2,32,1024]{3,2,1,0:T(8,128)(2,1)}, u32[]{:S(2)}, u32[]{:S(2)}) %collective-permute-start.23) | collective-permute-done | bytes 524320 | tf_op jit(solution)/shard_map/ppermute | solution.py:36
  92.3 2.4 %collective-permute-start.21 = (bf16[32,2048]{1,0:T(8,128)(2,1)S(1)}, bf16[32,2048]{1,0:T(8,128)(2,1)S(1)}, u32[]{:S(2)}, u32[]{:S(2)}) collective-permute-start(bf16[32,2048]{1,0:T(8,128)(2,1)S(1)} %get-tuple-element.52), channel_id=1, source_target_pairs={{0,4},{2,6},{4,0},{6,2},{1,5},{3,7},{5,1},{7,3},{8,12},{10,14},{12... | collective-permute-start | bytes 393224 | tf_op jit(solution)/shard_map/ppermute | solution.py:36
  98.5 3.1 %collective-permute-start.27 = (bf16[32,1024]{1,0:T(8,128)(2,1)S(1)}, bf16[32,1024]{1,0:T(8,128)(2,1)S(1)}, u32[]{:S(2)}, u32[]{:S(2)}) collective-permute-start(bf16[32,1024]{1,0:T(8,128)(2,1)S(1)} %get-tuple-element.49), channel_id=1, source_target_pairs={{0,64},{32,96},{64,0},{96,32},{1,65},{33,97},{65,1},{97,33},{2,66}... | collective-permute-start | bytes 196616 | tf_op jit(solution)/shard_map/ppermute | solution.py:36
  101.6 2.0 %collective-permute-start.26 = (bf16[32,1024]{1,0:T(8,128)(2,1)S(1)}, bf16[32,1024]{1,0:T(8,128)(2,1)S(1)}, u32[]{:S(2)}, u32[]{:S(2)}) collective-permute-start(bf16[32,1024]{1,0:T(8,128)(2,1)S(1)} %get-tuple-element.50), channel_id=1, source_target_pairs={{0,96},{32,0},{64,32},{96,64},{1,97},{33,1},{65,33},{97,65},{2,98}... | collective-permute-start | bytes 196616 | tf_op jit(solution)/shard_map/ppermute | solution.py:36
  106.9 2.8 %collective-permute-done.26 = bf16[32,1024]{1,0:T(8,128)(2,1)S(1)} collective-permute-done((bf16[32,1024]{1,0:T(8,128)(2,1)S(1)}, bf16[32,1024]{1,0:T(8,128)(2,1)S(1)}, u32[]{:S(2)}, u32[]{:S(2)}) %collective-permute-start.26) | collective-permute-done | bytes 65568 | tf_op jit(solution)/shard_map/ppermute | solution.py:36
  (89 shorter events, 32.6 us)
Async XLA Ops:
  2.8 23.2 %collective-permute-start.2 = (bf16[384,256]{1,0:T(8,128)(2,1)S(1)}, bf16[384,256]{1,0:T(8,128)(2,1)S(1)}, u32[]{:S(2)}, u32[]{:S(2)}) collective-permute-start(bf16[384,256]{1,0:T(8,128)(2,1)S(1)} %pad_maximum_fusion.6), channel_id=1, source_target_pairs={{0,96},{32,0},{64,32},{96,64},{1,97},{33,1},{65,33},{97,65},{2,98}... | collective-permute-start | bytes 589832 | tf_op jit(solution)/shard_map/ppermute | solution.py:36
  9.2 16.8 %collective-permute-start.1 = (bf16[384,256]{1,0:T(8,128)(2,1)S(1)}, bf16[384,256]{1,0:T(8,128)(2,1)S(1)}, u32[]{:S(2)}, u32[]{:S(2)}) collective-permute-start(bf16[384,256]{1,0:T(8,128)(2,1)S(1)} %pad_maximum_fusion.5), channel_id=1, source_target_pairs={{0,64},{32,96},{64,0},{96,32},{1,65},{33,97},{65,1},{97,33},{2,66}... | collective-permute-start | bytes 589832 | tf_op jit(solution)/shard_map/ppermute | solution.py:36
  10.6 5.5 %collective-permute-start.5 = (bf16[32,512]{1,0:T(8,128)(2,1)S(1)}, bf16[32,512]{1,0:T(8,128)(2,1)S(1)}, u32[]{:S(2)}, u32[]{:S(2)}) collective-permute-start(bf16[32,512]{1,0:T(8,128)(2,1)S(1)} %get-tuple-element.80), channel_id=1, source_target_pairs={{0,128},{1,129},{128,0},{129,1},{2,130},{3,131},{130,2},{131,3},{4... | collective-permute-start | bytes 98312 | tf_op jit(solution)/shard_map/ppermute | solution.py:36
  16.1 11.3 %collective-permute-start = (bf16[384,256]{1,0:T(8,128)(2,1)S(1)}, bf16[384,256]{1,0:T(8,128)(2,1)S(1)}, u32[]{:S(2)}, u32[]{:S(2)}) collective-permute-start(bf16[384,256]{1,0:T(8,128)(2,1)S(1)} %pad_maximum_fusion.4), channel_id=1, source_target_pairs={{0,32},{32,64},{64,96},{96,0},{1,33},{33,65},{65,97},{97,1},{2,34}... | collective-permute-start | bytes 589832 | tf_op jit(solution)/shard_map/ppermute | solution.py:36
  19.0 8.5 %collective-permute-start.6 = (bf16[4,32,512]{2,1,0:T(8,128)(2,1)S(1)}, bf16[4,32,512]{2,1,0:T(8,128)(2,1)S(1)}, u32[]{:S(2)}, u32[]{:S(2)}) collective-permute-start(bf16[4,32,512]{2,1,0:T(8,128)(2,1)S(1)} %pad_maximum_fusion.7), channel_id=1, source_target_pairs={{0,2},{2,4},{4,6},{6,0},{1,3},{3,5},{5,7},{7,1},{8,10},{10,12},{12... | collective-permute-start | bytes 393224 | tf_op jit(solution)/shard_map/ppermute | solution.py:36
  20.7 6.9 %collective-permute-start.7 = (bf16[4,32,512]{2,1,0:T(8,128)(2,1)S(1)}, bf16[4,32,512]{2,1,0:T(8,128)(2,1)S(1)}, u32[]{:S(2)}, u32[]{:S(2)}) collective-permute-start(bf16[4,32,512]{2,1,0:T(8,128)(2,1)S(1)} %pad_maximum_fusion.7), channel_id=1, source_target_pairs={{0,6},{2,0},{4,2},{6,4},{1,7},{3,1},{5,3},{7,5},{8,14},{10,8},{12,... | collective-permute-start | bytes 393224 | tf_op jit(solution)/shard_map/ppermute | solution.py:36
  27.6 8.7 %collective-permute-start.10 = (bf16[1024,256]{1,0:T(8,128)(2,1)S(1)}, bf16[1024,256]{1,0:T(8,128)(2,1)S(1)}, u32[]{:S(2)}, u32[]{:S(2)}) collective-permute-start(bf16[1024,256]{1,0:T(8,128)(2,1)S(1)} %constant_dynamic-update-slice_fusion.3.k0.v0), channel_id=1, source_target_pairs={{0,8},{8,0},{1,9},{9,1},{2,10},{10,2},{3,11},{11,3},{4,12},{12,4},... | collective-permute-start | bytes 1572872 | tf_op jit(solution)/shard_map/ppermute | solution.py:36
  27.7 17.0 %collective-permute-start.8 = (bf16[1024,256]{1,0:T(8,128)(2,1)S(1)}, bf16[1024,256]{1,0:T(8,128)(2,1)S(1)}, u32[]{:S(2)}, u32[]{:S(2)}) collective-permute-start(bf16[1024,256]{1,0:T(8,128)(2,1)S(1)} %constant_dynamic-update-slice_fusion.3.k0.v0), channel_id=1, source_target_pairs={{0,128},{128,0},{1,129},{129,1},{2,130},{130,2},{3,131},{131,3},{4... | collective-permute-start | bytes 1572872 | tf_op jit(solution)/shard_map/ppermute | solution.py:36
  31.1 11.8 %collective-permute-start.9 = (bf16[512,256]{1,0:T(8,128)(2,1)S(1)}, bf16[512,256]{1,0:T(8,128)(2,1)S(1)}, u32[]{:S(2)}, u32[]{:S(2)}) collective-permute-start(bf16[512,256]{1,0:T(8,128)(2,1)S(1)} %pad_maximum_fusion.2.q_ref), channel_id=1, source_target_pairs={{0,16},{16,0},{1,17},{17,1},{2,18},{18,2},{3,19},{19,3},{4,20},{20... | collective-permute-start | bytes 786440 | tf_op jit(solution)/shard_map/ppermute | solution.py:36
  48.8 11.0 %collective-permute-start.12 = (bf16[544,256]{1,0:T(8,128)(2,1)S(1)}, bf16[544,256]{1,0:T(8,128)(2,1)S(1)}, u32[]{:S(2)}, u32[]{:S(2)}) collective-permute-start(bf16[544,256]{1,0:T(8,128)(2,1)S(1)} %shard_map.81), channel_id=1, source_target_pairs={{0,16},{16,0},{1,17},{17,1},{2,18},{18,2},{3,19},{19,3},{4,20},{20... | collective-permute-start | bytes 835592 | tf_op jit(solution)/shard_map/ppermute | solution.py:36
  55.9 10.1 %collective-permute-start.22 = (bf16[4,32,512]{2,1,0:T(8,128)(2,1)S(1)}, bf16[4,32,512]{2,1,0:T(8,128)(2,1)S(1)}, u32[]{:S(2)}, u32[]{:S(2)}) collective-permute-start(bf16[4,32,512]{2,1,0:T(8,128)(2,1)S(1)} %pad_maximum_fusion.7), channel_id=1, source_target_pairs={{0,4},{2,6},{4,0},{6,2},{1,5},{3,7},{5,1},{7,3},{8,12},{10,14},{12... | collective-permute-start | bytes 393224 | tf_op jit(solution)/shard_map/ppermute | solution.py:36
  60.3 6.0 %collective-permute-start.13 = (bf16[128,256]{1,0:T(8,128)(2,1)S(1)}, bf16[128,256]{1,0:T(8,128)(2,1)S(1)}, u32[]{:S(2)}, u32[]{:S(2)}) collective-permute-start(bf16[128,256]{1,0:T(8,128)(2,1)S(1)} %get-tuple-element.56), channel_id=1, source_target_pairs={{0,96},{32,0},{64,32},{96,64},{1,97},{33,1},{65,33},{97,65},{2,98}... | collective-permute-start | bytes 196616 | tf_op jit(solution)/shard_map/ppermute | solution.py:36
  62.0 7.6 %collective-permute-start.14 = (bf16[128,256]{1,0:T(8,128)(2,1)S(1)}, bf16[128,256]{1,0:T(8,128)(2,1)S(1)}, u32[]{:S(2)}, u32[]{:S(2)}) collective-permute-start(bf16[128,256]{1,0:T(8,128)(2,1)S(1)} %get-tuple-element.55), channel_id=1, source_target_pairs={{0,32},{32,64},{64,96},{96,0},{1,33},{33,65},{65,97},{97,1},{2,34}... | collective-permute-start | bytes 196616 | tf_op jit(solution)/shard_map/ppermute | solution.py:36
  63.3 8.4 %collective-permute-start.15 = (bf16[128,256]{1,0:T(8,128)(2,1)S(1)}, bf16[128,256]{1,0:T(8,128)(2,1)S(1)}, u32[]{:S(2)}, u32[]{:S(2)}) collective-permute-start(bf16[128,256]{1,0:T(8,128)(2,1)S(1)} %get-tuple-element.54), channel_id=1, source_target_pairs={{0,64},{32,96},{64,0},{96,32},{1,65},{33,97},{65,1},{97,33},{2,66}... | collective-permute-start | bytes 196616 | tf_op jit(solution)/shard_map/ppermute | solution.py:36
  71.6 10.2 %collective-permute-start.18 = (bf16[128,1024]{1,0:T(8,128)(2,1)S(1)}, bf16[128,1024]{1,0:T(8,128)(2,1)S(1)}, u32[]{:S(2)}, u32[]{:S(2)}) collective-permute-start(bf16[128,1024]{1,0:T(8,128)(2,1)S(1)} %constant_dynamic-update-slice_fusion), channel_id=1, source_target_pairs={{0,128},{1,129},{128,0},{129,1},{2,130},{3,131},{130,2},{131,3},{4... | collective-permute-start | bytes 786440 | tf_op jit(solution)/shard_map/ppermute | solution.py:36
  75.1 10.4 %collective-permute-start.17 = (bf16[128,1024]{1,0:T(8,128)(2,1)S(1)}, bf16[128,1024]{1,0:T(8,128)(2,1)S(1)}, u32[]{:S(2)}, u32[]{:S(2)}) collective-permute-start(bf16[128,1024]{1,0:T(8,128)(2,1)S(1)} %constant_dynamic-update-slice_fusion), channel_id=1, source_target_pairs={{0,129},{1,128},{128,1},{129,0},{2,131},{3,130},{130,3},{131,2},{4... | collective-permute-start | bytes 786440 | tf_op jit(solution)/shard_map/ppermute | solution.py:36
  76.2 9.5 %collective-permute-start.16 = (bf16[128,1024]{1,0:T(8,128)(2,1)S(1)}, bf16[128,1024]{1,0:T(8,128)(2,1)S(1)}, u32[]{:S(2)}, u32[]{:S(2)}) collective-permute-start(bf16[128,1024]{1,0:T(8,128)(2,1)S(1)} %constant_dynamic-update-slice_fusion), channel_id=1, source_target_pairs={{0,1},{1,0},{128,129},{129,128},{2,3},{3,2},{130,131},{131,130},{4... | collective-permute-start | bytes 786440 | tf_op jit(solution)/shard_map/ppermute | solution.py:36
  90.0 8.4 %collective-permute-start.24 = (bf16[4,32,1024]{2,1,0:T(8,128)(2,1)S(1)}, bf16[4,32,1024]{2,1,0:T(8,128)(2,1)S(1)}, u32[]{:S(2)}, u32[]{:S(2)}) collective-permute-start(bf16[4,32,1024]{2,1,0:T(8,128)(2,1)S(1)} %fusion.3), channel_id=1, source_target_pairs={{0,16},{16,0},{1,17},{17,1},{2,18},{18,2},{3,19},{19,3},{4,20},{20... | collective-permute-start | bytes 786440 | tf_op jit(solution)/shard_map/ppermute | solution.py:36
  92.3 11.3 %collective-permute-start.21 = (bf16[32,2048]{1,0:T(8,128)(2,1)S(1)}, bf16[32,2048]{1,0:T(8,128)(2,1)S(1)}, u32[]{:S(2)}, u32[]{:S(2)}) collective-permute-start(bf16[32,2048]{1,0:T(8,128)(2,1)S(1)} %get-tuple-element.52), channel_id=1, source_target_pairs={{0,4},{2,6},{4,0},{6,2},{1,5},{3,7},{5,1},{7,3},{8,12},{10,14},{12... | collective-permute-start | bytes 393224 | tf_op jit(solution)/shard_map/ppermute | solution.py:36
  94.6 9.9 %collective-permute-start.20 = (bf16[32,2048]{1,0:T(8,128)(2,1)S(1)}, bf16[32,2048]{1,0:T(8,128)(2,1)S(1)}, u32[]{:S(2)}, u32[]{:S(2)}) collective-permute-start(bf16[32,2048]{1,0:T(8,128)(2,1)S(1)} %get-tuple-element.53), channel_id=1, source_target_pairs={{0,6},{2,0},{4,2},{6,4},{1,7},{3,1},{5,3},{7,5},{8,14},{10,8},{12,... | collective-permute-start | bytes 393224 | tf_op jit(solution)/shard_map/ppermute | solution.py:36
  96.0 8.6 %collective-permute-start.19 = (bf16[32,2048]{1,0:T(8,128)(2,1)S(1)}, bf16[32,2048]{1,0:T(8,128)(2,1)S(1)}, u32[]{:S(2)}, u32[]{:S(2)}) collective-permute-start(bf16[32,2048]{1,0:T(8,128)(2,1)S(1)} %get-tuple-element.51), channel_id=1, source_target_pairs={{0,2},{2,4},{4,6},{6,0},{1,3},{3,5},{5,7},{7,1},{8,10},{10,12},{12... | collective-permute-start | bytes 393224 | tf_op jit(solution)/shard_map/ppermute | solution.py:36
  98.5 8.4 %collective-permute-start.27 = (bf16[32,1024]{1,0:T(8,128)(2,1)S(1)}, bf16[32,1024]{1,0:T(8,128)(2,1)S(1)}, u32[]{:S(2)}, u32[]{:S(2)}) collective-permute-start(bf16[32,1024]{1,0:T(8,128)(2,1)S(1)} %get-tuple-element.49), channel_id=1, source_target_pairs={{0,64},{32,96},{64,0},{96,32},{1,65},{33,97},{65,1},{97,33},{2,66}... | collective-permute-start | bytes 196616 | tf_op jit(solution)/shard_map/ppermute | solution.py:36
  101.6 8.1 %collective-permute-start.26 = (bf16[32,1024]{1,0:T(8,128)(2,1)S(1)}, bf16[32,1024]{1,0:T(8,128)(2,1)S(1)}, u32[]{:S(2)}, u32[]{:S(2)}) collective-permute-start(bf16[32,1024]{1,0:T(8,128)(2,1)S(1)} %get-tuple-element.50), channel_id=1, source_target_pairs={{0,96},{32,0},{64,32},{96,64},{1,97},{33,1},{65,33},{97,65},{2,98}... | collective-permute-start | bytes 196616 | tf_op jit(solution)/shard_map/ppermute | solution.py:36
  103.6 6.4 %collective-permute-start.25 = (bf16[32,1024]{1,0:T(8,128)(2,1)S(1)}, bf16[32,1024]{1,0:T(8,128)(2,1)S(1)}, u32[]{:S(2)}, u32[]{:S(2)}) collective-permute-start(bf16[32,1024]{1,0:T(8,128)(2,1)S(1)} %get-tuple-element.48), channel_id=1, source_target_pairs={{0,32},{32,64},{64,96},{96,0},{1,33},{33,65},{65,97},{97,1},{2,34}... | collective-permute-start | bytes 196616 | tf_op jit(solution)/shard_map/ppermute | solution.py:36
  (6 other events, 33.8 us)

commit v4 on v3

--- a/solution.py
+++ b/solution.py
@@ -158,26 +158,31 @@
     )(mine, mine_stat, theirs, theirs, live)
 
 
-def columns_body(grad, swap, out):
+def columns_body(grad, swap, earlier, out):
     for xh in range(2):
         for zq in range(4):
             at = (xh * 4 + zq) * 256
             both = jnp.dot(grad[:, at : at + 256], swap[...], preferred_element_type=F32).astype(BF)
             for xl in range(2):
-                out[xh, xl, :, zq * 128 : (zq + 1) * 128] = both[:, xl * 128 : (xl + 1) * 128]
-
-
-def by_owner(grad):
+                for core in range(2):
+                    at, to = xl * 128 + core * 64, core * 256 + zq * 64
+                    out[xh, xl, :, to : to + 64] = both[:, at : at + 64]
+
+
+def by_owner(grad, earlier):
     rows, width = grad.shape
     place = jnp.arange(256)
-    source = place % 128 // 32 * 64 + place // 128 * 32 + place % 32
+    source = place % 64 // 32 * 128 + place % 128 // 64 * 64 + place // 128 * 32 + place % 32
     swap = (place[:, None] == source[None, :]).astype(BF)
+    whole = pl.BlockSpec(memory_space=pltpu.VMEM)
     return pl.pallas_call(
         columns_body,
+        in_specs=[whole, whole, pl.BlockSpec(memory_space=pl.ANY)],
+        out_specs=whole,
         out_shape=jax.ShapeDtypeStruct((2, 2, rows, width // 4), BF),
         compiler_params=pltpu.CompilerParams(vmem_limit_bytes=VMEM // 2),
         cost_estimate=pl.CostEstimate(flops=2 * rows * width * 256, bytes_accessed=2**19, transcendentals=0),
-    )(grad, swap)
+    )(grad, swap, earlier)
 
 
 def beside(value, dh, dl):
@@ -194,12 +199,14 @@
         return lax.dynamic_slice_in_dim(array, ((zq + steps) % 4) * HEAD_DIM, HEAD_DIM, 1)
 
     sent = {d: jnp.concatenate([head_of(key, d), head_of(query, d), head_of(value, d)]) for d in range(4)}
+    owned = by_owner(out_grad[0], sent[2])
+    sent[3] = after(sent[3], owned)
     sent = {d: moved(sent[d], zq=d) if d else sent[d] for d in (1, 3, 2, 0)}
     k_own, q_own, v_own = (
         jnp.concatenate([sent[d][i * count : (i + 1) * count] for d in range(4)]) for i in range(3)
     )
     rows, width = out_grad.shape[1:]
-    grad = by_owner(out_grad[0])
+    grad = owned
 
     sides = ((0, 0), (0, 1), (1, 1), (1, 0))
 
@@ -247,15 +254,19 @@
         grad_rows = lax.dynamic_update_index_in_dim(grad_rows, grad_y[d], (y - d) % 4, 1)
     grad_rows = grad_rows.reshape(16 * rows, width // 4)
 
-    gathered = jnp.concatenate([beside(mine_back, *side) for side in sides])
+    half = grad_rows.shape[1] // 2
+    give = lax.dynamic_slice_in_dim(grad_rows, (1 - core) * half, half, 1)
+    keep = lax.dynamic_slice_in_dim(grad_rows, core * half, half, 1)
+    grad_rows = jnp.concatenate([keep, moved(after(give, mine_back), core=1)])
+    gathered = [beside(mine_back, *side) for side in sides]
+    gathered = jnp.concatenate(gathered + [moved(part, core=1) for part in gathered])
     projected = jnp.dot(mine_back, out_weight, preferred_element_type=F32).astype(BF).reshape(4, rows, width)
     gathered, projected = lax.optimization_barrier((gathered, projected))
     total = lax.dot_general(grad_rows, gathered, (((0,), (0,)), ((), ())), preferred_element_type=F32)
-    total = total.reshape(4, 2, 2, 32, 4 * HEAD_DIM)
-    for axis, name, place in ((2, "core", core), (1, "zr", zr)):
-        keep = lax.dynamic_index_in_dim(total, place, axis, keepdims=False)
-        give = lax.dynamic_index_in_dim(total, 1 - place, axis, keepdims=False)
-        total = keep + moved(give.astype(BF), **{name: 1}).astype(F32)
+    total = total.reshape(4, 2, 32, 4 * HEAD_DIM)
+    keep = lax.dynamic_index_in_dim(total, zr, 1, keepdims=False)
+    give = lax.dynamic_index_in_dim(total, 1 - zr, 1, keepdims=False)
+    total = keep + moved(give.astype(BF), zr=1).astype(F32)
     weight_grad = lax.dynamic_index_in_dim(total, zq, 0, keepdims=False)
     for d in (1, 3, 2):
         part = lax.dynamic_index_in_dim(total, (zq + d) % 4, 0, keepdims=False)

time: 112 us -> 110 us (0.982); the launches traced: 111 us -> 110 us
  waiting for transfers between devices: 33 us -> 41.8 us
  matrix products: 4.43 us -> 1.45 us
  starting transfers between devices: 54 us -> 51.7 us
  other arithmetic: 4.23 us -> 2.05 us
  local copies, waits for them, and re-layouts: 4.7 us -> 2.67 us
    ppermute x28 -> x32, waiting for transfers between devices: 33 us -> 41.8 us  [moved(): return lax.ppermute(value, names, pairs)]
    dot_general x1, matrix products: 3.69 us -> 0.73 us  [local(): jnp.dot(mine_back, out_weight, preferred_element_type=F32).astype(BF)]
    ppermute x28 -> x32, starting transfers between devices: 54 us -> 51.7 us  [moved(): return lax.ppermute(value, names, pairs)]
    add x3 -> x2, other arithmetic: 1.29 us -> 0.08 us  [the longest x1 0.07 us: local(): total = keep + moved(give.astype(BF), zr=1).astype(F32)]
  transfers between devices with their start and end apart: 28 -> 32, of which waited for: 16 -> 15; matrix products, arithmetic and copies ran while one was open for 8% -> 2% of each run, Pallas kernels for 6% -> 6%
where the time goes in v4:
time: 110 us
  starting transfers between devices  51.7 us (47%)
  waiting for transfers between devices  41.8 us (38%)
  Pallas kernels  8.58 us (8%)
  local copies, waits for them, and re-layouts  2.67 us (2%)
  other arithmetic  2.05 us (2%)
  between operations  1.86 us (2%)
  matrix products  1.45 us (1%)
    ppermute x32, starting transfers between devices, moved(): return lax.ppermute(value, names, pairs)  51.7 us
    ppermute x32, waiting for transfers between devices, moved(): return lax.ppermute(value, names, pairs)  41.8 us
    pallas_call x4, Pallas kernels, attend(): pl.pallas_call(functools.partial(attend_body, first=first, packed=packed)...  7.85 us
  transfers between devices with their start and end apart: 32, of which 15 were waited for; matrix products, arithmetic and copies ran while one was open for 2% of the time, Pallas kernels for 6%

profile of v4, /device:TPU:8, one launch (start us, length us, event | category | flops | bytes accessed | tf_op | source)
XLA Modules:
  0.0 110.1 jit_solution(5339878656635312165)
XLA Ops:
  2.8 7.3 %collective-permute-start.1 = (bf16[384,256]{1,0:T(8,128)(2,1)S(1)}, bf16[384,256]{1,0:T(8,128)(2,1)S(1)}, u32[]{:S(2)}, u32[]{:S(2)}) collective-permute-start(bf16[384,256]{1,0:T(8,128)(2,1)S(1)} %pad_maximum_fusion.4.earlier), channel_id=1, source_target_pairs={{0,64},{32,96},{64,0},{96,32},{1,65},{33,97},{65,1},{97,33},{2,66}... | collective-permute-start | bytes 589832 | tf_op jit(solution)/shard_map/ppermute | solution.py:36
  12.2 2.1 %collective-permute-start.4 = (bf16[32,512]{1,0:T(8,128)(2,1)S(1)}, bf16[32,512]{1,0:T(8,128)(2,1)S(1)}, u32[]{:S(2)}, u32[]{:S(2)}) collective-permute-start(bf16[32,512]{1,0:T(8,128)(2,1)S(1)} %get-tuple-element.87), channel_id=1, source_target_pairs={{0,129},{1,128},{128,1},{129,0},{2,131},{3,130},{130,3},{131,2},{4... | collective-permute-start | bytes 98312 | tf_op jit(solution)/shard_map/ppermute | solution.py:36
  17.6 2.7 %collective-permute-start.2 = (bf16[384,256]{1,0:T(8,128)(2,1)S(1)}, bf16[384,256]{1,0:T(8,128)(2,1)S(1)}, u32[]{:S(2)}, u32[]{:S(2)}) collective-permute-start(bf16[384,256]{1,0:T(8,128)(2,1)S(1)} %pad_maximum_fusion.5), channel_id=1, source_target_pairs={{0,96},{32,0},{64,32},{96,64},{1,97},{33,1},{65,33},{97,65},{2,98}... | collective-permute-start | bytes 589832 | tf_op jit(solution)/shard_map/ppermute | solution.py:36
  23.1 5.4 %collective-permute-done.2 = bf16[384,256]{1,0:T(8,128)(2,1)S(1)} collective-permute-done((bf16[384,256]{1,0:T(8,128)(2,1)S(1)}, bf16[384,256]{1,0:T(8,128)(2,1)S(1)}, u32[]{:S(2)}, u32[]{:S(2)}) %collective-permute-start.2) | collective-permute-done | bytes 196640 | tf_op jit(solution)/shard_map/ppermute | solution.py:36
  28.7 2.8 %collective-permute-start.8 = (bf16[1024,256]{1,0:T(8,128)(2,1)S(1)}, bf16[1024,256]{1,0:T(8,128)(2,1)S(1)}, u32[]{:S(2)}, u32[]{:S(2)}) collective-permute-start(bf16[1024,256]{1,0:T(8,128)(2,1)S(1)} %constant_dynamic-update-slice_fusion.k0.v0), channel_id=1, source_target_pairs={{0,128},{128,0},{1,129},{129,1},{2,130},{130,2},{3,131},{131,3},{4... | collective-permute-start | bytes 1572872 | tf_op jit(solution)/shard_map/ppermute | solution.py:36
  32.1 1.9 %shard_map.79 = (f32[512,256]{1,0:T(8,128)S(1)}, f32[8,512]{1,0:T(8,128)S(1)}) custom-call(bf16[512,256]{1,0:T(8,128)(2,1)S(1)} %pad_maximum_fusion.1.q_ref, bf16[1024,256]{1,0:T(8,128)(2,1)S(1)} %constant_dynamic-update-slice_fusion.k0.v0, bf16[1024,256]{1,0:T(8,128)(2,1)S(1)} %collective-permute-done.10.k1.v1, ...), custom_call_target="tpu_custom_call" | custom-call | flops 536870912 | bytes 1048576 | tf_op jit(solution)/shard_map/pallas_call | solution.py:107
  34.0 5.9 %collective-permute-done.9.q_ref = bf16[512,256]{1,0:T(8,128)(2,1)S(1)} collective-permute-done((bf16[512,256]{1,0:T(8,128)(2,1)S(1)}, bf16[512,256]{1,0:T(8,128)(2,1)S(1)}, u32[]{:S(2)}, u32[]{:S(2)}) %collective-permute-start.9) | collective-permute-done | bytes 262176 | tf_op jit(solution)/shard_map/ppermute | solution.py:36
  39.9 1.9 %shard_map.78 = (f32[512,256]{1,0:T(8,128)S(1)}, f32[8,512]{1,0:T(8,128)S(1)}) custom-call(bf16[512,256]{1,0:T(8,128)(2,1)S(1)} %collective-permute-done.9.q_ref, bf16[1024,256]{1,0:T(8,128)(2,1)S(1)} %constant_dynamic-update-slice_fusion.k0.v0, bf16[1024,256]{1,0:T(8,128)(2,1)S(1)} %collective-permute-done.10.k1.v1, ...), custom_call_target="tpu_custom_call" | custom-call | flops 536870912 | bytes 1048576 | tf_op jit(solution)/shard_map/pallas_call | solution.py:107
  41.8 2.8 %collective-permute-done.8.k0.v0 = bf16[1024,256]{1,0:T(8,128)(2,1)S(1)} collective-permute-done((bf16[1024,256]{1,0:T(8,128)(2,1)S(1)}, bf16[1024,256]{1,0:T(8,128)(2,1)S(1)}, u32[]{:S(2)}, u32[]{:S(2)}) %collective-permute-start.8) | collective-permute-done | bytes 524320 | tf_op jit(solution)/shard_map/ppermute | solution.py:36
  46.5 2.1 %shard_map.81 = bf16[544,256]{1,0:T(8,128)(2,1)S(1)} custom-call(bf16[512,256]{1,0:T(8,128)(2,1)S(1)} %collective-permute-done.9.q_ref, bf16[1024,256]{1,0:T(8,128)(2,1)S(1)} %collective-permute-done.8.k0.v0, bf16[1024,256]{1,0:T(8,128)(2,1)S(1)} %collective-permute-done.11.k1.v1, bf16[1024,256]{1,0:T(8,128)(2,1)S(1)} %collective-permute-done.8.k0.v0, ...), custom_call_target="tpu_custom_call" | custom-call | flops 536870912 | bytes 1048576 | tf_op jit(solution)/shard_map/pallas_call | solution.py:107
  48.9 2.1 %shard_map.80 = (f32[512,256]{1,0:T(8,128)S(1)}, f32[8,512]{1,0:T(8,128)S(1)}) custom-call(bf16[512,256]{1,0:T(8,128)(2,1)S(1)} %pad_maximum_fusion.1.q_ref, bf16[1024,256]{1,0:T(8,128)(2,1)S(1)} %collective-permute-done.8.k0.v0, bf16[1024,256]{1,0:T(8,128)(2,1)S(1)} %collective-permute-done.11.k1.v1, bf16[1024,256]{1,0:T(8,128)(2,1)S(1)} %collective-permute-done.8.k0.v0, ...), custom_call_target="tpu_custom_call" | custom-call | flops 536870912 | bytes 1048576 | tf_op jit(solution)/shard_map/pallas_call | solution.py:107
  51.0 2.6 %collective-permute-start.26 = (bf16[4,32,512]{2,1,0:T(8,128)(2,1)S(1)}, bf16[4,32,512]{2,1,0:T(8,128)(2,1)S(1)}, u32[]{:S(2)}, u32[]{:S(2)}) collective-permute-start(bf16[4,32,512]{2,1,0:T(8,128)(2,1)S(1)} %pad_maximum_fusion.6), channel_id=1, source_target_pairs={{0,4},{2,6},{4,0},{6,2},{1,5},{3,7},{5,1},{7,3},{8,12},{10,14},{12... | collective-permute-start | bytes 393224 | tf_op jit(solution)/shard_map/ppermute | solution.py:36
  53.6 3.8 %collective-permute-done.12.theirs.theirs_stat = bf16[544,256]{1,0:T(8,128)(2,1)S(1)} collective-permute-done((bf16[544,256]{1,0:T(8,128)(2,1)S(1)}, bf16[544,256]{1,0:T(8,128)(2,1)S(1)}, u32[]{:S(2)}, u32[]{:S(2)}) %collective-permute-start.12) | collective-permute-done | bytes 278560 | tf_op jit(solution)/shard_map/ppermute | solution.py:36
  58.1 4.1 %collective-permute-start.13 = (bf16[128,256]{1,0:T(8,128)(2,1)S(1)}, bf16[128,256]{1,0:T(8,128)(2,1)S(1)}, u32[]{:S(2)}, u32[]{:S(2)}) collective-permute-start(bf16[128,256]{1,0:T(8,128)(2,1)S(1)} %get-tuple-element.62), channel_id=1, source_target_pairs={{0,96},{32,0},{64,32},{96,64},{1,97},{33,1},{65,33},{97,65},{2,98}... | collective-permute-start | bytes 196616 | tf_op jit(solution)/shard_map/ppermute | solution.py:36
  62.2 4.1 %collective-permute-start.15 = (bf16[128,256]{1,0:T(8,128)(2,1)S(1)}, bf16[128,256]{1,0:T(8,128)(2,1)S(1)}, u32[]{:S(2)}, u32[]{:S(2)}) collective-permute-start(bf16[128,256]{1,0:T(8,128)(2,1)S(1)} %get-tuple-element.60), channel_id=1, source_target_pairs={{0,64},{32,96},{64,0},{96,32},{1,65},{33,97},{65,1},{97,33},{2,66}... | collective-permute-start | bytes 196616 | tf_op jit(solution)/shard_map/ppermute | solution.py:36
  66.4 4.3 %collective-permute-done.14 = bf16[128,256]{1,0:T(8,128)(2,1)S(1)} collective-permute-done((bf16[128,256]{1,0:T(8,128)(2,1)S(1)}, bf16[128,256]{1,0:T(8,128)(2,1)S(1)}, u32[]{:S(2)}, u32[]{:S(2)}) %collective-permute-start.14) | collective-permute-done | bytes 65568 | tf_op jit(solution)/shard_map/ppermute | solution.py:36
  72.1 2.1 %collective-permute-start.17 = (bf16[128,1024]{1,0:T(8,128)(2,1)S(1)}, bf16[128,1024]{1,0:T(8,128)(2,1)S(1)}, u32[]{:S(2)}, u32[]{:S(2)}) collective-permute-start(bf16[128,1024]{1,0:T(8,128)(2,1)S(1)} %constant_dynamic-update-slice_fusion.10), channel_id=1, source_target_pairs={{0,129},{1,128},{128,1},{129,0},{2,131},{3,130},{130,3},{131,2},{4... | collective-permute-start | bytes 786440 | tf_op jit(solution)/shard_map/ppermute | solution.py:36
  76.3 3.3 %collective-permute-done.16 = bf16[128,1024]{1,0:T(8,128)(2,1)S(1)} collective-permute-done((bf16[128,1024]{1,0:T(8,128)(2,1)S(1)}, bf16[128,1024]{1,0:T(8,128)(2,1)S(1)}, u32[]{:S(2)}, u32[]{:S(2)}) %collective-permute-start.16) | collective-permute-done | bytes 262176 | tf_op jit(solution)/shard_map/ppermute | solution.py:36
  79.6 4.8 %collective-permute-done.17 = bf16[128,1024]{1,0:T(8,128)(2,1)S(1)} collective-permute-done((bf16[128,1024]{1,0:T(8,128)(2,1)S(1)}, bf16[128,1024]{1,0:T(8,128)(2,1)S(1)}, u32[]{:S(2)}, u32[]{:S(2)}) %collective-permute-start.17) | collective-permute-done | bytes 262176 | tf_op jit(solution)/shard_map/ppermute | solution.py:36
  90.3 2.3 %collective-permute-start.25 = (bf16[32,2048]{1,0:T(8,128)(2,1)S(1)}, bf16[32,2048]{1,0:T(8,128)(2,1)S(1)}, u32[]{:S(2)}, u32[]{:S(2)}) collective-permute-start(bf16[32,2048]{1,0:T(8,128)(2,1)S(1)} %get-tuple-element.58), channel_id=1, source_target_pairs={{0,4},{2,6},{4,0},{6,2},{1,5},{3,7},{5,1},{7,3},{8,12},{10,14},{12... | collective-permute-start | bytes 393224 | tf_op jit(solution)/shard_map/ppermute | solution.py:36
  92.6 3.1 %collective-permute-done.28 = bf16[4,32,1024]{2,1,0:T(8,128)(2,1)S(1)} collective-permute-done((bf16[4,32,1024]{2,1,0:T(8,128)(2,1)S(1)}, bf16[4,32,1024]{2,1,0:T(8,128)(2,1)S(1)}, u32[]{:S(2)}, u32[]{:S(2)}) %collective-permute-start.28) | collective-permute-done | bytes 262176 | tf_op jit(solution)/shard_map/ppermute | solution.py:36
  95.8 4.7 %collective-permute-start.29 = (bf16[32,1024]{1,0:T(8,128)(2,1)S(1)}, bf16[32,1024]{1,0:T(8,128)(2,1)S(1)}, u32[]{:S(2)}, u32[]{:S(2)}) collective-permute-start(bf16[32,1024]{1,0:T(8,128)(2,1)S(1)} %get-tuple-element.52), channel_id=1, source_target_pairs={{0,32},{32,64},{64,96},{96,0},{1,33},{33,65},{65,97},{97,1},{2,34}... | collective-permute-start | bytes 196616 | tf_op jit(solution)/shard_map/ppermute | solution.py:36
  100.5 3.7 %collective-permute-start.31 = (bf16[32,1024]{1,0:T(8,128)(2,1)S(1)}, bf16[32,1024]{1,0:T(8,128)(2,1)S(1)}, u32[]{:S(2)}, u32[]{:S(2)}) collective-permute-start(bf16[32,1024]{1,0:T(8,128)(2,1)S(1)} %get-tuple-element.53), channel_id=1, source_target_pairs={{0,64},{32,96},{64,0},{96,32},{1,65},{33,97},{65,1},{97,33},{2,66}... | collective-permute-start | bytes 196616 | tf_op jit(solution)/shard_map/ppermute | solution.py:36
  106.5 2.9 %collective-permute-done.31 = bf16[32,1024]{1,0:T(8,128)(2,1)S(1)} collective-permute-done((bf16[32,1024]{1,0:T(8,128)(2,1)S(1)}, bf16[32,1024]{1,0:T(8,128)(2,1)S(1)}, u32[]{:S(2)}, u32[]{:S(2)}) %collective-permute-start.31) | collective-permute-done | bytes 65568 | tf_op jit(solution)/shard_map/ppermute | solution.py:36
  (102 shorter events, 25.8 us)
Async XLA Ops:
  2.8 25.6 %collective-permute-start.1 = (bf16[384,256]{1,0:T(8,128)(2,1)S(1)}, bf16[384,256]{1,0:T(8,128)(2,1)S(1)}, u32[]{:S(2)}, u32[]{:S(2)}) collective-permute-start(bf16[384,256]{1,0:T(8,128)(2,1)S(1)} %pad_maximum_fusion.4.earlier), channel_id=1, source_target_pairs={{0,64},{32,96},{64,0},{96,32},{1,65},{33,97},{65,1},{97,33},{2,66}... | collective-permute-start | bytes 589832 | tf_op jit(solution)/shard_map/ppermute | solution.py:36
  10.6 7.0 %collective-permute-start.3 = (bf16[32,512]{1,0:T(8,128)(2,1)S(1)}, bf16[32,512]{1,0:T(8,128)(2,1)S(1)}, u32[]{:S(2)}, u32[]{:S(2)}) collective-permute-start(bf16[32,512]{1,0:T(8,128)(2,1)S(1)} %get-tuple-element.88), channel_id=1, source_target_pairs={{0,1},{1,0},{128,129},{129,128},{2,3},{3,2},{130,131},{131,130},{4... | collective-permute-start | bytes 98312 | tf_op jit(solution)/shard_map/ppermute | solution.py:36
  12.2 8.1 %collective-permute-start.4 = (bf16[32,512]{1,0:T(8,128)(2,1)S(1)}, bf16[32,512]{1,0:T(8,128)(2,1)S(1)}, u32[]{:S(2)}, u32[]{:S(2)}) collective-permute-start(bf16[32,512]{1,0:T(8,128)(2,1)S(1)} %get-tuple-element.87), channel_id=1, source_target_pairs={{0,129},{1,128},{128,1},{129,0},{2,131},{3,130},{130,3},{131,2},{4... | collective-permute-start | bytes 98312 | tf_op jit(solution)/shard_map/ppermute | solution.py:36
  15.0 8.1 %collective-permute-start = (bf16[384,256]{1,0:T(8,128)(2,1)S(1)}, bf16[384,256]{1,0:T(8,128)(2,1)S(1)}, u32[]{:S(2)}, u32[]{:S(2)}) collective-permute-start(bf16[384,256]{1,0:T(8,128)(2,1)S(1)} %pad_maximum_fusion.3), channel_id=1, source_target_pairs={{0,32},{32,64},{64,96},{96,0},{1,33},{33,65},{65,97},{97,1},{2,34}... | collective-permute-start | bytes 589832 | tf_op jit(solution)/shard_map/ppermute | solution.py:36
  17.6 10.8 %collective-permute-start.2 = (bf16[384,256]{1,0:T(8,128)(2,1)S(1)}, bf16[384,256]{1,0:T(8,128)(2,1)S(1)}, u32[]{:S(2)}, u32[]{:S(2)}) collective-permute-start(bf16[384,256]{1,0:T(8,128)(2,1)S(1)} %pad_maximum_fusion.5), channel_id=1, source_target_pairs={{0,96},{32,0},{64,32},{96,64},{1,97},{33,1},{65,33},{97,65},{2,98}... | collective-permute-start | bytes 589832 | tf_op jit(solution)/shard_map/ppermute | solution.py:36
  20.4 8.2 %collective-permute-start.6 = (bf16[4,32,512]{2,1,0:T(8,128)(2,1)S(1)}, bf16[4,32,512]{2,1,0:T(8,128)(2,1)S(1)}, u32[]{:S(2)}, u32[]{:S(2)}) collective-permute-start(bf16[4,32,512]{2,1,0:T(8,128)(2,1)S(1)} %pad_maximum_fusion.6), channel_id=1, source_target_pairs={{0,2},{2,4},{4,6},{6,0},{1,3},{3,5},{5,7},{7,1},{8,10},{10,12},{12... | collective-permute-start | bytes 393224 | tf_op jit(solution)/shard_map/ppermute | solution.py:36
  28.7 15.8 %collective-permute-start.8 = (bf16[1024,256]{1,0:T(8,128)(2,1)S(1)}, bf16[1024,256]{1,0:T(8,128)(2,1)S(1)}, u32[]{:S(2)}, u32[]{:S(2)}) collective-permute-start(bf16[1024,256]{1,0:T(8,128)(2,1)S(1)} %constant_dynamic-update-slice_fusion.k0.v0), channel_id=1, source_target_pairs={{0,128},{128,0},{1,129},{129,1},{2,130},{130,2},{3,131},{131,3},{4... | collective-permute-start | bytes 1572872 | tf_op jit(solution)/shard_map/ppermute | solution.py:36
  31.6 8.4 %collective-permute-start.9 = (bf16[512,256]{1,0:T(8,128)(2,1)S(1)}, bf16[512,256]{1,0:T(8,128)(2,1)S(1)}, u32[]{:S(2)}, u32[]{:S(2)}) collective-permute-start(bf16[512,256]{1,0:T(8,128)(2,1)S(1)} %pad_maximum_fusion.1.q_ref), channel_id=1, source_target_pairs={{0,16},{16,0},{1,17},{17,1},{2,18},{18,2},{3,19},{19,3},{4,20},{20... | collective-permute-start | bytes 786440 | tf_op jit(solution)/shard_map/ppermute | solution.py:36
  48.6 8.8 %collective-permute-start.12 = (bf16[544,256]{1,0:T(8,128)(2,1)S(1)}, bf16[544,256]{1,0:T(8,128)(2,1)S(1)}, u32[]{:S(2)}, u32[]{:S(2)}) collective-permute-start(bf16[544,256]{1,0:T(8,128)(2,1)S(1)} %shard_map.81), channel_id=1, source_target_pairs={{0,16},{16,0},{1,17},{17,1},{2,18},{18,2},{3,19},{19,3},{4,20},{20... | collective-permute-start | bytes 835592 | tf_op jit(solution)/shard_map/ppermute | solution.py:36
  51.0 7.1 %collective-permute-start.26 = (bf16[4,32,512]{2,1,0:T(8,128)(2,1)S(1)}, bf16[4,32,512]{2,1,0:T(8,128)(2,1)S(1)}, u32[]{:S(2)}, u32[]{:S(2)}) collective-permute-start(bf16[4,32,512]{2,1,0:T(8,128)(2,1)S(1)} %pad_maximum_fusion.6), channel_id=1, source_target_pairs={{0,4},{2,6},{4,0},{6,2},{1,5},{3,7},{5,1},{7,3},{8,12},{10,14},{12... | collective-permute-start | bytes 393224 | tf_op jit(solution)/shard_map/ppermute | solution.py:36
  58.1 8.3 %collective-permute-start.13 = (bf16[128,256]{1,0:T(8,128)(2,1)S(1)}, bf16[128,256]{1,0:T(8,128)(2,1)S(1)}, u32[]{:S(2)}, u32[]{:S(2)}) collective-permute-start(bf16[128,256]{1,0:T(8,128)(2,1)S(1)} %get-tuple-element.62), channel_id=1, source_target_pairs={{0,96},{32,0},{64,32},{96,64},{1,97},{33,1},{65,33},{97,65},{2,98}... | collective-permute-start | bytes 196616 | tf_op jit(solution)/shard_map/ppermute | solution.py:36
  62.2 8.5 %collective-permute-start.14 = (bf16[128,256]{1,0:T(8,128)(2,1)S(1)}, bf16[128,256]{1,0:T(8,128)(2,1)S(1)}, u32[]{:S(2)}, u32[]{:S(2)}) collective-permute-start(bf16[128,256]{1,0:T(8,128)(2,1)S(1)} %get-tuple-element.61), channel_id=1, source_target_pairs={{0,32},{32,64},{64,96},{96,0},{1,33},{33,65},{65,97},{97,1},{2,34}... | collective-permute-start | bytes 196616 | tf_op jit(solution)/shard_map/ppermute | solution.py:36
  62.2 8.5 %collective-permute-start.15 = (bf16[128,256]{1,0:T(8,128)(2,1)S(1)}, bf16[128,256]{1,0:T(8,128)(2,1)S(1)}, u32[]{:S(2)}, u32[]{:S(2)}) collective-permute-start(bf16[128,256]{1,0:T(8,128)(2,1)S(1)} %get-tuple-element.60), channel_id=1, source_target_pairs={{0,64},{32,96},{64,0},{96,32},{1,65},{33,97},{65,1},{97,33},{2,66}... | collective-permute-start | bytes 196616 | tf_op jit(solution)/shard_map/ppermute | solution.py:36
  70.8 8.8 %collective-permute-start.16 = (bf16[128,1024]{1,0:T(8,128)(2,1)S(1)}, bf16[128,1024]{1,0:T(8,128)(2,1)S(1)}, u32[]{:S(2)}, u32[]{:S(2)}) collective-permute-start(bf16[128,1024]{1,0:T(8,128)(2,1)S(1)} %constant_dynamic-update-slice_fusion.10), channel_id=1, source_target_pairs={{0,1},{1,0},{128,129},{129,128},{2,3},{3,2},{130,131},{131,130},{4... | collective-permute-start | bytes 786440 | tf_op jit(solution)/shard_map/ppermute | solution.py:36
  72.1 12.3 %collective-permute-start.17 = (bf16[128,1024]{1,0:T(8,128)(2,1)S(1)}, bf16[128,1024]{1,0:T(8,128)(2,1)S(1)}, u32[]{:S(2)}, u32[]{:S(2)}) collective-permute-start(bf16[128,1024]{1,0:T(8,128)(2,1)S(1)} %constant_dynamic-update-slice_fusion.10), channel_id=1, source_target_pairs={{0,129},{1,128},{128,1},{129,0},{2,131},{3,130},{130,3},{131,2},{4... | collective-permute-start | bytes 786440 | tf_op jit(solution)/shard_map/ppermute | solution.py:36
  74.2 10.2 %collective-permute-start.18 = (bf16[128,1024]{1,0:T(8,128)(2,1)S(1)}, bf16[128,1024]{1,0:T(8,128)(2,1)S(1)}, u32[]{:S(2)}, u32[]{:S(2)}) collective-permute-start(bf16[128,1024]{1,0:T(8,128)(2,1)S(1)} %constant_dynamic-update-slice_fusion.10), channel_id=1, source_target_pairs={{0,128},{1,129},{128,0},{129,1},{2,130},{3,131},{130,2},{131,3},{4... | collective-permute-start | bytes 786440 | tf_op jit(solution)/shard_map/ppermute | solution.py:36
  74.9 11.4 %collective-permute-start.27 = (bf16[512,256]{1,0:T(8,128)(2,1)S(1)}, bf16[512,256]{1,0:T(8,128)(2,1)S(1)}, u32[]{:S(2)}, u32[]{:S(2)}) collective-permute-start(bf16[512,256]{1,0:T(8,128)(2,1)S(1)} %get-tuple-element.50), channel_id=1, source_target_pairs={{0,8},{8,0},{1,9},{9,1},{2,10},{10,2},{3,11},{11,3},{4,12},{12,4},... | collective-permute-start | bytes 786440 | tf_op jit(solution)/shard_map/ppermute | solution.py:36
  75.7 9.4 %collective-permute-start.19 = (bf16[128,1024]{1,0:T(8,128)(2,1)S(1)}, bf16[128,1024]{1,0:T(8,128)(2,1)S(1)}, u32[]{:S(2)}, u32[]{:S(2)}) collective-permute-start(bf16[128,1024]{1,0:T(8,128)(2,1)S(1)} %constant_dynamic-update-slice_fusion.10), channel_id=1, source_target_pairs={{0,8},{8,0},{1,9},{9,1},{2,10},{10,2},{3,11},{11,3},{4,12},{12,4},... | collective-permute-start | bytes 786440 | tf_op jit(solution)/shard_map/ppermute | solution.py:36
  87.1 8.6 %collective-permute-start.28 = (bf16[4,32,1024]{2,1,0:T(8,128)(2,1)S(1)}, bf16[4,32,1024]{2,1,0:T(8,128)(2,1)S(1)}, u32[]{:S(2)}, u32[]{:S(2)}) collective-permute-start(bf16[4,32,1024]{2,1,0:T(8,128)(2,1)S(1)} %fusion.4), channel_id=1, source_target_pairs={{0,16},{16,0},{1,17},{17,1},{2,18},{18,2},{3,19},{19,3},{4,20},{20... | collective-permute-start | bytes 786440 | tf_op jit(solution)/shard_map/ppermute | solution.py:36
  88.2 12.3 %collective-permute-start.23 = (bf16[32,2048]{1,0:T(8,128)(2,1)S(1)}, bf16[32,2048]{1,0:T(8,128)(2,1)S(1)}, u32[]{:S(2)}, u32[]{:S(2)}) collective-permute-start(bf16[32,2048]{1,0:T(8,128)(2,1)S(1)} %get-tuple-element.57), channel_id=1, source_target_pairs={{0,2},{2,4},{4,6},{6,0},{1,3},{3,5},{5,7},{7,1},{8,10},{10,12},{12... | collective-permute-start | bytes 393224 | tf_op jit(solution)/shard_map/ppermute | solution.py:36
  89.9 14.3 %collective-permute-start.24 = (bf16[32,2048]{1,0:T(8,128)(2,1)S(1)}, bf16[32,2048]{1,0:T(8,128)(2,1)S(1)}, u32[]{:S(2)}, u32[]{:S(2)}) collective-permute-start(bf16[32,2048]{1,0:T(8,128)(2,1)S(1)} %get-tuple-element.59), channel_id=1, source_target_pairs={{0,6},{2,0},{4,2},{6,4},{1,7},{3,1},{5,3},{7,5},{8,14},{10,8},{12,... | collective-permute-start | bytes 393224 | tf_op jit(solution)/shard_map/ppermute | solution.py:36
  90.3 13.8 %collective-permute-start.25 = (bf16[32,2048]{1,0:T(8,128)(2,1)S(1)}, bf16[32,2048]{1,0:T(8,128)(2,1)S(1)}, u32[]{:S(2)}, u32[]{:S(2)}) collective-permute-start(bf16[32,2048]{1,0:T(8,128)(2,1)S(1)} %get-tuple-element.58), channel_id=1, source_target_pairs={{0,4},{2,6},{4,0},{6,2},{1,5},{3,7},{5,1},{7,3},{8,12},{10,14},{12... | collective-permute-start | bytes 393224 | tf_op jit(solution)/shard_map/ppermute | solution.py:36
  95.8 9.1 %collective-permute-start.29 = (bf16[32,1024]{1,0:T(8,128)(2,1)S(1)}, bf16[32,1024]{1,0:T(8,128)(2,1)S(1)}, u32[]{:S(2)}, u32[]{:S(2)}) collective-permute-start(bf16[32,1024]{1,0:T(8,128)(2,1)S(1)} %get-tuple-element.52), channel_id=1, source_target_pairs={{0,32},{32,64},{64,96},{96,0},{1,33},{33,65},{65,97},{97,1},{2,34}... | collective-permute-start | bytes 196616 | tf_op jit(solution)/shard_map/ppermute | solution.py:36
  100.5 8.9 %collective-permute-start.31 = (bf16[32,1024]{1,0:T(8,128)(2,1)S(1)}, bf16[32,1024]{1,0:T(8,128)(2,1)S(1)}, u32[]{:S(2)}, u32[]{:S(2)}) collective-permute-start(bf16[32,1024]{1,0:T(8,128)(2,1)S(1)} %get-tuple-element.53), channel_id=1, source_target_pairs={{0,64},{32,96},{64,0},{96,32},{1,65},{33,97},{65,1},{97,33},{2,66}... | collective-permute-start | bytes 196616 | tf_op jit(solution)/shard_map/ppermute | solution.py:36
  (10 other events, 64.0 us)

commit v5 on v4

--- a/solution.py
+++ b/solution.py
@@ -40,9 +40,10 @@
     return lax.optimization_barrier((value, *earlier))[0]
 
 
-def attend_body(q_ref, k0, k1, v0, v1, bias, *refs, first, packed):
+def attend_body(q_ref, *refs, first, packed, blocks):
     tile = q_ref.shape[0]
     q = q_ref[...]
+    keys, values, bias, refs = refs[:blocks], refs[blocks : 2 * blocks], refs[2 * blocks], refs[2 * blocks + 1 :]
     if first:
         out, stat_out = refs
         acc = jnp.zeros((tile, HEAD_DIM), F32)
@@ -57,7 +58,7 @@
         top, total = down(stat_in[0:1]), down(stat_in[4:5])
     parts = []
     new_top = top
-    for i, k in enumerate((k0, k1)):
+    for i, k in enumerate(keys):
         s = lax.dot_general(q, k[...], (((1,), (1,)), ((), ())), preferred_element_type=F32)
         width = k.shape[0]
         parts.append(s * (math.log2(math.e) / math.sqrt(HEAD_DIM)) + bias[:, i * width : (i + 1) * width])
@@ -67,12 +68,12 @@
         total = total * fade
         acc = acc_in[...] * fade
     top = new_top
-    for s, v in zip(parts, (v0, v1)):
+    for s, v in zip(parts, values):
         e = jnp.exp2(s - top)
         total += e.sum(axis=1, keepdims=True)
         acc += jnp.dot(e.astype(BF), v[...], preferred_element_type=F32)
     if not packed:
-        out[...] = acc if first else acc / total
+        out[...] = acc
         stat_out = stat_out if first else stat_out[0]
         stat_out[:4, :] = jnp.broadcast_to(top, (tile, 128)).T[:4]
         stat_out[4:, :] = jnp.broadcast_to(total, (tile, 128)).T[:4]
@@ -90,7 +91,7 @@
     out[pl.ds(below, 16), :] = jnp.concatenate(lines).astype(BF)
 
 
-def attend(q, pieces, bias, before=None, packed=False):
+def attend(q, pieces, bias, at=0, before=None, packed=False):
     rows = q.shape[0]
     tile = 256
     steps = rows // tile
@@ -105,17 +106,19 @@
         out_specs = [rows_spec, stat_spec]
         out_shape = [jax.ShapeDtypeStruct((rows, HEAD_DIM), F32), jax.ShapeDtypeStruct((8, rows), F32)]
     return pl.pallas_call(
-        functools.partial(attend_body, first=first, packed=packed),
+        functools.partial(attend_body, first=first, packed=packed, blocks=len(pieces)),
         grid=(steps,),
         in_specs=[rows_spec]
-        + [pl.BlockSpec((part, HEAD_DIM), lambda i, at=at: (at, 0)) for at in (0, 0, 1, 1)]
-        + [pl.BlockSpec((1, 2 * part), lambda i: (0, 0 if first else 1))]
+        + [pl.BlockSpec((part, HEAD_DIM), lambda i, at=at: (at, 0)) for at in (0,) * len(pieces) + (1,) * len(pieces)]
+        + [pl.BlockSpec((1, len(pieces) * part), lambda i: (0, at))]
         + ([] if first else [rows_spec, stat_spec]),
         out_specs=out_specs,
         out_shape=out_shape,
         compiler_params=pltpu.CompilerParams(vmem_limit_bytes=VMEM),
         cost_estimate=pl.CostEstimate(
-            flops=8 * rows * part * HEAD_DIM, bytes_accessed=8 * part * HEAD_DIM, transcendentals=2 * rows * part
+            flops=4 * len(pieces) * rows * part * HEAD_DIM,
+            bytes_accessed=4 * len(pieces) * part * HEAD_DIM,
+            transcendentals=len(pieces) * rows * part,
         ),
     )(q, *pieces * 2, bias, *(() if first else before))
 
@@ -127,7 +130,8 @@
 
     top_mine, top_theirs = mine_stat[0:1], joined(0)
     top = jnp.maximum(top_mine, top_theirs)
-    part_mine = mine_stat[4:5] * jnp.exp2(top_mine - top)
+    fade_mine = jnp.exp2(top_mine - top)
+    part_mine = mine_stat[4:5] * fade_mine
     part_theirs = joined(8) * jnp.exp2(top_theirs - top)
     factor = live[...] / (part_mine + part_theirs)
     tile = out.shape[0]
@@ -136,7 +140,7 @@
         wide = jnp.broadcast_to(row, (128, tile)).T
         return jnp.concatenate([wide, wide], axis=1)
 
-    out[...] = (mine[...] * down(part_mine * factor) + theirs[...].astype(F32) * down(part_theirs * factor)).astype(BF)
+    out[...] = (mine[...] * down(fade_mine * factor) + theirs[...].astype(F32) * down(part_theirs * factor)).astype(BF)
 
 
 def combine(mine, mine_stat, theirs, live):
@@ -235,10 +239,10 @@
     here = (own, moved(own, core=1))
     begun = attend(q_other, here, bias), attend(q_own, here, bias)
     other, begun = lax.optimization_barrier((other, begun))
-    there = (other, moved(other, core=1))
-    theirs = attend(q_other, there, bias, begun[0], packed=True)
+    there = moved(other, core=1)
+    theirs = attend(q_other, (there,), bias, 3, attend(q_other, (other,), bias, 2, begun[0]), packed=True)
     theirs = moved(theirs, zr=1)
-    mine, mine_stat = attend(q_own, there, bias, begun[1])
+    mine, mine_stat = attend(q_own, (other, there), bias, 1, begun[1])
     grad_y[2] = moved(after(grad_y[0], mine_stat), y=2)
     context = combine(mine, mine_stat, theirs, live)
 

time: 110 us -> 110 us (level)
  waiting for transfers between devices: 41.8 us -> 40.5 us
    ppermute x32, waiting for transfers between devices: 41.8 us -> 40.5 us  [moved(): return lax.ppermute(value, names, pairs)]
    pallas_call x4 -> x5, Pallas kernels: 7.85 us -> 8.85 us  [attend(): pl.pallas_call(functools.partial(attend_body, first=first, packed=packed,...]
  transfers between devices with their start and end apart: 32 -> 32, of which waited for: 15 -> 15; matrix products, arithmetic and copies ran while one was open for 2% -> 2% of each run, Pallas kernels for 6% -> 7%
where the time goes in v5:
time: 110 us
  starting transfers between devices  51.6 us (47%)
  waiting for transfers between devices  40.5 us (37%)
  Pallas kernels  9.58 us (9%)
  local copies, waits for them, and re-layouts  2.67 us (2%)
  other arithmetic  2.05 us (2%)
  between operations  1.86 us (2%)
  matrix products  1.46 us (1%)
    ppermute x32, starting transfers between devices, moved(): return lax.ppermute(value, names, pairs)  51.6 us
    ppermute x32, waiting for transfers between devices, moved(): return lax.ppermute(value, names, pairs)  40.5 us
    pallas_call x5, Pallas kernels, attend(): pl.pallas_call(functools.partial(attend_body, first=first, packed=packed,...  8.85 us
  transfers between devices with their start and end apart: 32, of which 15 were waited for; matrix products, arithmetic and copies ran while one was open for 2% of the time, Pallas kernels for 7%

profile of v5, /device:TPU:8, one launch (start us, length us, event | category | flops | bytes accessed | tf_op | source)
XLA Modules:
  0.0 109.7 jit_solution(138174925389388369)
XLA Ops:
  2.8 7.3 %collective-permute-start.1 = (bf16[384,256]{1,0:T(8,128)(2,1)S(1)}, bf16[384,256]{1,0:T(8,128)(2,1)S(1)}, u32[]{:S(2)}, u32[]{:S(2)}) collective-permute-start(bf16[384,256]{1,0:T(8,128)(2,1)S(1)} %pad_maximum_fusion.4.earlier), channel_id=1, source_target_pairs={{0,64},{32,96},{64,0},{96,32},{1,65},{33,97},{65,1},{97,33},{2,66}... | collective-permute-start | bytes 589832 | tf_op jit(solution)/shard_map/ppermute | solution.py:36
  12.2 2.1 %collective-permute-start.4 = (bf16[32,512]{1,0:T(8,128)(2,1)S(1)}, bf16[32,512]{1,0:T(8,128)(2,1)S(1)}, u32[]{:S(2)}, u32[]{:S(2)}) collective-permute-start(bf16[32,512]{1,0:T(8,128)(2,1)S(1)} %get-tuple-element.91), channel_id=1, source_target_pairs={{0,129},{1,128},{128,1},{129,0},{2,131},{3,130},{130,3},{131,2},{4... | collective-permute-start | bytes 98312 | tf_op jit(solution)/shard_map/ppermute | solution.py:36
  17.6 2.7 %collective-permute-start.2 = (bf16[384,256]{1,0:T(8,128)(2,1)S(1)}, bf16[384,256]{1,0:T(8,128)(2,1)S(1)}, u32[]{:S(2)}, u32[]{:S(2)}) collective-permute-start(bf16[384,256]{1,0:T(8,128)(2,1)S(1)} %pad_maximum_fusion.5), channel_id=1, source_target_pairs={{0,96},{32,0},{64,32},{96,64},{1,97},{33,1},{65,33},{97,65},{2,98}... | collective-permute-start | bytes 589832 | tf_op jit(solution)/shard_map/ppermute | solution.py:36
  20.4 1.7 %collective-permute-start.6 = (bf16[4,32,512]{2,1,0:T(8,128)(2,1)S(1)}, bf16[4,32,512]{2,1,0:T(8,128)(2,1)S(1)}, u32[]{:S(2)}, u32[]{:S(2)}) collective-permute-start(bf16[4,32,512]{2,1,0:T(8,128)(2,1)S(1)} %pad_maximum_fusion.6), channel_id=1, source_target_pairs={{0,2},{2,4},{4,6},{6,0},{1,3},{3,5},{5,7},{7,1},{8,10},{10,12},{12... | collective-permute-start | bytes 393224 | tf_op jit(solution)/shard_map/ppermute | solution.py:36
  23.1 5.4 %collective-permute-done.2 = bf16[384,256]{1,0:T(8,128)(2,1)S(1)} collective-permute-done((bf16[384,256]{1,0:T(8,128)(2,1)S(1)}, bf16[384,256]{1,0:T(8,128)(2,1)S(1)}, u32[]{:S(2)}, u32[]{:S(2)}) %collective-permute-start.2) | collective-permute-done | bytes 196640 | tf_op jit(solution)/shard_map/ppermute | solution.py:36
  28.7 2.8 %collective-permute-start.8 = (bf16[1024,256]{1,0:T(8,128)(2,1)S(1)}, bf16[1024,256]{1,0:T(8,128)(2,1)S(1)}, u32[]{:S(2)}, u32[]{:S(2)}) collective-permute-start(bf16[1024,256]{1,0:T(8,128)(2,1)S(1)} %constant_dynamic-update-slice_fusion.refs_0_.refs_2_), channel_id=1, source_target_pairs={{0,128},{128,0},{1,129},{129,1},{2,130},{130,2},{3,131},{131,3},{4... | collective-permute-start | bytes 1572872 | tf_op jit(solution)/shard_map/ppermute | solution.py:36
  32.1 1.9 %shard_map.79 = (f32[512,256]{1,0:T(8,128)S(1)}, f32[8,512]{1,0:T(8,128)S(1)}) custom-call(bf16[512,256]{1,0:T(8,128)(2,1)S(1)} %pad_maximum_fusion.1.q_ref, bf16[1024,256]{1,0:T(8,128)(2,1)S(1)} %constant_dynamic-update-slice_fusion.refs_0_.refs_2_, bf16[1024,256]{1,0:T(8,128)(2,1)S(1)} %collective-permute-done.10.refs_1_.refs_3_, ...), custom_call_target="tpu_custom_call" | custom-call | flops 536870912 | bytes 1048576 | tf_op jit(solution)/shard_map/pallas_call | solution.py:108
  34.0 5.9 %collective-permute-done.9.q_ref = bf16[512,256]{1,0:T(8,128)(2,1)S(1)} collective-permute-done((bf16[512,256]{1,0:T(8,128)(2,1)S(1)}, bf16[512,256]{1,0:T(8,128)(2,1)S(1)}, u32[]{:S(2)}, u32[]{:S(2)}) %collective-permute-start.9) | collective-permute-done | bytes 262176 | tf_op jit(solution)/shard_map/ppermute | solution.py:36
  39.9 1.9 %shard_map.78 = (f32[512,256]{1,0:T(8,128)S(1)}, f32[8,512]{1,0:T(8,128)S(1)}) custom-call(bf16[512,256]{1,0:T(8,128)(2,1)S(1)} %collective-permute-done.9.q_ref, bf16[1024,256]{1,0:T(8,128)(2,1)S(1)} %constant_dynamic-update-slice_fusion.refs_0_.refs_2_, bf16[1024,256]{1,0:T(8,128)(2,1)S(1)} %collective-permute-done.10.refs_1_.refs_3_, ...), custom_call_target="tpu_custom_call" | custom-call | flops 536870912 | bytes 1048576 | tf_op jit(solution)/shard_map/pallas_call | solution.py:108
  41.8 2.8 %collective-permute-done.8.refs_0_.refs_2_.refs_1_ = bf16[1024,256]{1,0:T(8,128)(2,1)S(1)} collective-permute-done((bf16[1024,256]{1,0:T(8,128)(2,1)S(1)}, bf16[1024,256]{1,0:T(8,128)(2,1)S(1)}, u32[]{:S(2)}, u32[]{:S(2)}) %collective-permute-start.8) | collective-permute-done | bytes 524320 | tf_op jit(solution)/shard_map/ppermute | solution.py:36
  48.6 2.1 %shard_map.80 = (f32[512,256]{1,0:T(8,128)S(1)}, f32[8,512]{1,0:T(8,128)S(1)}) custom-call(bf16[512,256]{1,0:T(8,128)(2,1)S(1)} %pad_maximum_fusion.1.q_ref, bf16[1024,256]{1,0:T(8,128)(2,1)S(1)} %collective-permute-done.8.refs_0_.refs_2_.refs_1_, bf16[1024,256]{1,0:T(8,128)(2,1)S(1)} %collective-permute-done.11.refs_1_.refs_3_.refs_0_, ...), custom_call_target="tpu_custom_call" | custom-call | flops 536870912 | bytes 1048576 | tf_op jit(solution)/shard_map/pallas_call | solution.py:108
  50.6 2.4 %collective-permute-start.26 = (bf16[4,32,512]{2,1,0:T(8,128)(2,1)S(1)}, bf16[4,32,512]{2,1,0:T(8,128)(2,1)S(1)}, u32[]{:S(2)}, u32[]{:S(2)}) collective-permute-start(bf16[4,32,512]{2,1,0:T(8,128)(2,1)S(1)} %pad_maximum_fusion.6), channel_id=1, source_target_pairs={{0,4},{2,6},{4,0},{6,2},{1,5},{3,7},{5,1},{7,3},{8,12},{10,14},{12... | collective-permute-start | bytes 393224 | tf_op jit(solution)/shard_map/ppermute | solution.py:36
  53.1 4.0 %collective-permute-done.12.theirs.theirs_stat = bf16[544,256]{1,0:T(8,128)(2,1)S(1)} collective-permute-done((bf16[544,256]{1,0:T(8,128)(2,1)S(1)}, bf16[544,256]{1,0:T(8,128)(2,1)S(1)}, u32[]{:S(2)}, u32[]{:S(2)}) %collective-permute-start.12) | collective-permute-done | bytes 278560 | tf_op jit(solution)/shard_map/ppermute | solution.py:36
  57.7 4.1 %collective-permute-start.13 = (bf16[128,256]{1,0:T(8,128)(2,1)S(1)}, bf16[128,256]{1,0:T(8,128)(2,1)S(1)}, u32[]{:S(2)}, u32[]{:S(2)}) collective-permute-start(bf16[128,256]{1,0:T(8,128)(2,1)S(1)} %get-tuple-element.66), channel_id=1, source_target_pairs={{0,96},{32,0},{64,32},{96,64},{1,97},{33,1},{65,33},{97,65},{2,98}... | collective-permute-start | bytes 196616 | tf_op jit(solution)/shard_map/ppermute | solution.py:36
  61.8 4.1 %collective-permute-start.15 = (bf16[128,256]{1,0:T(8,128)(2,1)S(1)}, bf16[128,256]{1,0:T(8,128)(2,1)S(1)}, u32[]{:S(2)}, u32[]{:S(2)}) collective-permute-start(bf16[128,256]{1,0:T(8,128)(2,1)S(1)} %get-tuple-element.64), channel_id=1, source_target_pairs={{0,64},{32,96},{64,0},{96,32},{1,65},{33,97},{65,1},{97,33},{2,66}... | collective-permute-start | bytes 196616 | tf_op jit(solution)/shard_map/ppermute | solution.py:36
  66.0 4.3 %collective-permute-done.14 = bf16[128,256]{1,0:T(8,128)(2,1)S(1)} collective-permute-done((bf16[128,256]{1,0:T(8,128)(2,1)S(1)}, bf16[128,256]{1,0:T(8,128)(2,1)S(1)}, u32[]{:S(2)}, u32[]{:S(2)}) %collective-permute-start.14) | collective-permute-done | bytes 65568 | tf_op jit(solution)/shard_map/ppermute | solution.py:36
  71.7 2.1 %collective-permute-start.17 = (bf16[128,1024]{1,0:T(8,128)(2,1)S(1)}, bf16[128,1024]{1,0:T(8,128)(2,1)S(1)}, u32[]{:S(2)}, u32[]{:S(2)}) collective-permute-start(bf16[128,1024]{1,0:T(8,128)(2,1)S(1)} %constant_dynamic-update-slice_fusion.10), channel_id=1, source_target_pairs={{0,129},{1,128},{128,1},{129,0},{2,131},{3,130},{130,3},{131,2},{4... | collective-permute-start | bytes 786440 | tf_op jit(solution)/shard_map/ppermute | solution.py:36
  75.9 3.8 %collective-permute-done.16 = bf16[128,1024]{1,0:T(8,128)(2,1)S(1)} collective-permute-done((bf16[128,1024]{1,0:T(8,128)(2,1)S(1)}, bf16[128,1024]{1,0:T(8,128)(2,1)S(1)}, u32[]{:S(2)}, u32[]{:S(2)}) %collective-permute-start.16) | collective-permute-done | bytes 262176 | tf_op jit(solution)/shard_map/ppermute | solution.py:36
  79.7 4.4 %collective-permute-done.17 = bf16[128,1024]{1,0:T(8,128)(2,1)S(1)} collective-permute-done((bf16[128,1024]{1,0:T(8,128)(2,1)S(1)}, bf16[128,1024]{1,0:T(8,128)(2,1)S(1)}, u32[]{:S(2)}, u32[]{:S(2)}) %collective-permute-start.17) | collective-permute-done | bytes 262176 | tf_op jit(solution)/shard_map/ppermute | solution.py:36
  90.0 2.3 %collective-permute-start.25 = (bf16[32,2048]{1,0:T(8,128)(2,1)S(1)}, bf16[32,2048]{1,0:T(8,128)(2,1)S(1)}, u32[]{:S(2)}, u32[]{:S(2)}) collective-permute-start(bf16[32,2048]{1,0:T(8,128)(2,1)S(1)} %get-tuple-element.62), channel_id=1, source_target_pairs={{0,4},{2,6},{4,0},{6,2},{1,5},{3,7},{5,1},{7,3},{8,12},{10,14},{12... | collective-permute-start | bytes 393224 | tf_op jit(solution)/shard_map/ppermute | solution.py:36
  92.3 3.1 %collective-permute-done.28 = bf16[4,32,1024]{2,1,0:T(8,128)(2,1)S(1)} collective-permute-done((bf16[4,32,1024]{2,1,0:T(8,128)(2,1)S(1)}, bf16[4,32,1024]{2,1,0:T(8,128)(2,1)S(1)}, u32[]{:S(2)}, u32[]{:S(2)}) %collective-permute-start.28) | collective-permute-done | bytes 262176 | tf_op jit(solution)/shard_map/ppermute | solution.py:36
  95.5 4.6 %collective-permute-start.29 = (bf16[32,1024]{1,0:T(8,128)(2,1)S(1)}, bf16[32,1024]{1,0:T(8,128)(2,1)S(1)}, u32[]{:S(2)}, u32[]{:S(2)}) collective-permute-start(bf16[32,1024]{1,0:T(8,128)(2,1)S(1)} %get-tuple-element.56), channel_id=1, source_target_pairs={{0,32},{32,64},{64,96},{96,0},{1,33},{33,65},{65,97},{97,1},{2,34}... | collective-permute-start | bytes 196616 | tf_op jit(solution)/shard_map/ppermute | solution.py:36
  100.1 3.7 %collective-permute-start.31 = (bf16[32,1024]{1,0:T(8,128)(2,1)S(1)}, bf16[32,1024]{1,0:T(8,128)(2,1)S(1)}, u32[]{:S(2)}, u32[]{:S(2)}) collective-permute-start(bf16[32,1024]{1,0:T(8,128)(2,1)S(1)} %get-tuple-element.57), channel_id=1, source_target_pairs={{0,64},{32,96},{64,0},{96,32},{1,65},{33,97},{65,1},{97,33},{2,66}... | collective-permute-start | bytes 196616 | tf_op jit(solution)/shard_map/ppermute | solution.py:36
  106.1 3.0 %collective-permute-done.31 = bf16[32,1024]{1,0:T(8,128)(2,1)S(1)} collective-permute-done((bf16[32,1024]{1,0:T(8,128)(2,1)S(1)}, bf16[32,1024]{1,0:T(8,128)(2,1)S(1)}, u32[]{:S(2)}, u32[]{:S(2)}) %collective-permute-start.31) | collective-permute-done | bytes 65568 | tf_op jit(solution)/shard_map/ppermute | solution.py:36
  (103 shorter events, 25.6 us)
Async XLA Ops:
  2.8 25.6 %collective-permute-start.1 = (bf16[384,256]{1,0:T(8,128)(2,1)S(1)}, bf16[384,256]{1,0:T(8,128)(2,1)S(1)}, u32[]{:S(2)}, u32[]{:S(2)}) collective-permute-start(bf16[384,256]{1,0:T(8,128)(2,1)S(1)} %pad_maximum_fusion.4.earlier), channel_id=1, source_target_pairs={{0,64},{32,96},{64,0},{96,32},{1,65},{33,97},{65,1},{97,33},{2,66}... | collective-permute-start | bytes 589832 | tf_op jit(solution)/shard_map/ppermute | solution.py:36
  10.6 7.0 %collective-permute-start.3 = (bf16[32,512]{1,0:T(8,128)(2,1)S(1)}, bf16[32,512]{1,0:T(8,128)(2,1)S(1)}, u32[]{:S(2)}, u32[]{:S(2)}) collective-permute-start(bf16[32,512]{1,0:T(8,128)(2,1)S(1)} %get-tuple-element.92), channel_id=1, source_target_pairs={{0,1},{1,0},{128,129},{129,128},{2,3},{3,2},{130,131},{131,130},{4... | collective-permute-start | bytes 98312 | tf_op jit(solution)/shard_map/ppermute | solution.py:36
  12.2 8.1 %collective-permute-start.4 = (bf16[32,512]{1,0:T(8,128)(2,1)S(1)}, bf16[32,512]{1,0:T(8,128)(2,1)S(1)}, u32[]{:S(2)}, u32[]{:S(2)}) collective-permute-start(bf16[32,512]{1,0:T(8,128)(2,1)S(1)} %get-tuple-element.91), channel_id=1, source_target_pairs={{0,129},{1,128},{128,1},{129,0},{2,131},{3,130},{130,3},{131,2},{4... | collective-permute-start | bytes 98312 | tf_op jit(solution)/shard_map/ppermute | solution.py:36
  15.0 8.1 %collective-permute-start = (bf16[384,256]{1,0:T(8,128)(2,1)S(1)}, bf16[384,256]{1,0:T(8,128)(2,1)S(1)}, u32[]{:S(2)}, u32[]{:S(2)}) collective-permute-start(bf16[384,256]{1,0:T(8,128)(2,1)S(1)} %pad_maximum_fusion.3), channel_id=1, source_target_pairs={{0,32},{32,64},{64,96},{96,0},{1,33},{33,65},{65,97},{97,1},{2,34}... | collective-permute-start | bytes 589832 | tf_op jit(solution)/shard_map/ppermute | solution.py:36
  17.6 10.8 %collective-permute-start.2 = (bf16[384,256]{1,0:T(8,128)(2,1)S(1)}, bf16[384,256]{1,0:T(8,128)(2,1)S(1)}, u32[]{:S(2)}, u32[]{:S(2)}) collective-permute-start(bf16[384,256]{1,0:T(8,128)(2,1)S(1)} %pad_maximum_fusion.5), channel_id=1, source_target_pairs={{0,96},{32,0},{64,32},{96,64},{1,97},{33,1},{65,33},{97,65},{2,98}... | collective-permute-start | bytes 589832 | tf_op jit(solution)/shard_map/ppermute | solution.py:36
  20.4 8.2 %collective-permute-start.6 = (bf16[4,32,512]{2,1,0:T(8,128)(2,1)S(1)}, bf16[4,32,512]{2,1,0:T(8,128)(2,1)S(1)}, u32[]{:S(2)}, u32[]{:S(2)}) collective-permute-start(bf16[4,32,512]{2,1,0:T(8,128)(2,1)S(1)} %pad_maximum_fusion.6), channel_id=1, source_target_pairs={{0,2},{2,4},{4,6},{6,0},{1,3},{3,5},{5,7},{7,1},{8,10},{10,12},{12... | collective-permute-start | bytes 393224 | tf_op jit(solution)/shard_map/ppermute | solution.py:36
  28.7 15.8 %collective-permute-start.8 = (bf16[1024,256]{1,0:T(8,128)(2,1)S(1)}, bf16[1024,256]{1,0:T(8,128)(2,1)S(1)}, u32[]{:S(2)}, u32[]{:S(2)}) collective-permute-start(bf16[1024,256]{1,0:T(8,128)(2,1)S(1)} %constant_dynamic-update-slice_fusion.refs_0_.refs_2_), channel_id=1, source_target_pairs={{0,128},{128,0},{1,129},{129,1},{2,130},{130,2},{3,131},{131,3},{4... | collective-permute-start | bytes 1572872 | tf_op jit(solution)/shard_map/ppermute | solution.py:36
  31.6 8.4 %collective-permute-start.9 = (bf16[512,256]{1,0:T(8,128)(2,1)S(1)}, bf16[512,256]{1,0:T(8,128)(2,1)S(1)}, u32[]{:S(2)}, u32[]{:S(2)}) collective-permute-start(bf16[512,256]{1,0:T(8,128)(2,1)S(1)} %pad_maximum_fusion.1.q_ref), channel_id=1, source_target_pairs={{0,16},{16,0},{1,17},{17,1},{2,18},{18,2},{3,19},{19,3},{4,20},{20... | collective-permute-start | bytes 786440 | tf_op jit(solution)/shard_map/ppermute | solution.py:36
  48.0 9.1 %collective-permute-start.12 = (bf16[544,256]{1,0:T(8,128)(2,1)S(1)}, bf16[544,256]{1,0:T(8,128)(2,1)S(1)}, u32[]{:S(2)}, u32[]{:S(2)}) collective-permute-start(bf16[544,256]{1,0:T(8,128)(2,1)S(1)} %shard_map.82), channel_id=1, source_target_pairs={{0,16},{16,0},{1,17},{17,1},{2,18},{18,2},{3,19},{19,3},{4,20},{20... | collective-permute-start | bytes 835592 | tf_op jit(solution)/shard_map/ppermute | solution.py:36
  50.6 7.0 %collective-permute-start.26 = (bf16[4,32,512]{2,1,0:T(8,128)(2,1)S(1)}, bf16[4,32,512]{2,1,0:T(8,128)(2,1)S(1)}, u32[]{:S(2)}, u32[]{:S(2)}) collective-permute-start(bf16[4,32,512]{2,1,0:T(8,128)(2,1)S(1)} %pad_maximum_fusion.6), channel_id=1, source_target_pairs={{0,4},{2,6},{4,0},{6,2},{1,5},{3,7},{5,1},{7,3},{8,12},{10,14},{12... | collective-permute-start | bytes 393224 | tf_op jit(solution)/shard_map/ppermute | solution.py:36
  57.7 8.3 %collective-permute-start.13 = (bf16[128,256]{1,0:T(8,128)(2,1)S(1)}, bf16[128,256]{1,0:T(8,128)(2,1)S(1)}, u32[]{:S(2)}, u32[]{:S(2)}) collective-permute-start(bf16[128,256]{1,0:T(8,128)(2,1)S(1)} %get-tuple-element.66), channel_id=1, source_target_pairs={{0,96},{32,0},{64,32},{96,64},{1,97},{33,1},{65,33},{97,65},{2,98}... | collective-permute-start | bytes 196616 | tf_op jit(solution)/shard_map/ppermute | solution.py:36
  61.8 8.5 %collective-permute-start.14 = (bf16[128,256]{1,0:T(8,128)(2,1)S(1)}, bf16[128,256]{1,0:T(8,128)(2,1)S(1)}, u32[]{:S(2)}, u32[]{:S(2)}) collective-permute-start(bf16[128,256]{1,0:T(8,128)(2,1)S(1)} %get-tuple-element.65), channel_id=1, source_target_pairs={{0,32},{32,64},{64,96},{96,0},{1,33},{33,65},{65,97},{97,1},{2,34}... | collective-permute-start | bytes 196616 | tf_op jit(solution)/shard_map/ppermute | solution.py:36
  61.8 8.5 %collective-permute-start.15 = (bf16[128,256]{1,0:T(8,128)(2,1)S(1)}, bf16[128,256]{1,0:T(8,128)(2,1)S(1)}, u32[]{:S(2)}, u32[]{:S(2)}) collective-permute-start(bf16[128,256]{1,0:T(8,128)(2,1)S(1)} %get-tuple-element.64), channel_id=1, source_target_pairs={{0,64},{32,96},{64,0},{96,32},{1,65},{33,97},{65,1},{97,33},{2,66}... | collective-permute-start | bytes 196616 | tf_op jit(solution)/shard_map/ppermute | solution.py:36
  70.4 9.3 %collective-permute-start.16 = (bf16[128,1024]{1,0:T(8,128)(2,1)S(1)}, bf16[128,1024]{1,0:T(8,128)(2,1)S(1)}, u32[]{:S(2)}, u32[]{:S(2)}) collective-permute-start(bf16[128,1024]{1,0:T(8,128)(2,1)S(1)} %constant_dynamic-update-slice_fusion.10), channel_id=1, source_target_pairs={{0,1},{1,0},{128,129},{129,128},{2,3},{3,2},{130,131},{131,130},{4... | collective-permute-start | bytes 786440 | tf_op jit(solution)/shard_map/ppermute | solution.py:36
  71.7 12.4 %collective-permute-start.17 = (bf16[128,1024]{1,0:T(8,128)(2,1)S(1)}, bf16[128,1024]{1,0:T(8,128)(2,1)S(1)}, u32[]{:S(2)}, u32[]{:S(2)}) collective-permute-start(bf16[128,1024]{1,0:T(8,128)(2,1)S(1)} %constant_dynamic-update-slice_fusion.10), channel_id=1, source_target_pairs={{0,129},{1,128},{128,1},{129,0},{2,131},{3,130},{130,3},{131,2},{4... | collective-permute-start | bytes 786440 | tf_op jit(solution)/shard_map/ppermute | solution.py:36
  73.8 10.3 %collective-permute-start.18 = (bf16[128,1024]{1,0:T(8,128)(2,1)S(1)}, bf16[128,1024]{1,0:T(8,128)(2,1)S(1)}, u32[]{:S(2)}, u32[]{:S(2)}) collective-permute-start(bf16[128,1024]{1,0:T(8,128)(2,1)S(1)} %constant_dynamic-update-slice_fusion.10), channel_id=1, source_target_pairs={{0,128},{1,129},{128,0},{129,1},{2,130},{3,131},{130,2},{131,3},{4... | collective-permute-start | bytes 786440 | tf_op jit(solution)/shard_map/ppermute | solution.py:36
  74.5 11.5 %collective-permute-start.27 = (bf16[512,256]{1,0:T(8,128)(2,1)S(1)}, bf16[512,256]{1,0:T(8,128)(2,1)S(1)}, u32[]{:S(2)}, u32[]{:S(2)}) collective-permute-start(bf16[512,256]{1,0:T(8,128)(2,1)S(1)} %get-tuple-element.54), channel_id=1, source_target_pairs={{0,8},{8,0},{1,9},{9,1},{2,10},{10,2},{3,11},{11,3},{4,12},{12,4},... | collective-permute-start | bytes 786440 | tf_op jit(solution)/shard_map/ppermute | solution.py:36
  75.3 9.4 %collective-permute-start.19 = (bf16[128,1024]{1,0:T(8,128)(2,1)S(1)}, bf16[128,1024]{1,0:T(8,128)(2,1)S(1)}, u32[]{:S(2)}, u32[]{:S(2)}) collective-permute-start(bf16[128,1024]{1,0:T(8,128)(2,1)S(1)} %constant_dynamic-update-slice_fusion.10), channel_id=1, source_target_pairs={{0,8},{8,0},{1,9},{9,1},{2,10},{10,2},{3,11},{11,3},{4,12},{12,4},... | collective-permute-start | bytes 786440 | tf_op jit(solution)/shard_map/ppermute | solution.py:36
  86.8 8.6 %collective-permute-start.28 = (bf16[4,32,1024]{2,1,0:T(8,128)(2,1)S(1)}, bf16[4,32,1024]{2,1,0:T(8,128)(2,1)S(1)}, u32[]{:S(2)}, u32[]{:S(2)}) collective-permute-start(bf16[4,32,1024]{2,1,0:T(8,128)(2,1)S(1)} %fusion.4), channel_id=1, source_target_pairs={{0,16},{16,0},{1,17},{17,1},{2,18},{18,2},{3,19},{19,3},{4,20},{20... | collective-permute-start | bytes 786440 | tf_op jit(solution)/shard_map/ppermute | solution.py:36
  87.9 12.2 %collective-permute-start.23 = (bf16[32,2048]{1,0:T(8,128)(2,1)S(1)}, bf16[32,2048]{1,0:T(8,128)(2,1)S(1)}, u32[]{:S(2)}, u32[]{:S(2)}) collective-permute-start(bf16[32,2048]{1,0:T(8,128)(2,1)S(1)} %get-tuple-element.61), channel_id=1, source_target_pairs={{0,2},{2,4},{4,6},{6,0},{1,3},{3,5},{5,7},{7,1},{8,10},{10,12},{12... | collective-permute-start | bytes 393224 | tf_op jit(solution)/shard_map/ppermute | solution.py:36
  89.5 14.2 %collective-permute-start.24 = (bf16[32,2048]{1,0:T(8,128)(2,1)S(1)}, bf16[32,2048]{1,0:T(8,128)(2,1)S(1)}, u32[]{:S(2)}, u32[]{:S(2)}) collective-permute-start(bf16[32,2048]{1,0:T(8,128)(2,1)S(1)} %get-tuple-element.63), channel_id=1, source_target_pairs={{0,6},{2,0},{4,2},{6,4},{1,7},{3,1},{5,3},{7,5},{8,14},{10,8},{12,... | collective-permute-start | bytes 393224 | tf_op jit(solution)/shard_map/ppermute | solution.py:36
  90.0 13.8 %collective-permute-start.25 = (bf16[32,2048]{1,0:T(8,128)(2,1)S(1)}, bf16[32,2048]{1,0:T(8,128)(2,1)S(1)}, u32[]{:S(2)}, u32[]{:S(2)}) collective-permute-start(bf16[32,2048]{1,0:T(8,128)(2,1)S(1)} %get-tuple-element.62), channel_id=1, source_target_pairs={{0,4},{2,6},{4,0},{6,2},{1,5},{3,7},{5,1},{7,3},{8,12},{10,14},{12... | collective-permute-start | bytes 393224 | tf_op jit(solution)/shard_map/ppermute | solution.py:36
  95.5 9.0 %collective-permute-start.29 = (bf16[32,1024]{1,0:T(8,128)(2,1)S(1)}, bf16[32,1024]{1,0:T(8,128)(2,1)S(1)}, u32[]{:S(2)}, u32[]{:S(2)}) collective-permute-start(bf16[32,1024]{1,0:T(8,128)(2,1)S(1)} %get-tuple-element.56), channel_id=1, source_target_pairs={{0,32},{32,64},{64,96},{96,0},{1,33},{33,65},{65,97},{97,1},{2,34}... | collective-permute-start | bytes 196616 | tf_op jit(solution)/shard_map/ppermute | solution.py:36
  100.1 9.0 %collective-permute-start.31 = (bf16[32,1024]{1,0:T(8,128)(2,1)S(1)}, bf16[32,1024]{1,0:T(8,128)(2,1)S(1)}, u32[]{:S(2)}, u32[]{:S(2)}) collective-permute-start(bf16[32,1024]{1,0:T(8,128)(2,1)S(1)} %get-tuple-element.57), channel_id=1, source_target_pairs={{0,64},{32,96},{64,0},{96,32},{1,65},{33,97},{65,1},{97,33},{2,66}... | collective-permute-start | bytes 196616 | tf_op jit(solution)/shard_map/ppermute | solution.py:36
  (10 other events, 63.6 us)

commit v6 on v4

--- a/solution.py
+++ b/solution.py
@@ -244,7 +244,7 @@
 
     back = context.reshape(4, count, HEAD_DIM)
     mine_back = jnp.zeros((count, 4 * HEAD_DIM), BF)
-    for d in (0, 1, 3, 2):
+    for d in (0, 2, 1, 3):
         part = moved(back[d], zq=-d) if d else back[d]
         mine_back = lax.dynamic_update_slice_in_dim(mine_back, part, ((zq + d) % 4) * HEAD_DIM, 1)
 

time: 110 us -> 111 us (level)
  waiting for transfers between devices: 41.8 us -> 45.5 us
  starting transfers between devices: 51.7 us -> 49 us
    ppermute x32, waiting for transfers between devices: 41.8 us -> 45.5 us  [moved(): return lax.ppermute(value, names, pairs)]
    ppermute x32, starting transfers between devices: 51.7 us -> 49 us  [moved(): return lax.ppermute(value, names, pairs)]
  transfers between devices with their start and end apart: 32 -> 32, of which waited for: 15 -> 17; matrix products, arithmetic and copies ran while one was open for 2% -> 2% of each run, Pallas kernels for 6% -> 6%
where the time goes in v6:
time: 111 us
  starting transfers between devices  49 us (44%)
  waiting for transfers between devices  45.5 us (41%)
  Pallas kernels  8.58 us (8%)
  local copies, waits for them, and re-layouts  2.67 us (2%)
  other arithmetic  2.05 us (2%)
  between operations  1.91 us (2%)
  matrix products  1.45 us (1%)
    ppermute x32, starting transfers between devices, moved(): return lax.ppermute(value, names, pairs)  49 us
    ppermute x32, waiting for transfers between devices, moved(): return lax.ppermute(value, names, pairs)  45.5 us
    pallas_call x4, Pallas kernels, attend(): pl.pallas_call(functools.partial(attend_body, first=first, packed=packed)...  7.85 us
  transfers between devices with their start and end apart: 32, of which 17 were waited for; matrix products, arithmetic and copies ran while one was open for 2% of the time, Pallas kernels for 6%

profile of v6, /device:TPU:8, one launch (start us, length us, event | category | flops | bytes accessed | tf_op | source)
XLA Modules:
  0.0 111.2 jit_solution(2193992978020524608)
XLA Ops:
  2.8 7.3 %collective-permute-start.1 = (bf16[384,256]{1,0:T(8,128)(2,1)S(1)}, bf16[384,256]{1,0:T(8,128)(2,1)S(1)}, u32[]{:S(2)}, u32[]{:S(2)}) collective-permute-start(bf16[384,256]{1,0:T(8,128)(2,1)S(1)} %pad_maximum_fusion.4.earlier), channel_id=1, source_target_pairs={{0,64},{32,96},{64,0},{96,32},{1,65},{33,97},{65,1},{97,33},{2,66}... | collective-permute-start | bytes 589832 | tf_op jit(solution)/shard_map/ppermute | solution.py:36
  12.2 2.1 %collective-permute-start.4 = (bf16[32,512]{1,0:T(8,128)(2,1)S(1)}, bf16[32,512]{1,0:T(8,128)(2,1)S(1)}, u32[]{:S(2)}, u32[]{:S(2)}) collective-permute-start(bf16[32,512]{1,0:T(8,128)(2,1)S(1)} %get-tuple-element.87), channel_id=1, source_target_pairs={{0,129},{1,128},{128,1},{129,0},{2,131},{3,130},{130,3},{131,2},{4... | collective-permute-start | bytes 98312 | tf_op jit(solution)/shard_map/ppermute | solution.py:36
  17.6 2.7 %collective-permute-start.2 = (bf16[384,256]{1,0:T(8,128)(2,1)S(1)}, bf16[384,256]{1,0:T(8,128)(2,1)S(1)}, u32[]{:S(2)}, u32[]{:S(2)}) collective-permute-start(bf16[384,256]{1,0:T(8,128)(2,1)S(1)} %pad_maximum_fusion.5), channel_id=1, source_target_pairs={{0,96},{32,0},{64,32},{96,64},{1,97},{33,1},{65,33},{97,65},{2,98}... | collective-permute-start | bytes 589832 | tf_op jit(solution)/shard_map/ppermute | solution.py:36
  23.1 5.4 %collective-permute-done.2 = bf16[384,256]{1,0:T(8,128)(2,1)S(1)} collective-permute-done((bf16[384,256]{1,0:T(8,128)(2,1)S(1)}, bf16[384,256]{1,0:T(8,128)(2,1)S(1)}, u32[]{:S(2)}, u32[]{:S(2)}) %collective-permute-start.2) | collective-permute-done | bytes 196640 | tf_op jit(solution)/shard_map/ppermute | solution.py:36
  28.7 2.8 %collective-permute-start.8 = (bf16[1024,256]{1,0:T(8,128)(2,1)S(1)}, bf16[1024,256]{1,0:T(8,128)(2,1)S(1)}, u32[]{:S(2)}, u32[]{:S(2)}) collective-permute-start(bf16[1024,256]{1,0:T(8,128)(2,1)S(1)} %constant_dynamic-update-slice_fusion.k0.v0), channel_id=1, source_target_pairs={{0,128},{128,0},{1,129},{129,1},{2,130},{130,2},{3,131},{131,3},{4... | collective-permute-start | bytes 1572872 | tf_op jit(solution)/shard_map/ppermute | solution.py:36
  32.1 1.9 %shard_map.79 = (f32[512,256]{1,0:T(8,128)S(1)}, f32[8,512]{1,0:T(8,128)S(1)}) custom-call(bf16[512,256]{1,0:T(8,128)(2,1)S(1)} %pad_maximum_fusion.1.q_ref, bf16[1024,256]{1,0:T(8,128)(2,1)S(1)} %constant_dynamic-update-slice_fusion.k0.v0, bf16[1024,256]{1,0:T(8,128)(2,1)S(1)} %collective-permute-done.10.k1.v1, ...), custom_call_target="tpu_custom_call" | custom-call | flops 536870912 | bytes 1048576 | tf_op jit(solution)/shard_map/pallas_call | solution.py:107
  34.0 5.9 %collective-permute-done.9.q_ref = bf16[512,256]{1,0:T(8,128)(2,1)S(1)} collective-permute-done((bf16[512,256]{1,0:T(8,128)(2,1)S(1)}, bf16[512,256]{1,0:T(8,128)(2,1)S(1)}, u32[]{:S(2)}, u32[]{:S(2)}) %collective-permute-start.9) | collective-permute-done | bytes 262176 | tf_op jit(solution)/shard_map/ppermute | solution.py:36
  39.9 1.9 %shard_map.78 = (f32[512,256]{1,0:T(8,128)S(1)}, f32[8,512]{1,0:T(8,128)S(1)}) custom-call(bf16[512,256]{1,0:T(8,128)(2,1)S(1)} %collective-permute-done.9.q_ref, bf16[1024,256]{1,0:T(8,128)(2,1)S(1)} %constant_dynamic-update-slice_fusion.k0.v0, bf16[1024,256]{1,0:T(8,128)(2,1)S(1)} %collective-permute-done.10.k1.v1, ...), custom_call_target="tpu_custom_call" | custom-call | flops 536870912 | bytes 1048576 | tf_op jit(solution)/shard_map/pallas_call | solution.py:107
  41.8 2.8 %collective-permute-done.8.k0.v0 = bf16[1024,256]{1,0:T(8,128)(2,1)S(1)} collective-permute-done((bf16[1024,256]{1,0:T(8,128)(2,1)S(1)}, bf16[1024,256]{1,0:T(8,128)(2,1)S(1)}, u32[]{:S(2)}, u32[]{:S(2)}) %collective-permute-start.8) | collective-permute-done | bytes 524320 | tf_op jit(solution)/shard_map/ppermute | solution.py:36
  46.5 2.1 %shard_map.81 = bf16[544,256]{1,0:T(8,128)(2,1)S(1)} custom-call(bf16[512,256]{1,0:T(8,128)(2,1)S(1)} %collective-permute-done.9.q_ref, bf16[1024,256]{1,0:T(8,128)(2,1)S(1)} %collective-permute-done.8.k0.v0, bf16[1024,256]{1,0:T(8,128)(2,1)S(1)} %collective-permute-done.11.k1.v1, bf16[1024,256]{1,0:T(8,128)(2,1)S(1)} %collective-permute-done.8.k0.v0, ...), custom_call_target="tpu_custom_call" | custom-call | flops 536870912 | bytes 1048576 | tf_op jit(solution)/shard_map/pallas_call | solution.py:107
  48.9 2.1 %shard_map.80 = (f32[512,256]{1,0:T(8,128)S(1)}, f32[8,512]{1,0:T(8,128)S(1)}) custom-call(bf16[512,256]{1,0:T(8,128)(2,1)S(1)} %pad_maximum_fusion.1.q_ref, bf16[1024,256]{1,0:T(8,128)(2,1)S(1)} %collective-permute-done.8.k0.v0, bf16[1024,256]{1,0:T(8,128)(2,1)S(1)} %collective-permute-done.11.k1.v1, bf16[1024,256]{1,0:T(8,128)(2,1)S(1)} %collective-permute-done.8.k0.v0, ...), custom_call_target="tpu_custom_call" | custom-call | flops 536870912 | bytes 1048576 | tf_op jit(solution)/shard_map/pallas_call | solution.py:107
  51.0 2.6 %collective-permute-start.26 = (bf16[4,32,512]{2,1,0:T(8,128)(2,1)S(1)}, bf16[4,32,512]{2,1,0:T(8,128)(2,1)S(1)}, u32[]{:S(2)}, u32[]{:S(2)}) collective-permute-start(bf16[4,32,512]{2,1,0:T(8,128)(2,1)S(1)} %pad_maximum_fusion.6), channel_id=1, source_target_pairs={{0,4},{2,6},{4,0},{6,2},{1,5},{3,7},{5,1},{7,3},{8,12},{10,14},{12... | collective-permute-start | bytes 393224 | tf_op jit(solution)/shard_map/ppermute | solution.py:36
  53.6 3.8 %collective-permute-done.12.theirs.theirs_stat = bf16[544,256]{1,0:T(8,128)(2,1)S(1)} collective-permute-done((bf16[544,256]{1,0:T(8,128)(2,1)S(1)}, bf16[544,256]{1,0:T(8,128)(2,1)S(1)}, u32[]{:S(2)}, u32[]{:S(2)}) %collective-permute-start.12) | collective-permute-done | bytes 278560 | tf_op jit(solution)/shard_map/ppermute | solution.py:36
  58.1 5.3 %collective-permute-start.13 = (bf16[128,256]{1,0:T(8,128)(2,1)S(1)}, bf16[128,256]{1,0:T(8,128)(2,1)S(1)}, u32[]{:S(2)}, u32[]{:S(2)}) collective-permute-start(bf16[128,256]{1,0:T(8,128)(2,1)S(1)} %get-tuple-element.62), channel_id=1, source_target_pairs={{0,64},{32,96},{64,0},{96,32},{1,65},{33,97},{65,1},{97,33},{2,66}... | collective-permute-start | bytes 196616 | tf_op jit(solution)/shard_map/ppermute | solution.py:36
  64.1 2.2 %collective-permute-start.15 = (bf16[128,256]{1,0:T(8,128)(2,1)S(1)}, bf16[128,256]{1,0:T(8,128)(2,1)S(1)}, u32[]{:S(2)}, u32[]{:S(2)}) collective-permute-start(bf16[128,256]{1,0:T(8,128)(2,1)S(1)} %get-tuple-element.60), channel_id=1, source_target_pairs={{0,32},{32,64},{64,96},{96,0},{1,33},{33,65},{65,97},{97,1},{2,34}... | collective-permute-start | bytes 196616 | tf_op jit(solution)/shard_map/ppermute | solution.py:36
  66.5 4.0 %collective-permute-done.14 = bf16[128,256]{1,0:T(8,128)(2,1)S(1)} collective-permute-done((bf16[128,256]{1,0:T(8,128)(2,1)S(1)}, bf16[128,256]{1,0:T(8,128)(2,1)S(1)}, u32[]{:S(2)}, u32[]{:S(2)}) %collective-permute-start.14) | collective-permute-done | bytes 65568 | tf_op jit(solution)/shard_map/ppermute | solution.py:36
  72.1 2.1 %collective-permute-start.17 = (bf16[128,1024]{1,0:T(8,128)(2,1)S(1)}, bf16[128,1024]{1,0:T(8,128)(2,1)S(1)}, u32[]{:S(2)}, u32[]{:S(2)}) collective-permute-start(bf16[128,1024]{1,0:T(8,128)(2,1)S(1)} %constant_dynamic-update-slice_fusion.10), channel_id=1, source_target_pairs={{0,129},{1,128},{128,1},{129,0},{2,131},{3,130},{130,3},{131,2},{4... | collective-permute-start | bytes 786440 | tf_op jit(solution)/shard_map/ppermute | solution.py:36
  76.2 3.6 %collective-permute-done.16 = bf16[128,1024]{1,0:T(8,128)(2,1)S(1)} collective-permute-done((bf16[128,1024]{1,0:T(8,128)(2,1)S(1)}, bf16[128,1024]{1,0:T(8,128)(2,1)S(1)}, u32[]{:S(2)}, u32[]{:S(2)}) %collective-permute-start.16) | collective-permute-done | bytes 262176 | tf_op jit(solution)/shard_map/ppermute | solution.py:36
  79.8 6.7 %collective-permute-done.17 = bf16[128,1024]{1,0:T(8,128)(2,1)S(1)} collective-permute-done((bf16[128,1024]{1,0:T(8,128)(2,1)S(1)}, bf16[128,1024]{1,0:T(8,128)(2,1)S(1)}, u32[]{:S(2)}, u32[]{:S(2)}) %collective-permute-start.17) | collective-permute-done | bytes 262176 | tf_op jit(solution)/shard_map/ppermute | solution.py:36
  91.6 2.3 %collective-permute-start.25 = (bf16[32,2048]{1,0:T(8,128)(2,1)S(1)}, bf16[32,2048]{1,0:T(8,128)(2,1)S(1)}, u32[]{:S(2)}, u32[]{:S(2)}) collective-permute-start(bf16[32,2048]{1,0:T(8,128)(2,1)S(1)} %get-tuple-element.58), channel_id=1, source_target_pairs={{0,4},{2,6},{4,0},{6,2},{1,5},{3,7},{5,1},{7,3},{8,12},{10,14},{12... | collective-permute-start | bytes 393224 | tf_op jit(solution)/shard_map/ppermute | solution.py:36
  93.8 4.0 %collective-permute-done.28 = bf16[4,32,1024]{2,1,0:T(8,128)(2,1)S(1)} collective-permute-done((bf16[4,32,1024]{2,1,0:T(8,128)(2,1)S(1)}, bf16[4,32,1024]{2,1,0:T(8,128)(2,1)S(1)}, u32[]{:S(2)}, u32[]{:S(2)}) %collective-permute-start.28) | collective-permute-done | bytes 262176 | tf_op jit(solution)/shard_map/ppermute | solution.py:36
  98.1 4.0 %collective-permute-start.30 = (bf16[32,1024]{1,0:T(8,128)(2,1)S(1)}, bf16[32,1024]{1,0:T(8,128)(2,1)S(1)}, u32[]{:S(2)}, u32[]{:S(2)}) collective-permute-start(bf16[32,1024]{1,0:T(8,128)(2,1)S(1)} %get-tuple-element.54), channel_id=1, source_target_pairs={{0,96},{32,0},{64,32},{96,64},{1,97},{33,1},{65,33},{97,65},{2,98}... | collective-permute-start | bytes 196616 | tf_op jit(solution)/shard_map/ppermute | solution.py:36
  102.1 2.3 %collective-permute-start.31 = (bf16[32,1024]{1,0:T(8,128)(2,1)S(1)}, bf16[32,1024]{1,0:T(8,128)(2,1)S(1)}, u32[]{:S(2)}, u32[]{:S(2)}) collective-permute-start(bf16[32,1024]{1,0:T(8,128)(2,1)S(1)} %get-tuple-element.53), channel_id=1, source_target_pairs={{0,64},{32,96},{64,0},{96,32},{1,65},{33,97},{65,1},{97,33},{2,66}... | collective-permute-start | bytes 196616 | tf_op jit(solution)/shard_map/ppermute | solution.py:36
  105.8 4.8 %collective-permute-done.31 = bf16[32,1024]{1,0:T(8,128)(2,1)S(1)} collective-permute-done((bf16[32,1024]{1,0:T(8,128)(2,1)S(1)}, bf16[32,1024]{1,0:T(8,128)(2,1)S(1)}, u32[]{:S(2)}, u32[]{:S(2)}) %collective-permute-start.31) | collective-permute-done | bytes 65568 | tf_op jit(solution)/shard_map/ppermute | solution.py:36
  (102 shorter events, 25.0 us)
Async XLA Ops:
  2.8 25.6 %collective-permute-start.1 = (bf16[384,256]{1,0:T(8,128)(2,1)S(1)}, bf16[384,256]{1,0:T(8,128)(2,1)S(1)}, u32[]{:S(2)}, u32[]{:S(2)}) collective-permute-start(bf16[384,256]{1,0:T(8,128)(2,1)S(1)} %pad_maximum_fusion.4.earlier), channel_id=1, source_target_pairs={{0,64},{32,96},{64,0},{96,32},{1,65},{33,97},{65,1},{97,33},{2,66}... | collective-permute-start | bytes 589832 | tf_op jit(solution)/shard_map/ppermute | solution.py:36
  12.2 8.1 %collective-permute-start.4 = (bf16[32,512]{1,0:T(8,128)(2,1)S(1)}, bf16[32,512]{1,0:T(8,128)(2,1)S(1)}, u32[]{:S(2)}, u32[]{:S(2)}) collective-permute-start(bf16[32,512]{1,0:T(8,128)(2,1)S(1)} %get-tuple-element.87), channel_id=1, source_target_pairs={{0,129},{1,128},{128,1},{129,0},{2,131},{3,130},{130,3},{131,2},{4... | collective-permute-start | bytes 98312 | tf_op jit(solution)/shard_map/ppermute | solution.py:36
  15.0 8.1 %collective-permute-start = (bf16[384,256]{1,0:T(8,128)(2,1)S(1)}, bf16[384,256]{1,0:T(8,128)(2,1)S(1)}, u32[]{:S(2)}, u32[]{:S(2)}) collective-permute-start(bf16[384,256]{1,0:T(8,128)(2,1)S(1)} %pad_maximum_fusion.3), channel_id=1, source_target_pairs={{0,32},{32,64},{64,96},{96,0},{1,33},{33,65},{65,97},{97,1},{2,34}... | collective-permute-start | bytes 589832 | tf_op jit(solution)/shard_map/ppermute | solution.py:36
  17.6 10.8 %collective-permute-start.2 = (bf16[384,256]{1,0:T(8,128)(2,1)S(1)}, bf16[384,256]{1,0:T(8,128)(2,1)S(1)}, u32[]{:S(2)}, u32[]{:S(2)}) collective-permute-start(bf16[384,256]{1,0:T(8,128)(2,1)S(1)} %pad_maximum_fusion.5), channel_id=1, source_target_pairs={{0,96},{32,0},{64,32},{96,64},{1,97},{33,1},{65,33},{97,65},{2,98}... | collective-permute-start | bytes 589832 | tf_op jit(solution)/shard_map/ppermute | solution.py:36
  20.4 8.2 %collective-permute-start.6 = (bf16[4,32,512]{2,1,0:T(8,128)(2,1)S(1)}, bf16[4,32,512]{2,1,0:T(8,128)(2,1)S(1)}, u32[]{:S(2)}, u32[]{:S(2)}) collective-permute-start(bf16[4,32,512]{2,1,0:T(8,128)(2,1)S(1)} %pad_maximum_fusion.6), channel_id=1, source_target_pairs={{0,2},{2,4},{4,6},{6,0},{1,3},{3,5},{5,7},{7,1},{8,10},{10,12},{12... | collective-permute-start | bytes 393224 | tf_op jit(solution)/shard_map/ppermute | solution.py:36
  28.7 15.8 %collective-permute-start.8 = (bf16[1024,256]{1,0:T(8,128)(2,1)S(1)}, bf16[1024,256]{1,0:T(8,128)(2,1)S(1)}, u32[]{:S(2)}, u32[]{:S(2)}) collective-permute-start(bf16[1024,256]{1,0:T(8,128)(2,1)S(1)} %constant_dynamic-update-slice_fusion.k0.v0), channel_id=1, source_target_pairs={{0,128},{128,0},{1,129},{129,1},{2,130},{130,2},{3,131},{131,3},{4... | collective-permute-start | bytes 1572872 | tf_op jit(solution)/shard_map/ppermute | solution.py:36
  31.6 8.4 %collective-permute-start.9 = (bf16[512,256]{1,0:T(8,128)(2,1)S(1)}, bf16[512,256]{1,0:T(8,128)(2,1)S(1)}, u32[]{:S(2)}, u32[]{:S(2)}) collective-permute-start(bf16[512,256]{1,0:T(8,128)(2,1)S(1)} %pad_maximum_fusion.1.q_ref), channel_id=1, source_target_pairs={{0,16},{16,0},{1,17},{17,1},{2,18},{18,2},{3,19},{19,3},{4,20},{20... | collective-permute-start | bytes 786440 | tf_op jit(solution)/shard_map/ppermute | solution.py:36
  48.6 8.8 %collective-permute-start.12 = (bf16[544,256]{1,0:T(8,128)(2,1)S(1)}, bf16[544,256]{1,0:T(8,128)(2,1)S(1)}, u32[]{:S(2)}, u32[]{:S(2)}) collective-permute-start(bf16[544,256]{1,0:T(8,128)(2,1)S(1)} %shard_map.81), channel_id=1, source_target_pairs={{0,16},{16,0},{1,17},{17,1},{2,18},{18,2},{3,19},{19,3},{4,20},{20... | collective-permute-start | bytes 835592 | tf_op jit(solution)/shard_map/ppermute | solution.py:36
  51.0 7.1 %collective-permute-start.26 = (bf16[4,32,512]{2,1,0:T(8,128)(2,1)S(1)}, bf16[4,32,512]{2,1,0:T(8,128)(2,1)S(1)}, u32[]{:S(2)}, u32[]{:S(2)}) collective-permute-start(bf16[4,32,512]{2,1,0:T(8,128)(2,1)S(1)} %pad_maximum_fusion.6), channel_id=1, source_target_pairs={{0,4},{2,6},{4,0},{6,2},{1,5},{3,7},{5,1},{7,3},{8,12},{10,14},{12... | collective-permute-start | bytes 393224 | tf_op jit(solution)/shard_map/ppermute | solution.py:36
  58.1 8.4 %collective-permute-start.13 = (bf16[128,256]{1,0:T(8,128)(2,1)S(1)}, bf16[128,256]{1,0:T(8,128)(2,1)S(1)}, u32[]{:S(2)}, u32[]{:S(2)}) collective-permute-start(bf16[128,256]{1,0:T(8,128)(2,1)S(1)} %get-tuple-element.62), channel_id=1, source_target_pairs={{0,64},{32,96},{64,0},{96,32},{1,65},{33,97},{65,1},{97,33},{2,66}... | collective-permute-start | bytes 196616 | tf_op jit(solution)/shard_map/ppermute | solution.py:36
  63.4 7.1 %collective-permute-start.14 = (bf16[128,256]{1,0:T(8,128)(2,1)S(1)}, bf16[128,256]{1,0:T(8,128)(2,1)S(1)}, u32[]{:S(2)}, u32[]{:S(2)}) collective-permute-start(bf16[128,256]{1,0:T(8,128)(2,1)S(1)} %get-tuple-element.61), channel_id=1, source_target_pairs={{0,96},{32,0},{64,32},{96,64},{1,97},{33,1},{65,33},{97,65},{2,98}... | collective-permute-start | bytes 196616 | tf_op jit(solution)/shard_map/ppermute | solution.py:36
  70.5 9.3 %collective-permute-start.16 = (bf16[128,1024]{1,0:T(8,128)(2,1)S(1)}, bf16[128,1024]{1,0:T(8,128)(2,1)S(1)}, u32[]{:S(2)}, u32[]{:S(2)}) collective-permute-start(bf16[128,1024]{1,0:T(8,128)(2,1)S(1)} %constant_dynamic-update-slice_fusion.10), channel_id=1, source_target_pairs={{0,1},{1,0},{128,129},{129,128},{2,3},{3,2},{130,131},{131,130},{4... | collective-permute-start | bytes 786440 | tf_op jit(solution)/shard_map/ppermute | solution.py:36
  72.1 14.4 %collective-permute-start.17 = (bf16[128,1024]{1,0:T(8,128)(2,1)S(1)}, bf16[128,1024]{1,0:T(8,128)(2,1)S(1)}, u32[]{:S(2)}, u32[]{:S(2)}) collective-permute-start(bf16[128,1024]{1,0:T(8,128)(2,1)S(1)} %constant_dynamic-update-slice_fusion.10), channel_id=1, source_target_pairs={{0,129},{1,128},{128,1},{129,0},{2,131},{3,130},{130,3},{131,2},{4... | collective-permute-start | bytes 786440 | tf_op jit(solution)/shard_map/ppermute | solution.py:36
  74.2 12.3 %collective-permute-start.18 = (bf16[128,1024]{1,0:T(8,128)(2,1)S(1)}, bf16[128,1024]{1,0:T(8,128)(2,1)S(1)}, u32[]{:S(2)}, u32[]{:S(2)}) collective-permute-start(bf16[128,1024]{1,0:T(8,128)(2,1)S(1)} %constant_dynamic-update-slice_fusion.10), channel_id=1, source_target_pairs={{0,128},{1,129},{128,0},{129,1},{2,130},{3,131},{130,2},{131,3},{4... | collective-permute-start | bytes 786440 | tf_op jit(solution)/shard_map/ppermute | solution.py:36
  74.9 13.6 %collective-permute-start.27 = (bf16[512,256]{1,0:T(8,128)(2,1)S(1)}, bf16[512,256]{1,0:T(8,128)(2,1)S(1)}, u32[]{:S(2)}, u32[]{:S(2)}) collective-permute-start(bf16[512,256]{1,0:T(8,128)(2,1)S(1)} %get-tuple-element.50), channel_id=1, source_target_pairs={{0,8},{8,0},{1,9},{9,1},{2,10},{10,2},{3,11},{11,3},{4,12},{12,4},... | collective-permute-start | bytes 786440 | tf_op jit(solution)/shard_map/ppermute | solution.py:36
  75.6 11.6 %collective-permute-start.19 = (bf16[128,1024]{1,0:T(8,128)(2,1)S(1)}, bf16[128,1024]{1,0:T(8,128)(2,1)S(1)}, u32[]{:S(2)}, u32[]{:S(2)}) collective-permute-start(bf16[128,1024]{1,0:T(8,128)(2,1)S(1)} %constant_dynamic-update-slice_fusion.10), channel_id=1, source_target_pairs={{0,8},{8,0},{1,9},{9,1},{2,10},{10,2},{3,11},{11,3},{4,12},{12,4},... | collective-permute-start | bytes 786440 | tf_op jit(solution)/shard_map/ppermute | solution.py:36
  79.8 7.4 %collective-permute-start.20 = (bf16[128,1024]{1,0:T(8,128)(2,1)S(1)}, bf16[128,1024]{1,0:T(8,128)(2,1)S(1)}, u32[]{:S(2)}, u32[]{:S(2)}) collective-permute-start(bf16[128,1024]{1,0:T(8,128)(2,1)S(1)} %collective-permute-done.16), channel_id=1, source_target_pairs={{0,8},{8,0},{1,9},{9,1},{2,10},{10,2},{3,11},{11,3},{4,12},{12,4},... | collective-permute-start | bytes 786440 | tf_op jit(solution)/shard_map/ppermute | solution.py:36
  89.3 8.6 %collective-permute-start.28 = (bf16[4,32,1024]{2,1,0:T(8,128)(2,1)S(1)}, bf16[4,32,1024]{2,1,0:T(8,128)(2,1)S(1)}, u32[]{:S(2)}, u32[]{:S(2)}) collective-permute-start(bf16[4,32,1024]{2,1,0:T(8,128)(2,1)S(1)} %fusion.4), channel_id=1, source_target_pairs={{0,16},{16,0},{1,17},{17,1},{2,18},{18,2},{3,19},{19,3},{4,20},{20... | collective-permute-start | bytes 786440 | tf_op jit(solution)/shard_map/ppermute | solution.py:36
  89.5 12.7 %collective-permute-start.23 = (bf16[32,2048]{1,0:T(8,128)(2,1)S(1)}, bf16[32,2048]{1,0:T(8,128)(2,1)S(1)}, u32[]{:S(2)}, u32[]{:S(2)}) collective-permute-start(bf16[32,2048]{1,0:T(8,128)(2,1)S(1)} %get-tuple-element.57), channel_id=1, source_target_pairs={{0,2},{2,4},{4,6},{6,0},{1,3},{3,5},{5,7},{7,1},{8,10},{10,12},{12... | collective-permute-start | bytes 393224 | tf_op jit(solution)/shard_map/ppermute | solution.py:36
  91.1 13.3 %collective-permute-start.24 = (bf16[32,2048]{1,0:T(8,128)(2,1)S(1)}, bf16[32,2048]{1,0:T(8,128)(2,1)S(1)}, u32[]{:S(2)}, u32[]{:S(2)}) collective-permute-start(bf16[32,2048]{1,0:T(8,128)(2,1)S(1)} %get-tuple-element.59), channel_id=1, source_target_pairs={{0,6},{2,0},{4,2},{6,4},{1,7},{3,1},{5,3},{7,5},{8,14},{10,8},{12,... | collective-permute-start | bytes 393224 | tf_op jit(solution)/shard_map/ppermute | solution.py:36
  91.6 12.8 %collective-permute-start.25 = (bf16[32,2048]{1,0:T(8,128)(2,1)S(1)}, bf16[32,2048]{1,0:T(8,128)(2,1)S(1)}, u32[]{:S(2)}, u32[]{:S(2)}) collective-permute-start(bf16[32,2048]{1,0:T(8,128)(2,1)S(1)} %get-tuple-element.58), channel_id=1, source_target_pairs={{0,4},{2,6},{4,0},{6,2},{1,5},{3,7},{5,1},{7,3},{8,12},{10,14},{12... | collective-permute-start | bytes 393224 | tf_op jit(solution)/shard_map/ppermute | solution.py:36
  97.9 7.3 %collective-permute-start.29 = (bf16[32,1024]{1,0:T(8,128)(2,1)S(1)}, bf16[32,1024]{1,0:T(8,128)(2,1)S(1)}, u32[]{:S(2)}, u32[]{:S(2)}) collective-permute-start(bf16[32,1024]{1,0:T(8,128)(2,1)S(1)} %get-tuple-element.52), channel_id=1, source_target_pairs={{0,32},{32,64},{64,96},{96,0},{1,33},{33,65},{65,97},{97,1},{2,34}... | collective-permute-start | bytes 196616 | tf_op jit(solution)/shard_map/ppermute | solution.py:36
  98.1 7.7 %collective-permute-start.30 = (bf16[32,1024]{1,0:T(8,128)(2,1)S(1)}, bf16[32,1024]{1,0:T(8,128)(2,1)S(1)}, u32[]{:S(2)}, u32[]{:S(2)}) collective-permute-start(bf16[32,1024]{1,0:T(8,128)(2,1)S(1)} %get-tuple-element.54), channel_id=1, source_target_pairs={{0,96},{32,0},{64,32},{96,64},{1,97},{33,1},{65,33},{97,65},{2,98}... | collective-permute-start | bytes 196616 | tf_op jit(solution)/shard_map/ppermute | solution.py:36
  102.1 8.4 %collective-permute-start.31 = (bf16[32,1024]{1,0:T(8,128)(2,1)S(1)}, bf16[32,1024]{1,0:T(8,128)(2,1)S(1)}, u32[]{:S(2)}, u32[]{:S(2)}) collective-permute-start(bf16[32,1024]{1,0:T(8,128)(2,1)S(1)} %get-tuple-element.53), channel_id=1, source_target_pairs={{0,64},{32,96},{64,0},{96,32},{1,65},{33,97},{65,1},{97,33},{2,66}... | collective-permute-start | bytes 196616 | tf_op jit(solution)/shard_map/ppermute | solution.py:36
  (10 other events, 65.7 us)
